TPU v7x, 32 devices: a whole 2x2x4 slice. The times are simulated.
32 devices in a mesh: groups: 2 (over y), rollout: 8 (over z, x), tensor: 2 (over core).
Axes of the slice: x: 2, y: 2, z: 4, core: 2. Of those that a mesh axis runs over, the one named last changes fastest.
Arguments:
- hidden: bfloat16 [4, 3072, 8192], P(None, ('groups', 'rollout'), 'tensor'), parts along dimension 1, may hold values from -6 to 6
- counts: int32 [128], P('groups'), parts along dimension 0, may hold values from 1 to 72, 1536 in all
- key_value_weight: bfloat16 [8192, 2048], P('tensor'), may hold values from -0.09375 to 0.09375
- down_factor_weight: bfloat16 [128, 32, 8192], P(('groups', 'rollout'), None, 'tensor'), parts along dimension 0, may hold values from -0.0625 to 0.0625
- up_factor_weight: bfloat16 [128, 32, 2048], P(('groups', 'rollout'), None, 'tensor'), parts along dimension 0, may hold values from -1 to 1
Outputs:
- kv_new: bfloat16 [2048, 4, 3072], P('tensor', None, ('groups', 'rollout')), parts along dimension 2
There are 2 independent parts, one for each index of `groups`. A program takes and returns all parts, laid end to end along the dimension named above; an argument that names none is the same for every part. Nothing has to cross between parts.
Inputs may be any that keep to these rules, and one draw needn't show every extreme that they name: counts sum to 1536; rows are stored grouped by adapter in increasing adapter order, adapter a holding the counts[a] rows after those of adapters 0 to a-1.
All inputs are finite; a program needn't handle non-finite values.
Results may differ from a plain program's by a relative error of at most 0.0095.
Values may be sent and summed in bfloat16 or wider, within the bound.
No kernel may reach another device: no remote copies, remote signals or barrier semaphores. Data moves between devices by JAX's collectives and lax.ppermute only.
A program may use at most 128 MiB of HBM per device.

v0:
```python
import jax
import jax.numpy as jnp
from jax import lax
from jax.sharding import PartitionSpec as P


def adapter_order(gathered, owners):
    slots = gathered.shape[0]
    return (
        gathered.reshape((owners, slots // owners) + gathered.shape[1:])
        .transpose(1, 0, 2, 3)
        .reshape(gathered.shape)
    )


def local(hidden, counts, key_value_weight, down_factor_weight, up_factor_weight):
    step_count, row_count, width_local = hidden.shape
    adapter_count = counts.shape[0]
    owners = lax.axis_size("rollout")
    first_row = lax.axis_index("rollout") * row_count
    bounds = jnp.cumsum(counts)
    positions = first_row + jnp.arange(row_count, dtype=jnp.int32)
    adapter = jnp.sum((bounds[None, :] <= positions[:, None]).astype(jnp.int32), axis=1)
    down_slots, up_slots = (
        lax.all_gather(down_factor_weight, "rollout", axis=0, tiled=True),
        lax.all_gather(up_factor_weight, "rollout", axis=0, tiled=True),
    )
    down_all = adapter_order(down_slots, owners)
    up_all = adapter_order(up_slots, owners)
    rank_size = down_all.shape[1]
    onehot = (adapter[:, None] == jnp.arange(adapter_count, dtype=jnp.int32)[None, :]).astype(
        jnp.float32
    )
    all_scores = jnp.einsum("srd,akd->srak", hidden, down_all, preferred_element_type=jnp.float32)
    partial_rank = jnp.sum(all_scores * onehot[None, :, :, None], axis=2)
    summed = lax.psum(
        partial_rank.reshape(step_count, row_count * rank_size).astype(jnp.bfloat16), "tensor"
    ).astype(jnp.float32)
    rank_proj = summed.reshape(step_count, row_count, rank_size)
    rank_expanded = (rank_proj[:, :, None, :] * onehot[None, :, :, None]).reshape(
        step_count, row_count, adapter_count * rank_size
    )
    up_factor_flattened = up_all.reshape(adapter_count * rank_size, up_all.shape[2]).astype(
        jnp.float32
    )
    low_rank_delta = jnp.einsum(
        "bhw,wv->vbh", rank_expanded, up_factor_flattened, precision=lax.Precision.HIGHEST
    )
    own_columns = key_value_weight.shape[1] // lax.axis_size("tensor")
    results = []
    for step_index in range(step_count):
        step_rows = hidden[step_index]

        def term_one(row_start, row_count_term, step_rows=step_rows):
            return jnp.einsum(
                "dk,rd->kr", key_value_weight, step_rows, preferred_element_type=jnp.float32
            )

        results.append(
            lax.psum_scatter(
                term_one(jnp.int32(0), lax.axis_size("tensor") * own_columns).astype(jnp.bfloat16),
                "tensor",
                scatter_dimension=0,
                tiled=True,
            ).astype(jnp.float32)
        )
    shared_output = jnp.stack(results, axis=1)
    return (shared_output + low_rank_delta).astype(jnp.bfloat16)


def solution(mesh):
    placed = (
        P(None, ("groups", "rollout"), "tensor"),
        P("groups"),
        P("tensor", None),
        P(("groups", "rollout"), None, "tensor"),
        P(("groups", "rollout"), None, "tensor"),
    )
    return jax.shard_map(
        local,
        mesh=mesh,
        in_specs=placed,
        out_specs=P("tensor", None, ("groups", "rollout")),
        check_vma=False,
    )
```

profile of v0, /device:TPU:0, one launch (start us, length us, event | category | flops | bytes accessed | tf_op | source)
XLA Modules:
  0.0 380.4 jit_solution(15858705474764425671)
XLA Ops:
  7.4 0.7 all-gather.5.cloned.1.call-update
  8.1 0.0 all-gather.3.cloned.1.call-start
  8.1 0.7 all-gather.3.cloned.1.call-update
  8.8 0.0 reduce-scatter.5.cloned.1.call-start
  8.9 10.6 %convolution_convert_fusion.3 = bf16[2048,192]{0,1:T(8,128)(2,1)} fusion(bf16[4096,2048]{1,0:T(8,128)(2,1)} %param.7, bf16[4,192,4096]{2,1,0:T(8,128)(2,1)} %param.5), kind=kOutput, calls=%fused_computation.11 | convolution fusion | flops 3221618688 | bytes 19136512 | tf_op jit(solution)/shard_map/dk,rd->kr/dot_general | solution.py:55
  19.5 0.0 reduce-scatter.7.cloned.1.call-start
  19.6 11.0 %convolution_convert_fusion.2 = bf16[2048,192]{0,1:T(8,128)(2,1)} fusion(bf16[4096,2048]{1,0:T(8,128)(2,1)} %param.7, bf16[4,192,4096]{2,1,0:T(8,128)(2,1)} %param.5), kind=kOutput, calls=%fused_computation.10 | convolution fusion | flops 3221618688 | bytes 19136512 | tf_op jit(solution)/shard_map/dk,rd->kr/dot_general | solution.py:55
  30.6 0.0 reduce-scatter.9.cloned.1.call-start
  30.7 10.7 %convolution_convert_fusion.1 = bf16[2048,192]{0,1:T(8,128)(2,1)} fusion(bf16[4096,2048]{1,0:T(8,128)(2,1)} %param.7, bf16[4,192,4096]{2,1,0:T(8,128)(2,1)} %param.5), kind=kOutput, calls=%fused_computation.9 | convolution fusion | flops 3221618688 | bytes 19136512 | tf_op jit(solution)/shard_map/dk,rd->kr/dot_general | solution.py:55
  41.3 0.0 reduce-scatter.9.cloned.1.call-update
  41.3 0.2 reduce-scatter.11.cloned.1.call-start
  41.6 11.1 %convolution_convert_fusion = bf16[2048,192]{0,1:T(8,128)(2,1)} fusion(bf16[4096,2048]{1,0:T(8,128)(2,1)} %param.7, bf16[4,192,4096]{2,1,0:T(8,128)(2,1)} %param.5), kind=kOutput, calls=%fused_computation.8 | convolution fusion | flops 3221618688 | bytes 19136512 | tf_op jit(solution)/shard_map/dk,rd->kr/dot_general | solution.py:55
  52.7 0.1 copy.20
  52.8 0.1 reduce-window.8
  52.9 0.1 reduce
  53.0 0.1 convert_reduce_fusion
  53.2 33.3 %all-gather.5.cloned.1.call-done = bf16[64,32,1024]{2,1,0:T(8,128)(2,1)} async-done(((bf16[8,32,1024]{2,1,0:T(8,128)(2,1)}), bf16[64,32,1024]{2,1,0:T(8,128)(2,1)}) %all-gather.5.cloned.1.call-update) | async-done | bytes 4194320 | tf_op jit(solution)/shard_map/all_gather | solution.py:26
  86.4 4.9 %copy.22 = bf16[8,8,32,1024]{3,2,0,1:T(8,128)(2,1)} copy(bf16[8,8,32,1024]{3,2,1,0:T(8,128)(2,1)} %bitcast.52) | data formatting | bytes 8388608 | tf_op jit(solution)/shard_map/reshape | solution.py:10
  91.4 223.1 %all-gather.3.cloned.1.call-done = bf16[64,32,4096]{2,1,0:T(8,128)(2,1)} async-done(((bf16[8,32,4096]{2,1,0:T(8,128)(2,1)}), bf16[64,32,4096]{2,1,0:T(8,128)(2,1)}) %all-gather.3.cloned.1.call-update) | async-done | bytes 16777232 | tf_op jit(solution)/shard_map/all_gather | solution.py:25
  314.5 29.2 %multiply_reduce_fusion = bf16[4,192,32]{1,2,0:T(8,128)(2,1)S(1)} fusion(f32[192,64]{0,1:T(8,128)S(1)} %fusion.17, bf16[8,8,32,4096]{3,2,1,0:T(8,128)(2,1)} %bitcast.55, bf16[4,192,4096]{2,1,0:T(8,128)(2,1)} %param.5), kind=kOutput, calls=%fused_computation.3 | convolution fusion | flops 12888023040 | bytes 23166976 | tf_op jit(solution)/shard_map/srd,akd->srak/dot_general | solution.py:34
  343.7 3.8 %psum.7 = bf16[4,192,32]{1,2,0:T(8,128)(2,1)S(1)} all-reduce(bf16[4,192,32]{1,2,0:T(8,128)(2,1)S(1)} %multiply_reduce_fusion), channel_id=1, replica_groups=mesh['groups'=2,'rollout'=8,'tensor'=2] {'tensor'}, use_global_device_ids=true, to_apply=%region_7.8 | all-reduce | flops 24576 | bytes 98304 | tf_op jit(solution)/shard_map/psum | solution.py:36
  347.5 1.2 broadcast_multiply_fusion
  348.7 8.1 %copy.21 = f32[4,192,64,32]{1,3,2,0:T(8,128)} copy(f32[4,192,64,32]{1,2,3,0:T(8,128)S(1)} %broadcast_multiply_fusion) | data formatting | bytes 12582912 | tf_op jit(solution)/shard_map/mul | solution.py:40
  356.8 16.0 %fusion.4 = bf16[1024,4,192]{0,2,1:T(8,128)(2,1)} fusion(f32[4,192,2048]{1,2,0:T(8,128)} %bitcast.51, bf16[2048,1024,1]{1,0,2:T(8,128)(2,1)} %bitcast.53, bf16[1024,1,192]{0,2,1:T(8,128)(2,1)} %bitcast.59, bf16[1024,1,192]{0,2,1:T(8,128)(2,1)} %bitcast.58, bf16[1024,1,192]{0,2,1:T(8,128)(2,1)} %bitcast.57, bf16[1024,1,192]{0,2,1:T(8,128)(2,1)} %bitcast.56), kind=kOutput, calls=%fused_computation.7 | convolution fusion | flops 19332071424 | bytes 13631488 | tf_op jit(solution)/shard_map/bhw,wv->vbh/dot_general | solution.py:46
  (13 shorter events, 0.1 us)
Async XLA Ops:
  7.4 79.1 %all-gather.5.cloned.1.call-start = ((), (), s32[]{:S(2)}) async-start(), calls=%async_computation.9 | async-start | bytes 4718592 | tf_op jit(solution)/shard_map/all_gather | solution.py:26
  8.1 306.4 %all-gather.3.cloned.1.call-start = ((), (), s32[]{:S(2)}) async-start(), calls=%async_computation.8 | async-start | bytes 18874368 | tf_op jit(solution)/shard_map/all_gather | solution.py:25
  8.8 348.0 %reduce-scatter.5.cloned.1.call-start = ((), (), s32[]{:S(2)}) async-start(), calls=%async_computation.4 | async-start | bytes 1179648 | tf_op jit(solution)/shard_map/reduce_scatter | solution.py:60
  19.5 337.3 %reduce-scatter.7.cloned.1.call-start = ((), (), s32[]{:S(2)}) async-start(), calls=%async_computation.5 | async-start | bytes 1179648 | tf_op jit(solution)/shard_map/reduce_scatter | solution.py:60
  30.6 326.2 %reduce-scatter.9.cloned.1.call-start = ((), (), s32[]{:S(2)}) async-start(), calls=%async_computation.6 | async-start | bytes 1179648 | tf_op jit(solution)/shard_map/reduce_scatter | solution.py:60
  41.3 11.4 %copy-start = (s32[64]{0:T(128)S(1)}, s32[64]{0:T(128)}, u32[]{:S(2)}) copy-start(s32[64]{0:T(128)} %param.6) | copy-start | bytes 772
  41.3 315.5 %reduce-scatter.11.cloned.1.call-start = ((), (), s32[]{:S(2)}) async-start(), calls=%async_computation.7 | async-start | bytes 1179648 | tf_op jit(solution)/shard_map/reduce_scatter | solution.py:60
Sparse Core Ops, SparseCore 0:
  10.3 76.0 all-gather.4
  88.6 225.8 all-gather.2
Sparse Core Ops, SparseCore 1:
  19.6 10.9 reduce-scatter.4
  32.7 9.3 reduce-scatter.6
  44.2 9.3 reduce-scatter.8
  56.0 9.3 reduce-scatter.10
where the time goes:
time: 381 us; the launch traced here: 380 us
  waiting for transfers between devices  258 us (68%)
  matrix products  88.5 us (23%)
  between operations  15.1 us (4%)
  local copies, waits for them, and re-layouts  13.1 us (3%)
  blocking collectives  3.81 us (1%)
    all_gather x1, waiting for transfers between devices, local(): lax.all_gather(down_factor_weight, 'rollout', axis=0, tiled=True)  223 us
    dot_general x4, matrix products, term_one(): jnp.einsum('dk,rd->kr', key_value_weight, step_rows, preferred_element_ty...  43.4 us
    all_gather x1, waiting for transfers between devices, local(): lax.all_gather(up_factor_weight, 'rollout', axis=0, tiled=True)  33.3 us
    dot_general x1, matrix products, local(): jnp.einsum('srd,akd->srak', hidden, down_all, preferred_element_type=jnp....  29.2 us
    dot_general x1, matrix products, local(): jnp.einsum('bhw,wv->vbh', rank_expanded, up_factor_flattened, precision=l...  16 us
    mul x1, local copies, waits for them, and re-layouts, local(): rank_proj[:, :, None, :] * onehot[None, :, :, None]  8.08 us
  transfers between devices with their start and end apart: 6, of which 2 were waited for; matrix products, arithmetic and copies ran while one was open for 23% of the time, Pallas kernels for 0%

commit v1 on v0

v1 whole, which is shorter than its diff:
```python
import jax
import jax.numpy as jnp
from jax import lax
from jax.sharding import PartitionSpec as P

PAIR_SLOTS = 3
FORWARD_SLOTS = 2
BF16 = jnp.bfloat16
F32 = jnp.float32
I32 = jnp.int32


def count_at_most(bounds, rows):
    return jnp.sum((bounds <= rows[..., None]).astype(I32), axis=-1)


def first_slot(owner, adapter, owners):
    return (adapter - owner + owners - 1) // owners


def end_slot(owner, adapter, owners):
    return (adapter - owner + owners) // owners


def slots_of(stored, start, size):
    return lax.dynamic_slice_in_dim(stored, start, size, axis=0)


def send(value, hop, owners):
    return lax.ppermute(value, "rollout", [(i, i ^ hop) for i in range(owners)])


def scores(hidden, factors, mask):
    every = jnp.einsum("srd,nkd->srnk", hidden, factors, preferred_element_type=F32)
    return jnp.sum(every * mask[None, :, :, None].astype(F32), axis=2)


def expand(rank_proj, mask):
    wide = rank_proj.astype(BF16)[:, :, None, :] * mask[None, :, :, None].astype(BF16)
    return wide.reshape(wide.shape[:2] + (-1,))


def delta(rank_proj, factors, mask):
    return jnp.einsum(
        "srw,wc->src",
        expand(rank_proj, mask),
        factors.reshape(-1, factors.shape[2]),
        preferred_element_type=F32,
    )


def local(hidden, counts, key_value_weight, down, up):
    steps, rows, width = hidden.shape
    adapters = counts.shape[0]
    owners = lax.axis_size("rollout")
    sides = lax.axis_size("tensor")
    held = down.shape[0]
    pair_slots = min(PAIR_SLOTS, held)
    forward_slots = min(FORWARD_SLOTS, pair_slots)
    me = lax.axis_index("rollout")
    side = lax.axis_index("tensor")

    order = jnp.arange(adapters, dtype=I32)
    bounds = jnp.sum(jnp.where(order[:, None] <= order[None, :], counts[:, None], 0), axis=0)
    row_adapter = count_at_most(bounds, me * rows + jnp.arange(rows, dtype=I32))
    device = jnp.arange(owners, dtype=I32)
    low = count_at_most(bounds, device * rows)
    high = count_at_most(bounds, device * rows + (rows - 1))
    owner = device[:, None]
    low_pair = low[device // 2 * 2]
    pair_start = jnp.minimum(first_slot(owner, low_pair[None, :], owners), held - pair_slots)
    forward_start = jnp.minimum(
        first_slot(owner, low[None, :], owners), pair_start + (pair_slots - forward_slots)
    )
    same_column = (owner % 2) == (device[None, :] % 2)
    covered = jnp.where(same_column, pair_start + pair_slots, forward_start + forward_slots)
    extra = jnp.max(jnp.maximum(end_slot(owner, high[None, :], owners) - covered, 0))
    group_count = lax.axis_size("groups")
    rounds = extra
    for turn in range(1, group_count):
        rounds = jnp.maximum(
            rounds,
            lax.ppermute(
                extra, "groups", [(i, (i + turn) % group_count) for i in range(group_count)]
            ),
        )

    hops = [2 * m for m in range(owners // 2)]

    def exchanged(stored):
        kept = []
        for hop in hops:
            if hop == 0:
                kept.append(slots_of(stored, pair_start[me, me], pair_slots))
            else:
                kept.append(
                    send(slots_of(stored, pair_start[me, me ^ hop], pair_slots), hop, owners)
                )
        passed = []
        for hop, block in zip(hops, kept):
            source = me ^ hop
            offset = forward_start[source, me ^ 1] - pair_start[source, me]
            passed.append(send(slots_of(block, offset, forward_slots), 1, owners))
        return kept, passed

    def slot_mask(source, start, size):
        ids = source + owners * (start + jnp.arange(size, dtype=I32))
        return row_adapter[:, None] == ids[None, :]

    kept_masks = [slot_mask(me ^ hop, pair_start[me ^ hop, me], pair_slots) for hop in hops]
    passed_masks = [
        slot_mask(me ^ 1 ^ hop, forward_start[me ^ 1 ^ hop, me], forward_slots) for hop in hops
    ]
    masks = kept_masks + passed_masks

    kept, passed = exchanged(down)
    kept_up, passed_up = exchanged(up)

    own_columns = key_value_weight.shape[1] // sides
    if sides == 2:
        theirs = lax.dynamic_slice_in_dim(
            key_value_weight, (1 - side) * own_columns, own_columns, axis=1
        )
        mine = lax.dynamic_slice_in_dim(key_value_weight, side * own_columns, own_columns, axis=1)
        base_sent = jnp.einsum(
            "srd,dc->src", hidden, theirs, preferred_element_type=F32
        ).astype(BF16)
        base_got = lax.ppermute(base_sent, "tensor", [(0, 1), (1, 0)])
        base_mine = jnp.einsum("srd,dc->src", hidden, mine, preferred_element_type=F32).astype(BF16)

        def base():
            return base_mine.astype(F32) + base_got.astype(F32)
    else:
        base_all = jnp.einsum(
            "srd,dc->src", hidden, key_value_weight, preferred_element_type=F32
        ).astype(BF16)
        base_sum = lax.psum_scatter(base_all, "tensor", scatter_dimension=2, tiled=True)

        def base():
            return base_sum.astype(F32)

    rank_part = None
    for block, mask in zip(kept + passed, masks):
        part = scores(hidden, block, mask)
        rank_part = part if rank_part is None else rank_part + part

    def round_blocks(stored, turn):
        blocks, valid = [], []
        for hop in range(owners):
            wanted = covered[me, me ^ hop] + turn
            block = slots_of(stored, jnp.minimum(wanted, held - 1), 1)
            blocks.append(block if hop == 0 else send(block, hop, owners))
            source = me ^ hop
            slot = covered[source, me] + turn
            valid.append(jnp.where(slot < held, source + owners * slot, -1))
        return jnp.concatenate(blocks), row_adapter[:, None] == jnp.stack(valid)[None, :]

    def more_rank(turn, total):
        blocks, mask = round_blocks(down, turn)
        return total + scores(hidden, blocks, mask)

    rank_part = lax.fori_loop(0, rounds, more_rank, rank_part)

    if sides == 2:
        rank_proj = rank_part + lax.ppermute(
            rank_part.astype(BF16), "tensor", [(0, 1), (1, 0)]
        ).astype(F32)
    else:
        rank_proj = lax.psum(rank_part.astype(BF16), "tensor").astype(F32)

    all_up = jnp.concatenate(kept_up + passed_up)
    all_mask = jnp.concatenate(masks, axis=1)

    def first():
        return base() + delta(rank_proj, all_up, all_mask)

    def finish(total):
        return total.astype(BF16)

    def more_delta(turn, total):
        blocks, mask = round_blocks(up, turn)
        return total + delta(rank_proj, blocks, mask)

    out = lax.cond(
        rounds > 0,
        lambda: finish(lax.fori_loop(0, rounds, more_delta, first())),
        lambda: finish(first()),
    )
    return out.transpose(2, 0, 1)


def solution(mesh):
    placed = (
        P(None, ("groups", "rollout"), "tensor"),
        P("groups"),
        P("tensor", None),
        P(("groups", "rollout"), None, "tensor"),
        P(("groups", "rollout"), None, "tensor"),
    )
    return jax.shard_map(
        local,
        mesh=mesh,
        in_specs=placed,
        out_specs=P("tensor", None, ("groups", "rollout")),
        check_vma=False,
    )
```

time: 381 us -> 169 us (0.44)
  waiting for transfers between devices: 258 us -> 54.7 us
  matrix products: 88.5 us -> 56 us
  starting transfers between devices: 0.4 us -> 19.3 us
  other arithmetic: 1.53 us -> 11.5 us
  blocking collectives: 3.81 us -> 0 us
    all_gather x2 -> x0, waiting for transfers between devices: 256 us -> none  [the longest x1 223 us: local(): lax.all_gather(down_factor_weight, 'rollout', axis=0, tiled=True)]
    ppermute x0 -> x17, waiting for transfers between devices: none -> 54.7 us  [the longest x14 53.5 us: send(): return lax.ppermute(value, 'rollout', [(i, i ^ hop) for i in range(owners)])]
    dot_general x6 -> x11, matrix products: 88.5 us -> 56 us  [the longest x8 26.8 us: scores(): jnp.einsum('srd,nkd->srnk', hidden, factors, preferred_element_type=F32)]
    ppermute x0 -> x17, starting transfers between devices: none -> 19.3 us  [the longest x14 16.3 us: send(): return lax.ppermute(value, 'rollout', [(i, i ^ hop) for i in range(owners)])]
    dynamic_slice x0 -> x13, local copies, waits for them, and re-layouts: none -> 11 us  [the longest x10 8.9 us: slots_of(): return lax.dynamic_slice_in_dim(stored, start, size, axis=0)]
    mul x1 -> x0, local copies, waits for them, and re-layouts: 8.08 us -> none  [local(): rank_proj[:, :, None, :] * onehot[None, :, :, None]]
    add x1 -> x11, other arithmetic: 0.01 us -> 5.02 us  [the longest x8 4.91 us: slot_mask(): ids = source + owners * (start + jnp.arange(size, dtype=I32))]
    reshape x1 -> x0, local copies, waits for them, and re-layouts: 4.92 us -> none  [adapter_order(): gathered.reshape((owners, slots // owners) + gathered.shape[1:])]
  transfers between devices with their start and end apart: 6 -> 17, of which waited for: 2 -> 5; matrix products, arithmetic and copies ran while one was open for 23% -> 39% of each run, Pallas kernels for 0% -> 0%
where the time goes in v1:
time: 169 us
  matrix products  56 us (33%)
  waiting for transfers between devices  54.7 us (32%)
  starting transfers between devices  19.3 us (11%)
  between operations  14.1 us (8%)
  local copies, waits for them, and re-layouts  12.8 us (8%)
  other arithmetic  11.5 us (7%)
    ppermute x14, waiting for transfers between devices, send(): return lax.ppermute(value, 'rollout', [(i, i ^ hop) for i in range(owners)])  53.5 us
    dot_general x8, matrix products, scores(): jnp.einsum('srd,nkd->srnk', hidden, factors, preferred_element_type=F32)  26.8 us
    ppermute x14, starting transfers between devices, send(): return lax.ppermute(value, 'rollout', [(i, i ^ hop) for i in range(owners)])  16.3 us
    dot_general x1, matrix products, local(): jnp.einsum('srd,dc->src', hidden, mine, preferred_element_type=F32)  12.1 us
    dot_general x1, matrix products, local(): jnp.einsum('srd,dc->src', hidden, theirs, preferred_element_type=F32)  12.1 us
    dynamic_slice x10, local copies, waits for them, and re-layouts, slots_of(): return lax.dynamic_slice_in_dim(stored, start, size, axis=0)  8.9 us
    dot_general x1, matrix products, delta(): jnp.einsum('srw,wc->src', expand(rank_proj, mask), factors.reshape(-1, fa...  5.01 us
    add x8, other arithmetic, slot_mask(): ids = source + owners * (start + jnp.arange(size, dtype=I32))  4.91 us
  transfers between devices with their start and end apart: 17, of which 5 were waited for; matrix products, arithmetic and copies ran while one was open for 39% of the time, Pallas kernels for 0%

profile of v1, /device:TPU:0, one launch (start us, length us, event | category | flops | bytes accessed | tf_op | source)
XLA Modules:
  0.0 168.6 jit_solution(3221702264436154043)
XLA Ops:
  2.4 3.0 %collective-permute-start.14 = (s32[]{:T(128)}, s32[]{:T(128)}, u32[]{:S(2)}, u32[]{:S(2)}) collective-permute-start(s32[]{:T(128)} %get-tuple-element.715), channel_id=1, source_target_pairs={{0,16},{16,0},{1,17},{17,1},{2,18},{18,2},{3,19},{19,3},{4,20},{20... | collective-permute-start | bytes 20 | tf_op jit(solution)/shard_map/ppermute | solution.py:83
  9.6 1.9 %constant_dynamic-slice_fusion.23 = bf16[2,32,4096]{2,1,0:T(8,128)(2,1)} fusion(bf16[8,32,4096]{2,1,0:T(8,128)(2,1)} %param.14, s32[]{:T(128)S(6)} %dynamic_slice.366), kind=kLoop, calls=%fused_computation.148 | loop fusion | bytes 1048580 | tf_op jit(solution)/shard_map/dynamic_slice | solution.py:26
  18.9 3.0 %constant_dynamic-slice_fusion.26 = (bf16[3,32,4096]{2,1,0:T(8,128)(2,1)}, bf16[3,32,4096]{2,1,0:T(8,128)(2,1)}, bf16[3,32,4096]{2,1,0:T(8,128)(2,1)S(1)}) fusion(bf16[8,32,4096]{2,1,0:T(8,128)(2,1)} %param.14, s32[]{:T(128)S(6)} %select_n.475, s32[]{:T(128)S(6)} %select_n.479, s32[]{:T(128)S(6)} %select_n.477), kind=kLoop, calls=%fused_computation.151 | loop fusion | bytes 4718604 | tf_op jit(solution)/shard_map/dynamic_slice | solution.py:26
  21.9 1.6 collective-permute-start.16
  23.5 2.5 %collective-permute-start.18 = (bf16[3,32,4096]{2,1,0:T(8,128)(2,1)}, bf16[3,32,4096]{2,1,0:T(8,128)(2,1)}, u32[]{:S(2)}, u32[]{:S(2)}) collective-permute-start(bf16[3,32,4096]{2,1,0:T(8,128)(2,1)} %get-tuple-element.678), channel_id=1, source_target_pairs={{0,12},{2,14},{4,8},{6,10},{8,4},{10,6},{12,0},{14,2},{1,13},{3,15... | collective-permute-start | bytes 2359304 | tf_op jit(solution)/shard_map/ppermute | solution.py:30
  37.4 5.3 %fusion.88 = f32[4,192,32]{1,2,0:T(8,128)S(1)} fusion(bf16[4,192,4096]{2,1,0:T(8,128)(2,1)} %param.11, bf16[8,32,4096]{2,1,0:T(8,128)(2,1)} %param.14, s32[]{:T(128)S(6)} %select_n.473, f32[192,3]{0,1:T(4,128)S(1)} %get-tuple-element.721), kind=kOutput, calls=%fused_computation.89 | convolution fusion | flops 604102656 | bytes 7178500 | tf_op jit(solution)/shard_map/srd,nkd->srnk/dot_general | solution.py:34
  44.2 5.1 %fusion.124 = f32[4,192,32]{1,2,0:T(8,128)S(1)} fusion(bf16[4,192,4096]{2,1,0:T(8,128)(2,1)} %param.11, bf16[2,32,4096]{2,1,0:T(8,128)(2,1)} %collective-permute-done.19, f32[192,2]{0,1:T(2,128)} %get-tuple-element.638), kind=kOutput, calls=%fused_computation.101 | convolution fusion | flops 402726912 | bytes 6915584 | tf_op jit(solution)/shard_map/srd,nkd->srnk/dot_general | solution.py:34
  51.1 10.6 %collective-permute-done.18 = bf16[3,32,4096]{2,1,0:T(8,128)(2,1)} collective-permute-done((bf16[3,32,4096]{2,1,0:T(8,128)(2,1)}, bf16[3,32,4096]{2,1,0:T(8,128)(2,1)}, u32[]{:S(2)}, u32[]{:S(2)}) %collective-permute-start.18) | collective-permute-done | bytes 786464 | tf_op jit(solution)/shard_map/ppermute | solution.py:30
  63.4 30.2 %collective-permute-done.17 = bf16[3,32,4096]{2,1,0:T(8,128)(2,1)} collective-permute-done((bf16[3,32,4096]{2,1,0:T(8,128)(2,1)S(1)}, bf16[3,32,4096]{2,1,0:T(8,128)(2,1)}, u32[]{:S(2)}, u32[]{:S(2)}) %collective-permute-start.17) | collective-permute-done | bytes 786464 | tf_op jit(solution)/shard_map/ppermute | solution.py:30
  95.3 3.3 %fusion.91 = f32[4,192,32]{1,2,0:T(8,128)S(1)} fusion(bf16[4,192,4096]{2,1,0:T(8,128)(2,1)S(1)} %bitcast.389, bf16[3,32,4096]{2,1,0:T(8,128)(2,1)} %collective-permute-done.16, f32[192,3]{0,1:T(4,128)S(1)} %copy-done.9), kind=kOutput, calls=%fused_computation.90 | convolution fusion | flops 604102656 | bytes 7178496 | tf_op jit(solution)/shard_map/srd,nkd->srnk/dot_general | solution.py:34
  98.6 3.3 %fusion.97 = f32[4,192,32]{1,2,0:T(8,128)S(1)} fusion(bf16[4,192,4096]{2,1,0:T(8,128)(2,1)S(1)} %bitcast.389, bf16[3,32,4096]{2,1,0:T(8,128)(2,1)} %collective-permute-done.18, f32[192,3]{0,1:T(4,128)S(1)} %copy-done.8), kind=kOutput, calls=%fused_computation.92 | convolution fusion | flops 604102656 | bytes 7178496 | tf_op jit(solution)/shard_map/srd,nkd->srnk/dot_general | solution.py:34
  101.9 3.3 %fusion.94 = f32[4,192,32]{1,2,0:T(8,128)S(1)} fusion(bf16[4,192,4096]{2,1,0:T(8,128)(2,1)S(1)} %bitcast.389, bf16[3,32,4096]{2,1,0:T(8,128)(2,1)} %collective-permute-done.17, f32[192,3]{0,1:T(4,128)S(1)} %copy-done.7), kind=kOutput, calls=%fused_computation.91 | convolution fusion | flops 604102656 | bytes 7178496 | tf_op jit(solution)/shard_map/srd,nkd->srnk/dot_general | solution.py:34
  105.3 2.1 %fusion.127 = f32[4,192,32]{1,2,0:T(8,128)S(1)} fusion(bf16[4,192,4096]{2,1,0:T(8,128)(2,1)S(1)} %bitcast.389, bf16[2,32,4096]{2,1,0:T(8,128)(2,1)S(1)} %collective-permute-done.20, f32[192,2]{0,1:T(2,128)S(1)} %copy-done.2), kind=kOutput, calls=%fused_computation.102 | convolution fusion | flops 402726912 | bytes 6915584 | tf_op jit(solution)/shard_map/srd,nkd->srnk/dot_general | solution.py:34
  107.4 2.1 %fusion.133 = f32[4,192,32]{1,2,0:T(8,128)S(1)} fusion(bf16[4,192,4096]{2,1,0:T(8,128)(2,1)S(1)} %bitcast.389, bf16[2,32,4096]{2,1,0:T(8,128)(2,1)S(1)} %collective-permute-done.22, f32[192,2]{0,1:T(2,128)S(1)} %get-tuple-element.727), kind=kOutput, calls=%fused_computation.104 | convolution fusion | flops 402726912 | bytes 6915584 | tf_op jit(solution)/shard_map/srd,nkd->srnk/dot_general | solution.py:34
  109.5 2.3 %fusion.130 = f32[4,192,32]{1,2,0:T(8,128)S(1)} fusion(bf16[4,192,4096]{2,1,0:T(8,128)(2,1)S(1)} %bitcast.389, bf16[2,32,4096]{2,1,0:T(8,128)(2,1)S(1)} %collective-permute-done.21, f32[192,2]{0,1:T(2,128)S(1)} %get-tuple-element.725), kind=kOutput, calls=%fused_computation.103 | convolution fusion | flops 402726912 | bytes 6915584 | tf_op jit(solution)/shard_map/srd,nkd->srnk/dot_general | solution.py:34
  114.3 12.1 %fusion.58 = bf16[4,192,1024]{2,1,0:T(8,128)(2,1)} fusion(bf16[4,192,4096]{2,1,0:T(8,128)(2,1)} %get-tuple-element.1321, bf16[4096,2048]{1,0:T(8,128)(2,1)} %param.13, s32[]{:T(128)S(6)} %select_n.471), kind=kOutput, calls=%fused_computation.79 | convolution fusion | flops 6443237376 | bytes 16252932 | tf_op jit(solution)/shard_map/srd,dc->src/dot_general | solution.py:125
  126.5 2.8 %collective-permute-start.26 = (bf16[3,32,1024]{2,1,0:T(8,128)(2,1)S(1)}, bf16[3,32,1024]{2,1,0:T(8,128)(2,1)S(1)}, u32[]{:S(2)}, u32[]{:S(2)}) collective-permute-start(bf16[3,32,1024]{2,1,0:T(8,128)(2,1)S(1)} %get-tuple-element.680), channel_id=1, source_target_pairs={{0,12},{2,14},{4,8},{6,10},{8,4},{10,6},{12,0},{14,2},{1,13},{3,15... | collective-permute-start | bytes 589832 | tf_op jit(solution)/shard_map/ppermute | solution.py:30
  129.3 12.1 %fusion.61 = bf16[4,192,1024]{2,1,0:T(8,128)(2,1)} fusion(bf16[4,192,4096]{2,1,0:T(8,128)(2,1)} %get-tuple-element.1321, bf16[4096,2048]{1,0:T(8,128)(2,1)} %param.13, s32[]{:T(128)S(6)} %select_n.470), kind=kOutput, calls=%fused_computation.80 | convolution fusion | flops 6443237376 | bytes 16252932 | tf_op jit(solution)/shard_map/srd,dc->src/dot_general | solution.py:129
  141.6 1.7 %collective-permute-start.25 = (bf16[3,32,1024]{2,1,0:T(8,128)(2,1)S(1)}, bf16[3,32,1024]{2,1,0:T(8,128)(2,1)S(1)}, u32[]{:S(2)}, u32[]{:S(2)}) collective-permute-start(bf16[3,32,1024]{2,1,0:T(8,128)(2,1)S(1)} %get-tuple-element.681), channel_id=1, source_target_pairs={{0,8},{2,10},{4,12},{6,14},{8,0},{10,2},{12,4},{14,6},{1,9},{3,11}... | collective-permute-start | bytes 589832 | tf_op jit(solution)/shard_map/ppermute | solution.py:30
  145.6 8.2 %collective-permute-done.25 = bf16[3,32,1024]{2,1,0:T(8,128)(2,1)S(1)} collective-permute-done((bf16[3,32,1024]{2,1,0:T(8,128)(2,1)S(1)}, bf16[3,32,1024]{2,1,0:T(8,128)(2,1)S(1)}, u32[]{:S(2)}, u32[]{:S(2)}) %collective-permute-start.25) | collective-permute-done | bytes 196640 | tf_op jit(solution)/shard_map/ppermute | solution.py:30
  154.5 4.4 %collective-permute-done.29 = bf16[2,32,1024]{2,1,0:T(8,128)(2,1)S(1)} collective-permute-done((bf16[2,32,1024]{2,1,0:T(8,128)(2,1)S(1)}, bf16[2,32,1024]{2,1,0:T(8,128)(2,1)S(1)}, u32[]{:S(2)}, u32[]{:S(2)}) %collective-permute-start.29) | collective-permute-done | bytes 131104 | tf_op jit(solution)/shard_map/ppermute | solution.py:30
  160.3 5.0 %conditional.2 = (f32[4,192,1024]{2,1,0:T(8,128)}) conditional(s32[]{:T(128)} %convert_element_type.154, (bf16[4,192,1024]{2,1,0:T(8,128)(2,1)}, bf16[4,192,1024]{2,1,0:T(8,128)(2,1)}, bf16[4,192,32]{1,2,0:T(8,128)(2,1)S(1)}, pred[192,20]{0,1:T(8,128)(4,1)S(1)}, bf16[20,32,1024]{2,1,0:T(8,128)(2,1)S(1)}) %tuple.37, ...), branch_computations={%region_16.17_spmd, %region_17.20_spmd} | conditional | flops 1413913344 | bytes 18345836
  160.3 5.0 %bitcast_add_fusion = f32[4,192,1024]{2,1,0:T(8,128)} fusion(bf16[4,192,1024]{2,1,0:T(8,128)(2,1)} %get-tuple-element.464, bf16[4,192,1024]{2,1,0:T(8,128)(2,1)} %get-tuple-element.463, bf16[20,32,1024]{2,1,0:T(8,128)(2,1)S(1)} %get-tuple-element.467, bf16[192,20]{0,1:T(8,128)(2,1)S(1)} %convert_element_type.126, bf16[4,192,32]{1,2,0:T(8,128)(2,1)S(1)} %get-tuple-element.465), kind=kOutput, calls=%fused_computation.23 | convolution fusion | flops 1010270208 | bytes 7659008 | tf_op jit(solution)/shard_map/cond/branch_0_fun/srw,wc->src/dot_general | solution.py:44
  165.3 3.3 %convert_bitcast_fusion = bf16[1024,4,192]{0,2,1:T(8,128)(2,1)} fusion(f32[4,192,1024]{2,1,0:T(8,128)} %get-tuple-element.1320), kind=kLoop, calls=%fused_computation.78 | loop fusion | flops 786432 | bytes 4718592 | tf_op jit(solution)/shard_map/transpose | solution.py:189
  (102 shorter events, 25.3 us)
Async XLA Ops:
  2.4 40.5 %collective-permute-start.14 = (s32[]{:T(128)}, s32[]{:T(128)}, u32[]{:S(2)}, u32[]{:S(2)}) collective-permute-start(s32[]{:T(128)} %get-tuple-element.715), channel_id=1, source_target_pairs={{0,16},{16,0},{1,17},{17,1},{2,18},{18,2},{3,19},{19,3},{4,20},{20... | collective-permute-start | bytes 20 | tf_op jit(solution)/shard_map/ppermute | solution.py:83
  11.5 32.7 %collective-permute-start.19 = (bf16[2,32,4096]{2,1,0:T(8,128)(2,1)}, bf16[2,32,4096]{2,1,0:T(8,128)(2,1)}, u32[]{:S(2)}, u32[]{:S(2)}) collective-permute-start(bf16[2,32,4096]{2,1,0:T(8,128)(2,1)} %constant_dynamic-slice_fusion.23), channel_id=1, source_target_pairs={{0,2},{2,0},{4,6},{6,4},{8,10},{10,8},{12,14},{14,12},{1,3},{3,1},... | collective-permute-start | bytes 1572872 | tf_op jit(solution)/shard_map/ppermute | solution.py:30
  18.9 17.9 %copy-start = (bf16[8,32,1024]{2,1,0:T(8,128)(2,1)S(1)}, bf16[8,32,1024]{2,1,0:T(8,128)(2,1)}, u32[]{:S(2)}) copy-start(bf16[8,32,1024]{2,1,0:T(8,128)(2,1)} %param.15) | copy-start | bytes 1572868
  21.9 27.5 %collective-permute-start.16 = (bf16[3,32,4096]{2,1,0:T(8,128)(2,1)}, bf16[3,32,4096]{2,1,0:T(8,128)(2,1)}, u32[]{:S(2)}, u32[]{:S(2)}) collective-permute-start(bf16[3,32,4096]{2,1,0:T(8,128)(2,1)} %get-tuple-element.677), channel_id=1, source_target_pairs={{0,4},{2,6},{4,0},{6,2},{8,12},{10,14},{12,8},{14,10},{1,5},{3,7},... | collective-permute-start | bytes 2359304 | tf_op jit(solution)/shard_map/ppermute | solution.py:30
  23.5 38.2 %collective-permute-start.18 = (bf16[3,32,4096]{2,1,0:T(8,128)(2,1)}, bf16[3,32,4096]{2,1,0:T(8,128)(2,1)}, u32[]{:S(2)}, u32[]{:S(2)}) collective-permute-start(bf16[3,32,4096]{2,1,0:T(8,128)(2,1)} %get-tuple-element.678), channel_id=1, source_target_pairs={{0,12},{2,14},{4,8},{6,10},{8,4},{10,6},{12,0},{14,2},{1,13},{3,15... | collective-permute-start | bytes 2359304 | tf_op jit(solution)/shard_map/ppermute | solution.py:30
  37.4 57.9 %slice-start = ((s8[6291456]{0:T(1024)(128)(4,1)}), s8[2097152]{0:T(1024)(128)(4,1)S(1)}, s32[]{:S(2)}) async-start(s8[6291456]{0:T(1024)(128)(4,1)} %bitcast.388), calls=%async_computation | async-start | bytes 4194304
  42.7 50.9 %collective-permute-start.17 = (bf16[3,32,4096]{2,1,0:T(8,128)(2,1)S(1)}, bf16[3,32,4096]{2,1,0:T(8,128)(2,1)}, u32[]{:S(2)}, u32[]{:S(2)}) collective-permute-start(bf16[3,32,4096]{2,1,0:T(8,128)(2,1)S(1)} %get-tuple-element.679), channel_id=1, source_target_pairs={{0,8},{2,10},{4,12},{6,14},{8,0},{10,2},{12,4},{14,6},{1,9},{3,11}... | collective-permute-start | bytes 2359304 | tf_op jit(solution)/shard_map/ppermute | solution.py:30
  44.2 51.1 %slice-start.1 = ((s8[6291456]{0:T(1024)(128)(4,1)}), s8[4194304]{0:T(1024)(128)(4,1)S(1)}, s32[]{:S(2)}) async-start(s8[6291456]{0:T(1024)(128)(4,1)} %bitcast.388), calls=%async_computation.1 | async-start | bytes 8388608
  49.4 45.9 %copy-start.9 = (f32[192,3]{0,1:T(4,128)S(1)}, f32[192,3]{0,1:T(4,128)}, u32[]{:S(2)}) copy-start(f32[192,3]{0,1:T(4,128)} %get-tuple-element.630) | copy-start | bytes 6916
  50.5 54.8 %collective-permute-start.20 = (bf16[2,32,4096]{2,1,0:T(8,128)(2,1)S(1)}, bf16[2,32,4096]{2,1,0:T(8,128)(2,1)S(1)}, u32[]{:S(2)}, u32[]{:S(2)}) collective-permute-start(bf16[2,32,4096]{2,1,0:T(8,128)(2,1)S(1)} %constant_dynamic-slice_fusion.22), channel_id=1, source_target_pairs={{0,2},{2,0},{4,6},{6,4},{8,10},{10,8},{12,14},{14,12},{1,3},{3,1},... | collective-permute-start | bytes 1572872 | tf_op jit(solution)/shard_map/ppermute | solution.py:30
  62.8 44.6 %collective-permute-start.22 = (bf16[2,32,4096]{2,1,0:T(8,128)(2,1)S(1)}, bf16[2,32,4096]{2,1,0:T(8,128)(2,1)S(1)}, u32[]{:S(2)}, u32[]{:S(2)}) collective-permute-start(bf16[2,32,4096]{2,1,0:T(8,128)(2,1)S(1)} %constant_dynamic-slice_fusion.20), channel_id=1, source_target_pairs={{0,2},{2,0},{4,6},{6,4},{8,10},{10,8},{12,14},{14,12},{1,3},{3,1},... | collective-permute-start | bytes 1572872 | tf_op jit(solution)/shard_map/ppermute | solution.py:30
  94.7 14.8 %collective-permute-start.21 = (bf16[2,32,4096]{2,1,0:T(8,128)(2,1)S(1)}, bf16[2,32,4096]{2,1,0:T(8,128)(2,1)S(1)}, u32[]{:S(2)}, u32[]{:S(2)}) collective-permute-start(bf16[2,32,4096]{2,1,0:T(8,128)(2,1)S(1)} %constant_dynamic-slice_fusion.21), channel_id=1, source_target_pairs={{0,2},{2,0},{4,6},{6,4},{8,10},{10,8},{12,14},{14,12},{1,3},{3,1},... | collective-permute-start | bytes 1572872 | tf_op jit(solution)/shard_map/ppermute | solution.py:30
  112.8 41.7 %collective-permute-start.27 = (bf16[2,32,1024]{2,1,0:T(8,128)(2,1)S(1)}, bf16[2,32,1024]{2,1,0:T(8,128)(2,1)S(1)}, u32[]{:S(2)}, u32[]{:S(2)}) collective-permute-start(bf16[2,32,1024]{2,1,0:T(8,128)(2,1)S(1)} %copy-done.1), channel_id=1, source_target_pairs={{0,2},{2,0},{4,6},{6,4},{8,10},{10,8},{12,14},{14,12},{1,3},{3,1},... | collective-permute-start | bytes 393224 | tf_op jit(solution)/shard_map/ppermute | solution.py:30
  126.4 33.9 %collective-permute-start.15 = (bf16[4,192,1024]{2,1,0:T(8,128)(2,1)}, bf16[4,192,1024]{2,1,0:T(8,128)(2,1)}, u32[]{:S(2)}, u32[]{:S(2)}) collective-permute-start(bf16[4,192,1024]{2,1,0:T(8,128)(2,1)} %fusion.58), channel_id=1, source_target_pairs={{0,1},{1,0},{2,3},{3,2},{4,5},{5,4},{6,7},{7,6},{8,9},{9,8},{10,11... | collective-permute-start | bytes 4718600 | tf_op jit(solution)/shard_map/ppermute | solution.py:128
  126.5 16.9 %collective-permute-start.26 = (bf16[3,32,1024]{2,1,0:T(8,128)(2,1)S(1)}, bf16[3,32,1024]{2,1,0:T(8,128)(2,1)S(1)}, u32[]{:S(2)}, u32[]{:S(2)}) collective-permute-start(bf16[3,32,1024]{2,1,0:T(8,128)(2,1)S(1)} %get-tuple-element.680), channel_id=1, source_target_pairs={{0,12},{2,14},{4,8},{6,10},{8,4},{10,6},{12,0},{14,2},{1,13},{3,15... | collective-permute-start | bytes 589832 | tf_op jit(solution)/shard_map/ppermute | solution.py:30
  129.2 14.8 %collective-permute-start.24 = (bf16[3,32,1024]{2,1,0:T(8,128)(2,1)S(1)}, bf16[3,32,1024]{2,1,0:T(8,128)(2,1)S(1)}, u32[]{:S(2)}, u32[]{:S(2)}) collective-permute-start(bf16[3,32,1024]{2,1,0:T(8,128)(2,1)S(1)} %get-tuple-element.682), channel_id=1, source_target_pairs={{0,4},{2,6},{4,0},{6,2},{8,12},{10,14},{12,8},{14,10},{1,5},{3,7},... | collective-permute-start | bytes 589832 | tf_op jit(solution)/shard_map/ppermute | solution.py:30
  129.2 12.1 %copy-start.6 = (pred[192,3]{0,1:T(4,128)(4,1)S(1)}, pred[192,3]{0,1:T(4,128)(4,1)}, u32[]{:S(2)}) copy-start(pred[192,3]{0,1:T(4,128)(4,1)} %get-tuple-element.722) | copy-start | bytes 1732
  129.2 12.1 %copy-start.10 = (pred[192,2]{0,1:T(4,128)(4,1)S(1)}, pred[192,2]{0,1:T(4,128)(4,1)}, u32[]{:S(2)}) copy-start(pred[192,2]{0,1:T(4,128)(4,1)} %get-tuple-element.639) | copy-start | bytes 1156
  129.2 12.1 %copy-start.11 = (pred[192,2]{0,1:T(4,128)(4,1)S(1)}, pred[192,2]{0,1:T(4,128)(4,1)}, u32[]{:S(2)}) copy-start(pred[192,2]{0,1:T(4,128)(4,1)} %get-tuple-element.724) | copy-start | bytes 1156
  141.6 12.2 %collective-permute-start.25 = (bf16[3,32,1024]{2,1,0:T(8,128)(2,1)S(1)}, bf16[3,32,1024]{2,1,0:T(8,128)(2,1)S(1)}, u32[]{:S(2)}, u32[]{:S(2)}) collective-permute-start(bf16[3,32,1024]{2,1,0:T(8,128)(2,1)S(1)} %get-tuple-element.681), channel_id=1, source_target_pairs={{0,8},{2,10},{4,12},{6,14},{8,0},{10,2},{12,4},{14,6},{1,9},{3,11}... | collective-permute-start | bytes 589832 | tf_op jit(solution)/shard_map/ppermute | solution.py:30
  143.4 15.7 %collective-permute-start.30 = (bf16[2,32,1024]{2,1,0:T(8,128)(2,1)S(1)}, bf16[2,32,1024]{2,1,0:T(8,128)(2,1)S(1)}, u32[]{:S(2)}, u32[]{:S(2)}) collective-permute-start(bf16[2,32,1024]{2,1,0:T(8,128)(2,1)S(1)} %constant_dynamic-slice_fusion.27), channel_id=1, source_target_pairs={{0,2},{2,0},{4,6},{6,4},{8,10},{10,8},{12,14},{14,12},{1,3},{3,1},... | collective-permute-start | bytes 393224 | tf_op jit(solution)/shard_map/ppermute | solution.py:30
  144.0 10.5 %collective-permute-start.28 = (bf16[2,32,1024]{2,1,0:T(8,128)(2,1)S(1)}, bf16[2,32,1024]{2,1,0:T(8,128)(2,1)S(1)}, u32[]{:S(2)}, u32[]{:S(2)}) collective-permute-start(bf16[2,32,1024]{2,1,0:T(8,128)(2,1)S(1)} %constant_dynamic-slice_fusion.15), channel_id=1, source_target_pairs={{0,2},{2,0},{4,6},{6,4},{8,10},{10,8},{12,14},{14,12},{1,3},{3,1},... | collective-permute-start | bytes 393224 | tf_op jit(solution)/shard_map/ppermute | solution.py:30
  153.9 5.0 %collective-permute-start.29 = (bf16[2,32,1024]{2,1,0:T(8,128)(2,1)S(1)}, bf16[2,32,1024]{2,1,0:T(8,128)(2,1)S(1)}, u32[]{:S(2)}, u32[]{:S(2)}) collective-permute-start(bf16[2,32,1024]{2,1,0:T(8,128)(2,1)S(1)} %constant_dynamic-slice_fusion.14), channel_id=1, source_target_pairs={{0,2},{2,0},{4,6},{6,4},{8,10},{10,8},{12,14},{14,12},{1,3},{3,1},... | collective-permute-start | bytes 393224 | tf_op jit(solution)/shard_map/ppermute | solution.py:30
  158.9 1.3 collective-permute-start.23
  (9 other events, 71.6 us)

commit v2 on v0

v2 whole, which is shorter than its diff:
```python
import functools

import jax
import jax.numpy as jnp
from jax import lax
from jax.experimental import pallas as pl
from jax.experimental.pallas import tpu as pltpu
from jax.sharding import PartitionSpec as P

PAIR_SLOTS = 3
FORWARD_SLOTS = 2
LANES = 128
VMEM_LIMIT = 48 * 1024 * 1024
BF16 = jnp.bfloat16
F32 = jnp.float32
I32 = jnp.int32
SMALL = pl.CostEstimate(flops=1000, bytes_accessed=1000, transcendentals=0)
PARAMS = pltpu.CompilerParams(vmem_limit_bytes=VMEM_LIMIT)
IN_SMEM = pl.BlockSpec(memory_space=pltpu.SMEM)
ANYWHERE = pl.BlockSpec(memory_space=pl.ANY)


def first_slot(owner, adapter, owners):
    return lax.div(adapter - owner + (owners - 1), jnp.int32(owners))


def end_slot(owner, adapter, owners):
    return lax.div(adapter - owner + owners, jnp.int32(owners))


def pair_start(owner, low_pair, sizes):
    return jnp.minimum(first_slot(owner, low_pair, sizes.owners), sizes.held - sizes.kept)


def forward_start(owner, low, low_pair, sizes):
    return jnp.minimum(
        first_slot(owner, low, sizes.owners),
        pair_start(owner, low_pair, sizes) + (sizes.kept - sizes.passed),
    )


class Sizes:
    def __init__(self, owners, adapters, held, rows):
        self.owners, self.adapters, self.held, self.rows = owners, adapters, held, rows
        self.kept = min(PAIR_SLOTS, held)
        self.passed = min(FORWARD_SLOTS, self.kept)
        self.pairs = owners // 2
        self.slots = self.pairs * (self.kept + self.passed)

    def kept_base(self, m):
        return m * self.kept

    def passed_base(self, m):
        return self.pairs * self.kept + m * self.passed


def pack_kernel(sizes, counts, stored, *refs):
    pairs = sizes.pairs
    sent, (passed0, bounds, windows, low_pair, sems) = refs[: pairs - 1], refs[pairs - 1 :]
    me = lax.axis_index("rollout")
    mine = lax.div(me, jnp.int32(2))
    odd_row = (2 * mine + 1) * sizes.rows
    bounds[0] = jnp.int32(0)

    def add(a, carry):
        end = carry[0] + counts[a]
        bounds[a + 1] = end
        lows = [
            low + (end <= 2 * p * sizes.rows).astype(I32) for p, low in enumerate(carry[1 : pairs + 1])
        ]
        return (end, *lows, carry[pairs + 1] + (end <= odd_row).astype(I32))

    found = lax.fori_loop(0, sizes.adapters, add, (jnp.int32(0),) * (pairs + 2), unroll=8)
    for p in range(pairs):
        low_pair[p] = found[1 + p]
    odd = found[pairs + 1]
    low_mine = low_pair[mine]
    is_even = me == 2 * mine
    low_other = jnp.where(is_even, odd, low_mine)
    copies = []
    for m in range(1, pairs):
        start = pair_start(me, low_pair[mine ^ m], sizes)
        windows[m] = start
        copies.append(
            pltpu.make_async_copy(stored.at[pl.ds(start, sizes.kept)], sent[m - 1], sems.at[m])
        )
    start = forward_start(me, low_other, low_mine, sizes)
    copies.insert(
        0, pltpu.make_async_copy(stored.at[pl.ds(start, sizes.passed)], passed0, sems.at[0])
    )
    for copy in copies:
        copy.start()
    windows[pairs] = start
    windows[0] = pair_start(me, low_mine, sizes)
    for m in range(pairs):
        source = me ^ (2 * m)
        windows[pairs + 1 + m] = forward_start(source, low_other, low_mine, sizes) - pair_start(
            source, low_mine, sizes
        )
    windows[2 * pairs + 1] = low_mine
    windows[2 * pairs + 2] = jnp.where(is_even, low_mine, odd)
    for copy in copies:
        copy.wait()


def pack(sizes, counts, stored):
    tail = stored.shape[1:]
    block = jax.ShapeDtypeStruct((sizes.kept,) + tail, stored.dtype)
    small = jax.ShapeDtypeStruct((sizes.passed,) + tail, stored.dtype)
    pairs = sizes.pairs
    return pl.pallas_call(
        functools.partial(pack_kernel, sizes),
        out_shape=[block] * (pairs - 1)
        + [
            small,
            jax.ShapeDtypeStruct((sizes.adapters + 1,), I32),
            jax.ShapeDtypeStruct((2 * pairs + 3,), I32),
        ],
        in_specs=[IN_SMEM, ANYWHERE],
        out_specs=[ANYWHERE] * pairs + [IN_SMEM, IN_SMEM],
        scratch_shapes=[pltpu.SMEM((pairs,), I32), pltpu.SemaphoreType.DMA((pairs,))],
        compiler_params=PARAMS,
        cost_estimate=SMALL,
        name="pack",
    )(counts, stored)


def pack_again_kernel(sizes, windows, stored, *refs):
    pairs = sizes.pairs
    sent, (passed0, kept0, sems) = refs[: pairs - 1], refs[pairs - 1 :]
    copies = [
        pltpu.make_async_copy(stored.at[pl.ds(windows[m], sizes.kept)], target, sems.at[m])
        for m, target in enumerate((kept0,) + tuple(sent))
    ]
    copies.append(
        pltpu.make_async_copy(
            stored.at[pl.ds(windows[pairs], sizes.passed)], passed0, sems.at[pairs]
        )
    )
    for copy in copies:
        copy.start()
    for copy in copies:
        copy.wait()


def pack_again(sizes, windows, stored):
    tail = stored.shape[1:]
    block = jax.ShapeDtypeStruct((sizes.kept,) + tail, stored.dtype)
    small = jax.ShapeDtypeStruct((sizes.passed,) + tail, stored.dtype)
    pairs = sizes.pairs
    return pl.pallas_call(
        functools.partial(pack_again_kernel, sizes),
        out_shape=[block] * (pairs - 1) + [small, block],
        in_specs=[IN_SMEM, ANYWHERE],
        out_specs=[ANYWHERE] * (pairs + 1),
        scratch_shapes=[pltpu.SemaphoreType.DMA((pairs + 1,))],
        compiler_params=PARAMS,
        cost_estimate=SMALL,
        name="pack_again",
    )(windows, stored)


def cut_kernel(index, size, windows, block, out, sem):
    copy = pltpu.make_async_copy(block.at[pl.ds(windows[index], size)], out, sem)
    copy.start()
    copy.wait()


def cut(windows, index, block, size):
    return pl.pallas_call(
        functools.partial(cut_kernel, index, size),
        out_shape=jax.ShapeDtypeStruct((size,) + block.shape[1:], block.dtype),
        in_specs=[IN_SMEM, ANYWHERE],
        out_specs=ANYWHERE,
        scratch_shapes=[pltpu.SemaphoreType.DMA],
        compiler_params=PARAMS,
        cost_estimate=SMALL,
        name="cut",
    )(windows, block)


def ranges_kernel(sizes, bounds, windows, ranges, rounds, lows, highs):
    me = lax.axis_index("rollout")
    low_mine = windows[2 * sizes.pairs + 1]
    low = windows[2 * sizes.pairs + 2]
    first_row = me * sizes.rows

    def fill(base, source, start, size):
        for k in range(size):
            adapter = source + sizes.owners * (start + k)
            ranges[2 * (base + k)] = bounds[adapter] - first_row
            ranges[2 * (base + k) + 1] = bounds[adapter + 1] - first_row

    for m in range(sizes.pairs):
        source = me ^ (2 * m)
        fill(sizes.kept_base(m), source, pair_start(source, low_mine, sizes), sizes.kept)
        source = me ^ 1 ^ (2 * m)
        fill(sizes.passed_base(m), source, forward_start(source, low, low_mine, sizes), sizes.passed)

    for d in range(sizes.owners):
        lows[d] = jnp.int32(0)
        highs[d] = jnp.int32(0)

    def count(a, carry):
        end = bounds[a + 1]
        return tuple(
            c + (end <= d * sizes.rows + last).astype(I32)
            for (d, last), c in zip(places, carry)
        )

    places = [(d, last) for last in (0, sizes.rows - 1) for d in range(sizes.owners)]
    found = lax.fori_loop(0, sizes.adapters, count, (jnp.int32(0),) * len(places))
    for d in range(sizes.owners):
        lows[d] = found[d]
        highs[d] = found[sizes.owners + d]

    def most(d, so_far):
        low_d, high_d, low_p = lows[d], highs[d], lows[lax.div(d, jnp.int32(2)) * 2]

        def each(owner, so_far):
            same = ((owner ^ d) & 1) == 0
            covered = jnp.where(
                same,
                pair_start(owner, low_p, sizes) + sizes.kept,
                forward_start(owner, low_d, low_p, sizes) + sizes.passed,
            )
            return jnp.maximum(so_far, end_slot(owner, high_d, sizes.owners) - covered)

        return lax.fori_loop(0, sizes.owners, each, so_far)

    rounds[0] = lax.fori_loop(0, sizes.owners, most, jnp.int32(0))


def ranges_of(sizes, bounds, windows):
    return pl.pallas_call(
        functools.partial(ranges_kernel, sizes),
        out_shape=[
            jax.ShapeDtypeStruct((2 * sizes.slots,), I32),
            jax.ShapeDtypeStruct((1,), I32),
        ],
        in_specs=[IN_SMEM, IN_SMEM],
        out_specs=[IN_SMEM, IN_SMEM],
        scratch_shapes=[pltpu.SMEM((sizes.owners,), I32), pltpu.SMEM((sizes.owners,), I32)],
        compiler_params=PARAMS,
        cost_estimate=SMALL,
        name="ranges",
    )(bounds, windows)


def lane_mask(ranges, base, size, rank, rows, steps):
    lane = lax.broadcasted_iota(I32, (1, size * rank), 1)
    low = jnp.zeros((1, size * rank), I32)
    high = jnp.zeros((1, size * rank), I32)
    for k in range(size):
        here = (lane >= k * rank) & (lane < (k + 1) * rank)
        low = jnp.where(here, ranges[2 * (base + k)], low)
        high = jnp.where(here, ranges[2 * (base + k) + 1], high)
    row = lax.broadcasted_iota(I32, (rows, size * rank), 0)
    one = (row >= low) & (row < high)
    return jnp.concatenate([one] * steps, axis=0) if steps > 1 else one


def scores_kernel(bases, rank, rows, fold, with_before, ranges, hidden, *refs):
    blocks, refs = refs[: len(bases)], refs[len(bases) :]
    before, refs = (refs[0], refs[1:]) if with_before else (None, refs)
    out = refs[0]
    sent = refs[1] if fold else None
    sums = refs[-len(bases) :]
    k = pl.program_id(0)
    steps = hidden.shape[0] // rows

    for block, total in zip(blocks, sums):
        part = lax.dot_general(
            hidden[...], block[...], (((1,), (1,)), ((), ())), preferred_element_type=F32
        )

        @pl.when(k == 0)
        def _(total=total, part=part):
            total[...] = part

        @pl.when(k > 0)
        def _(total=total, part=part):
            total[...] += part

    @pl.when(k == pl.num_programs(0) - 1)
    def _():
        for s in range(steps):
            here = pl.ds(s * rows, rows)
            acc = before[here, :] if with_before else jnp.zeros((rows, LANES), F32)
            for base, total in zip(bases, sums):
                wide = total.shape[1]
                masked = jnp.where(
                    lane_mask(ranges, base, wide // rank, rank, rows, 1), total[here, :], 0.0
                )
                if wide < LANES:
                    masked = jnp.concatenate(
                        [masked, jnp.zeros((rows, LANES - wide), F32)], axis=1
                    )
                acc = acc + masked
            if fold:
                shift = LANES // 2
                while shift >= rank:
                    acc = acc + pltpu.roll(acc, shift, 1)
                    shift //= 2
                sent[here, :] = acc.astype(BF16)
            out[here, :] = acc


def scores(ranges, hidden, blocks, bases, rows, before=None, fold=False):
    total_rows, width = hidden.shape
    rank = blocks[0].shape[1]
    tiles = 4 if width % 512 == 0 and width >= 2048 else 1
    tile = width // tiles
    flat = [b.reshape(-1, width) for b in blocks]
    whole = pl.BlockSpec((total_rows, LANES), lambda k: (0, 0))
    out_shape = [jax.ShapeDtypeStruct((total_rows, LANES), F32)]
    if fold:
        out_shape.append(jax.ShapeDtypeStruct((total_rows, LANES), BF16))
    with_before = before is not None
    return pl.pallas_call(
        functools.partial(scores_kernel, bases, rank, rows, fold, with_before),
        grid=(tiles,),
        out_shape=out_shape,
        in_specs=[IN_SMEM, pl.BlockSpec((total_rows, tile), lambda k: (0, k))]
        + [pl.BlockSpec((f.shape[0], tile), lambda k: (0, k)) for f in flat]
        + [whole] * with_before,
        out_specs=[whole] * len(out_shape),
        scratch_shapes=[pltpu.VMEM((total_rows, f.shape[0]), F32) for f in flat],
        compiler_params=PARAMS,
        cost_estimate=SMALL,
        name="scores",
    )(ranges, hidden, *flat, *([before] if with_before else []))


def base_kernel(which, hidden, weight, out):
    out[...] = jnp.dot(hidden[...], weight[...], preferred_element_type=F32).astype(BF16)


def base_product(which, hidden, weight, columns):
    total_rows, width = hidden.shape
    tile = min(256, columns)
    tiles = columns // tile
    return pl.pallas_call(
        base_kernel,
        grid_spec=pltpu.PrefetchScalarGridSpec(
            num_scalar_prefetch=1,
            grid=(tiles,),
            in_specs=[
                pl.BlockSpec((total_rows, width), lambda j, which: (0, 0)),
                pl.BlockSpec((width, tile), lambda j, which: (0, which[0] * tiles + j)),
            ],
            out_specs=pl.BlockSpec((total_rows, tile), lambda j, which: (0, j)),
        ),
        out_shape=jax.ShapeDtypeStruct((total_rows, columns), BF16),
        compiler_params=PARAMS,
        cost_estimate=SMALL,
        name="base_product",
    )(which, hidden, weight)


def final_kernel(bases, rank, rows, n_added, ranges, own, *refs):
    got, refs = refs[0], refs[1:]
    added, refs = refs[:n_added], refs[n_added:]
    blocks, (out, left, right) = refs[: len(bases)], refs[len(bases) :]
    group = LANES // rank
    slots = sum(b.shape[0] for b in blocks) // rank
    steps = own.shape[0] // rows

    @pl.when(pl.program_id(0) == 0)
    def _():
        for s in range(steps):
            here = pl.ds(s * rows, rows)
            proj = (own[here, :] + got[here, :].astype(F32)).astype(BF16)
            for g in range(left.shape[1] // LANES):
                size = min(group, slots - g * group)
                mask = lane_mask(ranges, g * group, size, rank, rows, 1)
                part = jnp.where(mask, proj[:, : size * rank].astype(F32), 0.0)
                if size < group:
                    part = jnp.concatenate(
                        [part, jnp.zeros((rows, LANES - size * rank), F32)], axis=1
                    )
                left[here, g * LANES : (g + 1) * LANES] = part.astype(BF16)
        right[...] = jnp.zeros_like(right)

    for base, block in zip(bases, blocks):
        right[base * rank : base * rank + block.shape[0], :] = block[...]
    total = jnp.dot(left[...], right[...], preferred_element_type=F32)
    for term in added:
        total = total + term[...].astype(F32)
    out[...] = total.astype(BF16)


def final(ranges, own, got, added, blocks, bases, rows):
    total_rows = own.shape[0]
    rank, columns = blocks[0].shape[1:]
    flat = [b.reshape(-1, columns) for b in blocks]
    tile = min(256, columns)
    deep = -(-sum(f.shape[0] for f in flat) // LANES) * LANES
    whole = pl.BlockSpec((total_rows, LANES), lambda j: (0, 0))
    part = pl.BlockSpec((total_rows, tile), lambda j: (0, j))
    return pl.pallas_call(
        functools.partial(final_kernel, bases, rank, rows, len(added)),
        grid=(columns // tile,),
        out_shape=jax.ShapeDtypeStruct((total_rows, columns), BF16),
        in_specs=[IN_SMEM, whole, whole]
        + [part] * len(added)
        + [pl.BlockSpec((f.shape[0], tile), lambda j: (0, j)) for f in flat],
        out_specs=part,
        scratch_shapes=[pltpu.VMEM((total_rows, deep), BF16), pltpu.VMEM((deep, tile), BF16)],
        compiler_params=PARAMS,
        cost_estimate=SMALL,
        name="final",
    )(ranges, own, got, *added, *flat)


def send(value, hop, owners):
    return lax.ppermute(value, "rollout", [(i, i ^ hop) for i in range(owners)])


class Extra:

    def __init__(self, sizes, counts):
        rows, owners = sizes.rows, sizes.owners
        self.sizes = sizes
        self.me = lax.axis_index("rollout")
        order = jnp.arange(sizes.adapters, dtype=I32)
        bounds = jnp.sum(jnp.where(order[:, None] <= order[None, :], counts[:, None], 0), axis=0)

        def at_most(positions):
            return jnp.sum((bounds <= positions[:, None]).astype(I32), axis=-1)

        self.row_adapter = at_most(self.me * rows + jnp.arange(rows, dtype=I32))
        device = jnp.arange(owners, dtype=I32)
        low = at_most(device * rows)
        owner = device[:, None]
        low_pair = low[device // 2 * 2][None, :]
        self.covered = jnp.where(
            (owner % 2) == (device[None, :] % 2),
            pair_start(owner, low_pair, sizes) + sizes.kept,
            forward_start(owner, low[None, :], low_pair, sizes) + sizes.passed,
        )

    def blocks(self, stored, turn):
        sizes, me = self.sizes, self.me
        blocks, adapters = [], []
        for hop in range(sizes.owners):
            wanted = jnp.minimum(self.covered[me, me ^ hop] + turn, sizes.held - 1)
            block = lax.dynamic_slice_in_dim(stored, wanted, 1, axis=0)
            blocks.append(block if hop == 0 else send(block, hop, sizes.owners))
            source = me ^ hop
            slot = self.covered[source, me] + turn
            adapters.append(jnp.where(slot < sizes.held, source + sizes.owners * slot, -1))
        return jnp.concatenate(blocks), self.row_adapter[:, None] == jnp.stack(adapters)[None, :]

    def more_rank(self, hidden, down, turn, total):
        blocks, mask = self.blocks(down, turn)
        rank = blocks.shape[1]
        every = jnp.einsum("srd,nkd->srnk", hidden, blocks, preferred_element_type=F32)
        more = jnp.sum(every * mask[None, :, :, None].astype(F32), axis=2)
        return total + jnp.concatenate([more] * (LANES // rank), axis=2).reshape(total.shape)

    def more_delta(self, rank_proj, up, turn, total):
        blocks, mask = self.blocks(up, turn)
        wide = rank_proj[:, :, None, :] * mask[None, :, :, None].astype(BF16)
        wide = wide.reshape(wide.shape[:2] + (-1,))
        more = jnp.einsum(
            "srw,wc->src",
            wide,
            blocks.reshape(-1, blocks.shape[2]),
            preferred_element_type=F32,
        )
        return total + more.reshape(total.shape)


def local(hidden, counts, key_value_weight, down, up):
    steps, rows, width = hidden.shape
    owners = lax.axis_size("rollout")
    sides = lax.axis_size("tensor")
    held, rank = down.shape[:2]
    sizes = Sizes(owners, counts.shape[0], held, rows)
    pairs = sizes.pairs
    side = lax.axis_index("tensor")
    flat = hidden.reshape(steps * rows, width)
    own_columns = key_value_weight.shape[1] // sides

    *to_pairs, to_side, bounds, windows = pack(sizes, counts, down)
    from_pairs = [send(b, 2 * m, owners) for m, b in zip(range(1, pairs), to_pairs)]
    from_side = send(to_side, 1, owners)

    ranges, extra = ranges_of(sizes, bounds, windows)
    *to_pairs_up, to_side_up, kept_up = pack_again(sizes, windows, up)

    if sides == 2:
        side_index = jnp.reshape(side, (1,)).astype(I32)
        theirs = base_product(1 - side_index, flat, key_value_weight, own_columns)
        added = [
            lax.ppermute(theirs, "tensor", [(0, 1), (1, 0)]),
            base_product(side_index, flat, key_value_weight, own_columns),
        ]
    else:
        partial = jnp.dot(flat, key_value_weight, preferred_element_type=F32).astype(BF16)
        added = [lax.psum_scatter(partial, "tensor", scatter_dimension=1, tiled=True)]

    group_count = lax.axis_size("groups")
    rounds = extra
    for turn in range(1, group_count):
        around = [(i, (i + turn) % group_count) for i in range(group_count)]
        rounds = jnp.maximum(rounds, lax.ppermute(extra, "groups", around))
    more = rounds[0] > 0

    kept = [cut(windows, 0, down, sizes.kept)] + from_pairs
    passed = [from_side] + [
        send(cut(windows, pairs + 1 + m, block, sizes.passed), 1, owners)
        for m, block in zip(range(1, pairs), from_pairs)
    ]
    kept_bases = [sizes.kept_base(m) for m in range(pairs)]
    passed_bases = [sizes.passed_base(m) for m in range(pairs)]

    acc = None
    for m in range(pairs - 1):
        acc = scores(ranges, flat, [kept[m]], [kept_bases[m]], rows, acc)[0]
        acc = scores(ranges, flat, [passed[m]], [passed_bases[m]], rows, acc)[0]
    acc = scores(ranges, flat, [kept[-1]], [kept_bases[-1]], rows, acc)[0]
    own, sent = scores(ranges, flat, [passed[-1]], [passed_bases[-1]], rows, acc, fold=True)

    def all_rank():
        rest = Extra(sizes, counts)
        total = lax.fori_loop(
            0, rounds[0], functools.partial(rest.more_rank, hidden, down), own
        )
        return total, total.astype(BF16)

    own, sent = lax.cond(more, all_rank, lambda: (own, sent))
    if sides == 2:
        got = lax.ppermute(sent, "tensor", [(0, 1), (1, 0)])
    else:
        got = lax.psum(sent, "tensor")
        own = jnp.zeros_like(own)

    from_pairs_up = [send(b, 2 * m, owners) for m, b in zip(range(1, pairs), to_pairs_up)]
    kept_ups = [kept_up] + from_pairs_up
    passed_ups = [send(to_side_up, 1, owners)] + [
        send(cut(windows, pairs + 1 + m, block, sizes.passed), 1, owners)
        for m, block in zip(range(1, pairs), from_pairs_up)
    ]

    def finish(terms):
        return final(
            ranges, own, got, terms, kept_ups + passed_ups, kept_bases + passed_bases, rows
        )

    def all_delta():
        rest = Extra(sizes, counts)
        proj = (own + got.astype(F32)).astype(BF16)[:, :rank].reshape(steps, rows, rank)
        delta = lax.fori_loop(
            0,
            rounds[0],
            functools.partial(rest.more_delta, proj, up),
            jnp.zeros(added[0].shape, F32),
        )
        return finish(added + [delta])

    out = lax.cond(more, all_delta, lambda: finish(added))
    return out.reshape(steps, rows, own_columns).transpose(2, 0, 1)


def solution(mesh):
    placed = (
        P(None, ("groups", "rollout"), "tensor"),
        P("groups"),
        P("tensor", None),
        P(("groups", "rollout"), None, "tensor"),
        P(("groups", "rollout"), None, "tensor"),
    )
    return jax.shard_map(
        local,
        mesh=mesh,
        in_specs=placed,
        out_specs=P("tensor", None, ("groups", "rollout")),
        check_vma=False,
    )
```

time: 381 us -> 197 us (0.52)
  waiting for transfers between devices: 258 us -> 61.1 us
  Pallas kernels: 0 us -> 98.5 us
  matrix products: 88.5 us -> 0 us
  starting transfers between devices: 0.4 us -> 32.7 us
  between operations: 15.1 us -> 1.7 us
  local copies, waits for them, and re-layouts: 13.1 us -> 2.51 us
  blocking collectives: 3.81 us -> 0 us
    all_gather x2 -> x0, waiting for transfers between devices: 256 us -> none  [the longest x1 223 us: local(): lax.all_gather(down_factor_weight, 'rollout', axis=0, tiled=True)]
    pallas_call x0 -> x21, Pallas kernels: none -> 98.5 us  [the longest x8 39.4 us: scores(): pl.pallas_call(functools.partial(scores_kernel, bases, rank, rows, fold,...]
    dot_general x6 -> x0, matrix products: 88.5 us -> none  [the longest x4 43.4 us: term_one(): jnp.einsum('dk,rd->kr', key_value_weight, step_rows, preferred_element_ty...]
    ppermute x0 -> x17, waiting for transfers between devices: none -> 61.1 us  [the longest x14 61.1 us: send(): return lax.ppermute(value, 'rollout', [(i, i ^ hop) for i in range(owners)])]
    ppermute x0 -> x17, starting transfers between devices: none -> 32.7 us  [the longest x14 31.1 us: send(): return lax.ppermute(value, 'rollout', [(i, i ^ hop) for i in range(owners)])]
    mul x1 -> x0, local copies, waits for them, and re-layouts: 8.08 us -> none  [local(): rank_proj[:, :, None, :] * onehot[None, :, :, None]]
    reshape x1 -> x0, local copies, waits for them, and re-layouts: 4.92 us -> none  [adapter_order(): gathered.reshape((owners, slots // owners) + gathered.shape[1:])]
  transfers between devices with their start and end apart: 6 -> 17, of which waited for: 2 -> 4; matrix products, arithmetic and copies ran while one was open for 23% -> 0% of each run, Pallas kernels for 0% -> 35%
where the time goes in v2:
time: 197 us
  Pallas kernels  98.5 us (50%)
  waiting for transfers between devices  61.1 us (31%)
  starting transfers between devices  32.7 us (17%)
  local copies, waits for them, and re-layouts  2.51 us (1%)
    ppermute x14, waiting for transfers between devices, send(): return lax.ppermute(value, 'rollout', [(i, i ^ hop) for i in range(owners)])  61.1 us
    pallas_call x8, Pallas kernels, scores(): pl.pallas_call(functools.partial(scores_kernel, bases, rank, rows, fold,...  39.4 us
    ppermute x14, starting transfers between devices, send(): return lax.ppermute(value, 'rollout', [(i, i ^ hop) for i in range(owners)])  31.1 us
    pallas_call x2, Pallas kernels, base_product(): pl.pallas_call(base_kernel, grid_spec=pltpu.PrefetchScalarGridSpec(num_sc...  22.3 us
    pallas_call x1, Pallas kernels, pack(): pl.pallas_call(functools.partial(pack_kernel, sizes), out_shape=[block] *...  18.8 us
    pallas_call x7, Pallas kernels, cut(): pl.pallas_call(functools.partial(cut_kernel, index, size), out_shape=jax....  6.83 us
    pallas_call x1, Pallas kernels, final(): pl.pallas_call(functools.partial(final_kernel, bases, rank, rows, len(add...  5.23 us
    pallas_call x1, Pallas kernels, ranges_of(): pl.pallas_call(functools.partial(ranges_kernel, sizes), out_shape=[jax.Sh...  4.41 us
  transfers between devices with their start and end apart: 17, of which 4 were waited for; matrix products, arithmetic and copies ran while one was open for 0% of the time, Pallas kernels for 35%

profile of v2, /device:TPU:0, one launch (start us, length us, event | category | flops | bytes accessed | tf_op | source)
XLA Modules:
  0.0 196.6 jit_solution(16140925750280288088)
XLA Ops:
  0.0 18.8 %pack.1 = (bf16[3,32,4096]{2,1,0:T(8,128)(2,1)S(1)}, bf16[3,32,4096]{2,1,0:T(8,128)(2,1)S(1)}, bf16[3,32,4096]{2,1,0:T(8,128)(2,1)S(1)}, bf16[2,32,4096]{2,1,0:T...) custom-call(s32[64]{0:T(128)} %counts.1, bf16[8,32,4096]{2,1,0:T(8,128)(2,1)} %block.1), custom_call_target="tpu_custom_call" | custom-call | flops 1000 | bytes 1000 | tf_op jit(solution)/shard_map/pack/pallas_call | solution.py:111
  18.8 3.1 %collective-permute-start.26 = (bf16[3,32,4096]{2,1,0:T(8,128)(2,1)S(1)}, bf16[3,32,4096]{2,1,0:T(8,128)(2,1)S(1)}, u32[]{:S(2)}, u32[]{:S(2)}) collective-permute-start(bf16[3,32,4096]{2,1,0:T(8,128)(2,1)S(1)} %get-tuple-element.595), channel_id=1, source_target_pairs={{0,4},{2,6},{4,0},{6,2},{8,12},{10,14},{12,8},{14,10},{1,5},{3,7},... | collective-permute-start | bytes 2359304 | tf_op jit(solution)/shard_map/ppermute | solution.py:417
  21.9 2.6 %collective-permute-start.24 = (bf16[3,32,4096]{2,1,0:T(8,128)(2,1)S(1)}, bf16[3,32,4096]{2,1,0:T(8,128)(2,1)S(1)}, u32[]{:S(2)}, u32[]{:S(2)}) collective-permute-start(bf16[3,32,4096]{2,1,0:T(8,128)(2,1)S(1)} %get-tuple-element.594), channel_id=1, source_target_pairs={{0,8},{2,10},{4,12},{6,14},{8,0},{10,2},{12,4},{14,6},{1,9},{3,11}... | collective-permute-start | bytes 2359304 | tf_op jit(solution)/shard_map/ppermute | solution.py:417
  24.5 1.7 collective-permute-start.28
  26.2 29.3 %collective-permute-done.26.block = bf16[3,32,4096]{2,1,0:T(8,128)(2,1)S(1)} collective-permute-done((bf16[3,32,4096]{2,1,0:T(8,128)(2,1)S(1)}, bf16[3,32,4096]{2,1,0:T(8,128)(2,1)S(1)}, u32[]{:S(2)}, u32[]{:S(2)}) %collective-permute-start.26) | collective-permute-done | bytes 786464 | tf_op jit(solution)/shard_map/ppermute | solution.py:417
  56.9 1.7 collective-permute-start.27
  58.6 18.4 %collective-permute-done.24.block = bf16[3,32,4096]{2,1,0:T(8,128)(2,1)S(1)} collective-permute-done((bf16[3,32,4096]{2,1,0:T(8,128)(2,1)S(1)}, bf16[3,32,4096]{2,1,0:T(8,128)(2,1)S(1)}, u32[]{:S(2)}, u32[]{:S(2)}) %collective-permute-start.24) | collective-permute-done | bytes 786464 | tf_op jit(solution)/shard_map/ppermute | solution.py:417
  81.9 4.4 %ranges.1 = (s32[40]{0:T(128)S(1)}, s32[1]{0:T(128)}) custom-call(s32[65]{0:T(128)S(1)} %get-tuple-element.584.bounds, s32[11]{0:T(128)S(1)} %get-tuple-element.585.windows), custom_call_target="tpu_custom_call" | custom-call | flops 1000 | bytes 1000 | tf_op jit(solution)/shard_map/ranges/pallas_call | solution.py:235
  86.3 1.6 collective-permute-start.14
  88.5 10.8 %base_product.2 = bf16[768,1024]{1,0:T(8,128)(2,1)S(1)} custom-call(s32[1]{0:T(128)S(6)} %sub.54.which, bf16[768,4096]{1,0:T(8,128)(2,1)} %bitcast.73.hidden, bf16[4096,2048]{1,0:T(8,128)(2,1)} %weight.3), custom_call_target="tpu_custom_call" | custom-call | flops 1000 | bytes 1000 | tf_op jit(solution)/shard_map/base_product/pallas_call | solution.py:343
  100.5 4.9 %scores.8.refs_1_ = f32[768,128]{1,0:T(8,128)S(1)} custom-call(s32[40]{0:T(128)S(1)} %get-tuple-element.592.ranges, bf16[768,4096]{1,0:T(8,128)(2,1)} %bitcast.73.hidden, bf16[96,4096]{1,0:T(8,128)(2,1)S(1)} %bitcast.223), custom_call_target="tpu_custom_call" | custom-call | flops 1000 | bytes 1000 | tf_op jit(solution)/shard_map/scores/pallas_call | solution.py:320
  106.8 4.9 %scores.9.refs_1_ = f32[768,128]{1,0:T(8,128)S(1)} custom-call(s32[40]{0:T(128)S(1)} %get-tuple-element.592.ranges, bf16[768,4096]{1,0:T(8,128)(2,1)} %bitcast.73.hidden, bf16[64,4096]{1,0:T(8,128)(2,1)} %bitcast.80.refs_0_, f32[768,128]{1,0:T(8,128)S(1)} %scores.8.refs_1_), custom_call_target="tpu_custom_call" | custom-call | flops 1000 | bytes 1000 | tf_op jit(solution)/shard_map/scores/pallas_call | solution.py:320
  111.6 4.9 %scores.10.refs_1_ = f32[768,128]{1,0:T(8,128)S(1)} custom-call(s32[40]{0:T(128)S(1)} %get-tuple-element.592.ranges, bf16[768,4096]{1,0:T(8,128)(2,1)} %bitcast.73.hidden, bf16[96,4096]{1,0:T(8,128)(2,1)S(1)} %bitcast.226, f32[768,128]{1,0:T(8,128)S(1)} %scores.9.refs_1_), custom_call_target="tpu_custom_call" | custom-call | flops 1000 | bytes 1000 | tf_op jit(solution)/shard_map/scores/pallas_call | solution.py:320
  116.6 4.9 %scores.11.refs_1_ = f32[768,128]{1,0:T(8,128)S(1)} custom-call(s32[40]{0:T(128)S(1)} %get-tuple-element.592.ranges, bf16[768,4096]{1,0:T(8,128)(2,1)} %bitcast.73.hidden, bf16[64,4096]{1,0:T(8,128)(2,1)} %bitcast.78.refs_0_, f32[768,128]{1,0:T(8,128)S(1)} %scores.10.refs_1_), custom_call_target="tpu_custom_call" | custom-call | flops 1000 | bytes 1000 | tf_op jit(solution)/shard_map/scores/pallas_call | solution.py:320
  121.5 4.9 %scores.12.refs_1_ = f32[768,128]{1,0:T(8,128)S(1)} custom-call(s32[40]{0:T(128)S(1)} %get-tuple-element.592.ranges, bf16[768,4096]{1,0:T(8,128)(2,1)} %bitcast.73.hidden, bf16[96,4096]{1,0:T(8,128)(2,1)S(1)} %bitcast.225, f32[768,128]{1,0:T(8,128)S(1)} %scores.11.refs_1_), custom_call_target="tpu_custom_call" | custom-call | flops 1000 | bytes 1000 | tf_op jit(solution)/shard_map/scores/pallas_call | solution.py:320
  126.4 4.9 %scores.13.refs_1_ = f32[768,128]{1,0:T(8,128)S(1)} custom-call(s32[40]{0:T(128)S(1)} %get-tuple-element.592.ranges, bf16[768,4096]{1,0:T(8,128)(2,1)} %bitcast.73.hidden, bf16[64,4096]{1,0:T(8,128)(2,1)} %bitcast.76.refs_0_, f32[768,128]{1,0:T(8,128)S(1)} %scores.12.refs_1_), custom_call_target="tpu_custom_call" | custom-call | flops 1000 | bytes 1000 | tf_op jit(solution)/shard_map/scores/pallas_call | solution.py:320
  131.3 4.9 %scores.14.refs_1_ = f32[768,128]{1,0:T(8,128)S(1)} custom-call(s32[40]{0:T(128)S(1)} %get-tuple-element.592.ranges, bf16[768,4096]{1,0:T(8,128)(2,1)} %bitcast.73.hidden, bf16[96,4096]{1,0:T(8,128)(2,1)S(1)} %bitcast.224, f32[768,128]{1,0:T(8,128)S(1)} %scores.13.refs_1_), custom_call_target="tpu_custom_call" | custom-call | flops 1000 | bytes 1000 | tf_op jit(solution)/shard_map/scores/pallas_call | solution.py:320
  136.2 5.2 %scores.15 = (f32[768,128]{1,0:T(8,128)S(1)}, bf16[768,128]{1,0:T(8,128)(2,1)S(1)}) custom-call(s32[40]{0:T(128)S(1)} %get-tuple-element.592.ranges, bf16[768,4096]{1,0:T(8,128)(2,1)} %bitcast.73.hidden, bf16[64,4096]{1,0:T(8,128)(2,1)} %bitcast.74.refs_0_, f32[768,128]{1,0:T(8,128)S(1)} %scores.14.refs_1_), custom_call_target="tpu_custom_call" | custom-call | flops 1000 | bytes 1000 | tf_op jit(solution)/shard_map/scores/pallas_call | solution.py:320
  144.5 14.1 %collective-permute-start.15 = (bf16[3,32,1024]{2,1,0:T(8,128)(2,1)S(1)}, bf16[3,32,1024]{2,1,0:T(8,128)(2,1)S(1)}, u32[]{:S(2)}, u32[]{:S(2)}) collective-permute-start(bf16[3,32,1024]{2,1,0:T(8,128)(2,1)S(1)} %get-tuple-element.588), channel_id=1, source_target_pairs={{0,4},{2,6},{4,0},{6,2},{8,12},{10,14},{12,8},{14,10},{1,5},{3,7},... | collective-permute-start | bytes 589832 | tf_op jit(solution)/shard_map/ppermute | solution.py:417
  161.6 6.2 %collective-permute-done.15.block = bf16[3,32,1024]{2,1,0:T(8,128)(2,1)S(1)} collective-permute-done((bf16[3,32,1024]{2,1,0:T(8,128)(2,1)S(1)}, bf16[3,32,1024]{2,1,0:T(8,128)(2,1)S(1)}, u32[]{:S(2)}, u32[]{:S(2)}) %collective-permute-start.15) | collective-permute-done | bytes 196640 | tf_op jit(solution)/shard_map/ppermute | solution.py:417
  168.5 7.2 %collective-permute-done.16.block = bf16[3,32,1024]{2,1,0:T(8,128)(2,1)S(1)} collective-permute-done((bf16[3,32,1024]{2,1,0:T(8,128)(2,1)S(1)}, bf16[3,32,1024]{2,1,0:T(8,128)(2,1)S(1)}, u32[]{:S(2)}, u32[]{:S(2)}) %collective-permute-start.16) | collective-permute-done | bytes 196640 | tf_op jit(solution)/shard_map/ppermute | solution.py:417
  179.9 11.5 %base_product.3 = bf16[768,1024]{1,0:T(8,128)(2,1)} custom-call(s32[1]{0:T(128)} %bitcast.82.which, bf16[768,4096]{1,0:T(8,128)(2,1)} %bitcast.73.hidden, bf16[4096,2048]{1,0:T(8,128)(2,1)} %weight.3), custom_call_target="tpu_custom_call" | custom-call | flops 1000 | bytes 1000 | tf_op jit(solution)/shard_map/base_product/pallas_call | solution.py:343
  191.4 5.2 %conditional.3 = (bf16[768,1024]{1,0:T(8,128)(2,1)}) conditional(s32[]{:T(128)} %bitcast.72, (bf16[3,32,1024]{2,1,0:T(8,128)(2,1)}, bf16[3,32,1024]{2,1,0:T(8,128)(2,1)S(1)}, bf16[3,32,1024]{2,1,0:T(8,128)(2,1)S(1)}, bf16[3,32,1024]{2,1,0:T(8,128)(2,1)S(1)}, bf16[2,32,1024]{2,1,0:T(8,128)(2,1)S(1)}, /*index=5*/bf16[2,32,1024]{2,1,0:T(8,128)(2,1)S(1)}, ...), branch_computations={%region_8.9_spmd, %region_9.15_spmd} | conditional | flops 403767392 | bytes 24742120 | solution.py:563
  191.4 5.2 %final.2 = bf16[768,1024]{1,0:T(8,128)(2,1)} custom-call(s32[40]{0:T(128)S(1)} %get-tuple-element.507.ranges, f32[768,128]{1,0:T(8,128)S(1)} %get-tuple-element.508.own, bf16[768,128]{1,0:T(8,128)(2,1)S(1)} %get-tuple-element.509.refs_0_, bf16[768,1024]{1,0:T(8,128)(2,1)} %get-tuple-element.510.refs_1_, bf16[768,1024]{1,0:T(8,128)(2,1)} %get-tuple-element.511.refs_2_, ...), custom_call_target="tpu_custom_call" | custom-call | flops 1000 | bytes 1000 | tf_op jit(solution)/shard_map/cond/branch_0_fun/final/pallas_call | solution.py:401
  (45 shorter events, 19.0 us)
Async XLA Ops:
  18.8 69.1 %copy-start.2 = (bf16[8,32,4096]{2,1,0:T(8,128)(2,1)S(1)}, bf16[8,32,4096]{2,1,0:T(8,128)(2,1)}, u32[]{:S(2)}) copy-start(bf16[8,32,4096]{2,1,0:T(8,128)(2,1)} %block.1) | copy-start | bytes 6291460
  18.8 36.7 %collective-permute-start.26 = (bf16[3,32,4096]{2,1,0:T(8,128)(2,1)S(1)}, bf16[3,32,4096]{2,1,0:T(8,128)(2,1)S(1)}, u32[]{:S(2)}, u32[]{:S(2)}) collective-permute-start(bf16[3,32,4096]{2,1,0:T(8,128)(2,1)S(1)} %get-tuple-element.595), channel_id=1, source_target_pairs={{0,4},{2,6},{4,0},{6,2},{8,12},{10,14},{12,8},{14,10},{1,5},{3,7},... | collective-permute-start | bytes 2359304 | tf_op jit(solution)/shard_map/ppermute | solution.py:417
  21.9 55.1 %collective-permute-start.24 = (bf16[3,32,4096]{2,1,0:T(8,128)(2,1)S(1)}, bf16[3,32,4096]{2,1,0:T(8,128)(2,1)S(1)}, u32[]{:S(2)}, u32[]{:S(2)}) collective-permute-start(bf16[3,32,4096]{2,1,0:T(8,128)(2,1)S(1)} %get-tuple-element.594), channel_id=1, source_target_pairs={{0,8},{2,10},{4,12},{6,14},{8,0},{10,2},{12,4},{14,6},{1,9},{3,11}... | collective-permute-start | bytes 2359304 | tf_op jit(solution)/shard_map/ppermute | solution.py:417
  24.5 55.4 %collective-permute-start.22 = (bf16[3,32,4096]{2,1,0:T(8,128)(2,1)S(1)}, bf16[3,32,4096]{2,1,0:T(8,128)(2,1)S(1)}, u32[]{:S(2)}, u32[]{:S(2)}) collective-permute-start(bf16[3,32,4096]{2,1,0:T(8,128)(2,1)S(1)} %get-tuple-element.593), channel_id=1, source_target_pairs={{0,12},{2,14},{4,8},{6,10},{8,4},{10,6},{12,0},{14,2},{1,13},{3,15... | collective-permute-start | bytes 2359304 | tf_op jit(solution)/shard_map/ppermute | solution.py:417
  24.5 82.2 %collective-permute-start.28 = (bf16[2,32,4096]{2,1,0:T(8,128)(2,1)}, bf16[2,32,4096]{2,1,0:T(8,128)(2,1)}, u32[]{:S(2)}, u32[]{:S(2)}) collective-permute-start(bf16[2,32,4096]{2,1,0:T(8,128)(2,1)} %get-tuple-element.596), channel_id=1, source_target_pairs={{0,2},{2,0},{4,6},{6,4},{8,10},{10,8},{12,14},{14,12},{1,3},{3,1},... | collective-permute-start | bytes 1572872 | tf_op jit(solution)/shard_map/ppermute | solution.py:417
  56.9 59.7 %collective-permute-start.27 = (bf16[2,32,4096]{2,1,0:T(8,128)(2,1)}, bf16[2,32,4096]{2,1,0:T(8,128)(2,1)}, u32[]{:S(2)}, u32[]{:S(2)}) collective-permute-start(bf16[2,32,4096]{2,1,0:T(8,128)(2,1)} %cut.12), channel_id=1, source_target_pairs={{0,2},{2,0},{4,6},{6,4},{8,10},{10,8},{12,14},{14,12},{1,3},{3,1},... | collective-permute-start | bytes 1572872 | tf_op jit(solution)/shard_map/ppermute | solution.py:417
  78.3 48.0 %collective-permute-start.25 = (bf16[2,32,4096]{2,1,0:T(8,128)(2,1)}, bf16[2,32,4096]{2,1,0:T(8,128)(2,1)}, u32[]{:S(2)}, u32[]{:S(2)}) collective-permute-start(bf16[2,32,4096]{2,1,0:T(8,128)(2,1)} %cut.11), channel_id=1, source_target_pairs={{0,2},{2,0},{4,6},{6,4},{8,10},{10,8},{12,14},{14,12},{1,3},{3,1},... | collective-permute-start | bytes 1572872 | tf_op jit(solution)/shard_map/ppermute | solution.py:417
  81.3 54.9 %collective-permute-start.23 = (bf16[2,32,4096]{2,1,0:T(8,128)(2,1)}, bf16[2,32,4096]{2,1,0:T(8,128)(2,1)}, u32[]{:S(2)}, u32[]{:S(2)}) collective-permute-start(bf16[2,32,4096]{2,1,0:T(8,128)(2,1)} %cut.10), channel_id=1, source_target_pairs={{0,2},{2,0},{4,6},{6,4},{8,10},{10,8},{12,14},{14,12},{1,3},{3,1},... | collective-permute-start | bytes 1572872 | tf_op jit(solution)/shard_map/ppermute | solution.py:417
  86.3 19.1 %collective-permute-start.14 = (s32[1]{0:T(128)}, s32[1]{0:T(128)}, u32[]{:S(2)}, u32[]{:S(2)}) collective-permute-start(s32[1]{0:T(128)} %get-tuple-element.586), channel_id=1, source_target_pairs={{0,16},{16,0},{1,17},{17,1},{2,18},{18,2},{3,19},{19,3},{4,20},{20... | collective-permute-start | bytes 20 | tf_op jit(solution)/shard_map/ppermute | solution.py:508
  99.3 1.1 copy-start
  136.2 5.2 %copy-start.12 = (s32[64]{0:T(128)S(1)}, s32[64]{0:T(128)}, u32[]{:S(2)}) copy-start(s32[64]{0:T(128)} %counts.1) | copy-start | bytes 772
  141.4 1.5 copy-start.1
  141.4 1.6 copy-start.4
  141.6 2.9 %copy-start.13 = (bf16[768,128]{1,0:T(8,128)(2,1)}, bf16[768,128]{1,0:T(8,128)(2,1)S(1)}, u32[]{:S(2)}) copy-start(bf16[768,128]{1,0:T(8,128)(2,1)S(1)} %get-tuple-element.599) | copy-start | bytes 589828
  142.9 48.5 %collective-permute-start.30 = (bf16[768,1024]{1,0:T(8,128)(2,1)S(1)}, bf16[768,1024]{1,0:T(8,128)(2,1)}, u32[]{:S(2)}, u32[]{:S(2)}) collective-permute-start(bf16[768,1024]{1,0:T(8,128)(2,1)S(1)} %copy-done.1), channel_id=1, source_target_pairs={{0,1},{1,0},{2,3},{3,2},{4,5},{5,4},{6,7},{7,6},{8,9},{9,8},{10,11... | collective-permute-start | bytes 4718600 | tf_op jit(solution)/shard_map/ppermute | solution.py:497
  144.5 23.3 %collective-permute-start.15 = (bf16[3,32,1024]{2,1,0:T(8,128)(2,1)S(1)}, bf16[3,32,1024]{2,1,0:T(8,128)(2,1)S(1)}, u32[]{:S(2)}, u32[]{:S(2)}) collective-permute-start(bf16[3,32,1024]{2,1,0:T(8,128)(2,1)S(1)} %get-tuple-element.588), channel_id=1, source_target_pairs={{0,4},{2,6},{4,0},{6,2},{8,12},{10,14},{12,8},{14,10},{1,5},{3,7},... | collective-permute-start | bytes 589832 | tf_op jit(solution)/shard_map/ppermute | solution.py:417
  158.6 17.1 %collective-permute-start.16 = (bf16[3,32,1024]{2,1,0:T(8,128)(2,1)S(1)}, bf16[3,32,1024]{2,1,0:T(8,128)(2,1)S(1)}, u32[]{:S(2)}, u32[]{:S(2)}) collective-permute-start(bf16[3,32,1024]{2,1,0:T(8,128)(2,1)S(1)} %get-tuple-element.589), channel_id=1, source_target_pairs={{0,8},{2,10},{4,12},{6,14},{8,0},{10,2},{12,4},{14,6},{1,9},{3,11}... | collective-permute-start | bytes 589832 | tf_op jit(solution)/shard_map/ppermute | solution.py:417
  159.7 17.3 %collective-permute-start.17 = (bf16[3,32,1024]{2,1,0:T(8,128)(2,1)S(1)}, bf16[3,32,1024]{2,1,0:T(8,128)(2,1)S(1)}, u32[]{:S(2)}, u32[]{:S(2)}) collective-permute-start(bf16[3,32,1024]{2,1,0:T(8,128)(2,1)S(1)} %get-tuple-element.590), channel_id=1, source_target_pairs={{0,12},{2,14},{4,8},{6,10},{8,4},{10,6},{12,0},{14,2},{1,13},{3,15... | collective-permute-start | bytes 589832 | tf_op jit(solution)/shard_map/ppermute | solution.py:417
  161.0 18.2 %collective-permute-start.18 = (bf16[2,32,1024]{2,1,0:T(8,128)(2,1)S(1)}, bf16[2,32,1024]{2,1,0:T(8,128)(2,1)S(1)}, u32[]{:S(2)}, u32[]{:S(2)}) collective-permute-start(bf16[2,32,1024]{2,1,0:T(8,128)(2,1)S(1)} %get-tuple-element.591), channel_id=1, source_target_pairs={{0,2},{2,0},{4,6},{6,4},{8,10},{10,8},{12,14},{14,12},{1,3},{3,1},... | collective-permute-start | bytes 393224 | tf_op jit(solution)/shard_map/ppermute | solution.py:417
  167.8 23.6 %collective-permute-start.29 = (bf16[768,128]{1,0:T(8,128)(2,1)}, bf16[768,128]{1,0:T(8,128)(2,1)S(1)}, u32[]{:S(2)}, u32[]{:S(2)}) collective-permute-start(bf16[768,128]{1,0:T(8,128)(2,1)} %copy-done.13), channel_id=1, source_target_pairs={{0,1},{1,0},{2,3},{3,2},{4,5},{5,4},{6,7},{7,6},{8,9},{9,8},{10,11... | collective-permute-start | bytes 589832 | tf_op jit(solution)/shard_map/ppermute | solution.py:535
  175.7 15.7 %collective-permute-start.19 = (bf16[2,32,1024]{2,1,0:T(8,128)(2,1)S(1)}, bf16[2,32,1024]{2,1,0:T(8,128)(2,1)S(1)}, u32[]{:S(2)}, u32[]{:S(2)}) collective-permute-start(bf16[2,32,1024]{2,1,0:T(8,128)(2,1)S(1)} %cut.7), channel_id=1, source_target_pairs={{0,2},{2,0},{4,6},{6,4},{8,10},{10,8},{12,14},{14,12},{1,3},{3,1},... | collective-permute-start | bytes 393224 | tf_op jit(solution)/shard_map/ppermute | solution.py:417
  177.0 14.4 %collective-permute-start.20 = (bf16[2,32,1024]{2,1,0:T(8,128)(2,1)S(1)}, bf16[2,32,1024]{2,1,0:T(8,128)(2,1)}, u32[]{:S(2)}, u32[]{:S(2)}) collective-permute-start(bf16[2,32,1024]{2,1,0:T(8,128)(2,1)S(1)} %cut.8), channel_id=1, source_target_pairs={{0,2},{2,0},{4,6},{6,4},{8,10},{10,8},{12,14},{14,12},{1,3},{3,1},... | collective-permute-start | bytes 393224 | tf_op jit(solution)/shard_map/ppermute | solution.py:417
  179.3 12.1 %collective-permute-start.21 = (bf16[2,32,1024]{2,1,0:T(8,128)(2,1)S(1)}, bf16[2,32,1024]{2,1,0:T(8,128)(2,1)}, u32[]{:S(2)}, u32[]{:S(2)}) collective-permute-start(bf16[2,32,1024]{2,1,0:T(8,128)(2,1)S(1)} %cut.9), channel_id=1, source_target_pairs={{0,2},{2,0},{4,6},{6,4},{8,10},{10,8},{12,14},{14,12},{1,3},{3,1},... | collective-permute-start | bytes 393224 | tf_op jit(solution)/shard_map/ppermute | solution.py:417

commit v3 on v2

v3 whole, which is shorter than its diff:
```python
import functools

import jax
import jax.numpy as jnp
from jax import lax
from jax.experimental import pallas as pl
from jax.experimental.pallas import tpu as pltpu
from jax.sharding import PartitionSpec as P

PAIR_SLOTS = 3
FORWARD_SLOTS = 2
VMEM_LIMIT = 24 * 1024 * 1024
BF16 = jnp.bfloat16
F32 = jnp.float32
I32 = jnp.int32
SMALL = pl.CostEstimate(flops=1000, bytes_accessed=1000, transcendentals=0)
PARAMS = pltpu.CompilerParams(vmem_limit_bytes=VMEM_LIMIT)
IN_SMEM = pl.BlockSpec(memory_space=pltpu.SMEM)
IN_VMEM = pl.BlockSpec(memory_space=pltpu.VMEM)
ANYWHERE = pl.BlockSpec(memory_space=pl.ANY)


def first_slot(owner, adapter, owners):
    return lax.div(adapter - owner + (owners - 1), jnp.int32(owners))


def end_slot(owner, adapter, owners):
    return lax.div(adapter - owner + owners, jnp.int32(owners))


def pair_start(owner, low_pair, sizes):
    return jnp.minimum(first_slot(owner, low_pair, sizes.owners), sizes.held - sizes.kept)


def forward_start(owner, low, low_pair, sizes):
    return jnp.minimum(
        first_slot(owner, low, sizes.owners),
        pair_start(owner, low_pair, sizes) + (sizes.kept - sizes.passed),
    )


class Sizes:
    def __init__(self, owners, adapters, held, rows):
        self.owners, self.adapters, self.held, self.rows = owners, adapters, held, rows
        self.kept = min(PAIR_SLOTS, held)
        self.passed = min(FORWARD_SLOTS, self.kept)
        self.pairs = owners // 2
        self.slots = self.pairs * (self.kept + self.passed)

    def kept_base(self, m):
        return m * self.kept

    def passed_base(self, m):
        return self.pairs * self.kept + m * self.passed


def pack_kernel(sizes, counts, stored, *refs):
    pairs = sizes.pairs
    sent, (passed0, bounds, windows, low_pair, sems) = refs[: pairs - 1], refs[pairs - 1 :]
    me = lax.axis_index("rollout")
    mine = lax.div(me, jnp.int32(2))
    odd_row = (2 * mine + 1) * sizes.rows
    bounds[0] = jnp.int32(0)

    def add(a, carry):
        end = carry[0] + counts[a]
        bounds[a + 1] = end
        lows = [
            low + (end <= 2 * p * sizes.rows).astype(I32) for p, low in enumerate(carry[1 : pairs + 1])
        ]
        return (end, *lows, carry[pairs + 1] + (end <= odd_row).astype(I32))

    found = lax.fori_loop(0, sizes.adapters, add, (jnp.int32(0),) * (pairs + 2), unroll=8)
    for p in range(pairs):
        low_pair[p] = found[1 + p]
    odd = found[pairs + 1]
    low_mine = low_pair[mine]
    is_even = me == 2 * mine
    low_other = jnp.where(is_even, odd, low_mine)
    copies = []
    for m in range(1, pairs):
        start = pair_start(me, low_pair[mine ^ m], sizes)
        windows[m] = start
        copies.append(
            pltpu.make_async_copy(stored.at[pl.ds(start, sizes.kept)], sent[m - 1], sems.at[m])
        )
    start = forward_start(me, low_other, low_mine, sizes)
    copies.insert(
        0, pltpu.make_async_copy(stored.at[pl.ds(start, sizes.passed)], passed0, sems.at[0])
    )
    for copy in copies:
        copy.start()
    windows[pairs] = start
    windows[0] = pair_start(me, low_mine, sizes)
    for m in range(pairs):
        source = me ^ (2 * m)
        windows[pairs + 1 + m] = forward_start(source, low_other, low_mine, sizes) - pair_start(
            source, low_mine, sizes
        )
    windows[2 * pairs + 1] = low_mine
    windows[2 * pairs + 2] = jnp.where(is_even, low_mine, odd)
    for copy in copies:
        copy.wait()


def in_vmem(size, like):
    return pltpu.VMEM((size,) + like.shape[1:], like.dtype)


def held_in_vmem(value):
    return pltpu.with_memory_space_constraint(value, pltpu.VMEM)


def pack(sizes, counts, stored):
    pairs = sizes.pairs
    return pl.pallas_call(
        functools.partial(pack_kernel, sizes),
        out_shape=[in_vmem(sizes.kept, stored)] * (pairs - 1)
        + [
            in_vmem(sizes.passed, stored),
            jax.ShapeDtypeStruct((sizes.adapters + 1,), I32),
            jax.ShapeDtypeStruct((2 * pairs + 3,), I32),
        ],
        in_specs=[IN_SMEM, ANYWHERE],
        out_specs=[IN_VMEM] * pairs + [IN_SMEM, IN_SMEM],
        scratch_shapes=[pltpu.SMEM((pairs,), I32), pltpu.SemaphoreType.DMA((pairs,))],
        compiler_params=PARAMS,
        cost_estimate=SMALL,
        name="pack",
    )(counts, stored)


def pack_again_kernel(sizes, n_after, windows, stored, *refs):
    refs = refs[n_after:]
    pairs = sizes.pairs
    sent, (passed0, kept0, sems) = refs[: pairs - 1], refs[pairs - 1 :]
    copies = [
        pltpu.make_async_copy(stored.at[pl.ds(windows[m], sizes.kept)], target, sems.at[m])
        for m, target in enumerate((kept0,) + tuple(sent))
    ]
    copies.append(
        pltpu.make_async_copy(
            stored.at[pl.ds(windows[pairs], sizes.passed)], passed0, sems.at[pairs]
        )
    )
    for copy in copies:
        copy.start()
    for copy in copies:
        copy.wait()


def pack_again(sizes, windows, stored, after):
    pairs = sizes.pairs
    return pl.pallas_call(
        functools.partial(pack_again_kernel, sizes, len(after)),
        out_shape=[in_vmem(sizes.kept, stored)] * (pairs - 1)
        + [in_vmem(sizes.passed, stored), in_vmem(sizes.kept, stored)],
        in_specs=[IN_SMEM, ANYWHERE] + [ANYWHERE] * len(after),
        out_specs=[IN_VMEM] * (pairs + 1),
        scratch_shapes=[pltpu.SemaphoreType.DMA((pairs + 1,))],
        compiler_params=PARAMS,
        cost_estimate=SMALL,
        name="pack_again",
    )(windows, stored, *after)


def cut_kernel(index, size, n_after, windows, block, *refs):
    out, sem = refs[n_after:]
    copy = pltpu.make_async_copy(block.at[pl.ds(windows[index], size)], out, sem)
    copy.start()
    copy.wait()


def cut(windows, index, block, size, after=()):
    return pl.pallas_call(
        functools.partial(cut_kernel, index, size, len(after)),
        out_shape=in_vmem(size, block),
        in_specs=[IN_SMEM, ANYWHERE] + [ANYWHERE] * len(after),
        out_specs=IN_VMEM,
        scratch_shapes=[pltpu.SemaphoreType.DMA],
        compiler_params=PARAMS,
        cost_estimate=SMALL,
        name="cut",
    )(windows, block, *after)


def gate_kernel(*refs):
    pass


def gate(values, after):
    n = len(values)
    return pl.pallas_call(
        gate_kernel,
        out_shape=[pltpu.VMEM(v.shape, v.dtype) for v in values],
        in_specs=[IN_VMEM] * n + [ANYWHERE] * len(after),
        out_specs=[IN_VMEM] * n,
        input_output_aliases={i: i for i in range(n)},
        compiler_params=PARAMS,
        cost_estimate=SMALL,
        name="gate",
    )(*[held_in_vmem(v) for v in values], *after)


def ranges_kernel(sizes, bounds, windows, ranges, rounds, lows, highs):
    me = lax.axis_index("rollout")
    low_mine = windows[2 * sizes.pairs + 1]
    low = windows[2 * sizes.pairs + 2]
    first_row = me * sizes.rows

    def fill(base, source, start, size):
        for k in range(size):
            adapter = source + sizes.owners * (start + k)
            ranges[2 * (base + k)] = bounds[adapter] - first_row
            ranges[2 * (base + k) + 1] = bounds[adapter + 1] - first_row

    for m in range(sizes.pairs):
        source = me ^ (2 * m)
        fill(sizes.kept_base(m), source, pair_start(source, low_mine, sizes), sizes.kept)
        source = me ^ 1 ^ (2 * m)
        fill(sizes.passed_base(m), source, forward_start(source, low, low_mine, sizes), sizes.passed)

    for d in range(sizes.owners):
        lows[d] = jnp.int32(0)
        highs[d] = jnp.int32(0)

    def count(a, carry):
        end = bounds[a + 1]
        return tuple(
            c + (end <= d * sizes.rows + last).astype(I32)
            for (d, last), c in zip(places, carry)
        )

    places = [(d, last) for last in (0, sizes.rows - 1) for d in range(sizes.owners)]
    found = lax.fori_loop(0, sizes.adapters, count, (jnp.int32(0),) * len(places))
    for d in range(sizes.owners):
        lows[d] = found[d]
        highs[d] = found[sizes.owners + d]

    def most(d, so_far):
        low_d, high_d, low_p = lows[d], highs[d], lows[lax.div(d, jnp.int32(2)) * 2]

        def each(owner, so_far):
            same = ((owner ^ d) & 1) == 0
            covered = jnp.where(
                same,
                pair_start(owner, low_p, sizes) + sizes.kept,
                forward_start(owner, low_d, low_p, sizes) + sizes.passed,
            )
            return jnp.maximum(so_far, end_slot(owner, high_d, sizes.owners) - covered)

        return lax.fori_loop(0, sizes.owners, each, so_far)

    rounds[0] = lax.fori_loop(0, sizes.owners, most, jnp.int32(0))


def ranges_of(sizes, bounds, windows):
    return pl.pallas_call(
        functools.partial(ranges_kernel, sizes),
        out_shape=[
            jax.ShapeDtypeStruct((2 * sizes.slots,), I32),
            jax.ShapeDtypeStruct((1,), I32),
        ],
        in_specs=[IN_SMEM, IN_SMEM],
        out_specs=[IN_SMEM, IN_SMEM],
        scratch_shapes=[pltpu.SMEM((sizes.owners,), I32), pltpu.SMEM((sizes.owners,), I32)],
        compiler_params=PARAMS,
        cost_estimate=SMALL,
        name="ranges",
    )(bounds, windows)


def row_of_lane(rows, steps):
    lane = lax.broadcasted_iota(I32, (1, steps * rows), 1)
    row = lane
    for s in range(1, steps):
        row = jnp.where(lane >= s * rows, lane - s * rows, row)
    return row


def scores_kernel(bases, rank, rows, fold, n_before, n_after, ranges, hidden, *refs):
    blocks, refs = refs[: len(bases)], refs[len(bases) :]
    before, refs = refs[:n_before], refs[n_before + n_after :]
    width = hidden.shape[1]
    tile = min(1024, width)
    total = None
    for k in range(0, width, tile):
        part = lax.dot_general(
            jnp.concatenate([b[:, k : k + tile] for b in blocks], axis=0),
            hidden[:, k : k + tile],
            (((1,), (1,)), ((), ())),
            preferred_element_type=F32,
        )
        total = part if total is None else total + part
    row = row_of_lane(rows, hidden.shape[0] // rows)
    acc = before[0][...] if n_before else jnp.zeros((rank, hidden.shape[0]), F32)
    place = 0
    for base, block in zip(bases, blocks):
        for k in range(block.shape[0] // rank):
            here = (row >= ranges[2 * (base + k)]) & (row < ranges[2 * (base + k) + 1])
            acc = acc + jnp.where(here, total[place : place + rank, :], 0.0)
            place += rank
    if fold:
        refs[1][...] = acc.astype(BF16)
    refs[0][...] = acc


def scores(ranges, hidden, blocks, bases, rows, before=(), after=(), fold=False):
    total_rows, width = hidden.shape
    rank = blocks[0].shape[1]
    flat = [held_in_vmem(b.reshape(-1, width)) for b in blocks]
    out_shape = [pltpu.VMEM((rank, total_rows), F32)]
    if fold:
        out_shape.append(pltpu.VMEM((rank, total_rows), BF16))
    return pl.pallas_call(
        functools.partial(scores_kernel, bases, rank, rows, fold, len(before), len(after)),
        out_shape=out_shape,
        in_specs=[IN_SMEM, IN_VMEM]
        + [IN_VMEM] * (len(flat) + len(before))
        + [ANYWHERE] * len(after),
        out_specs=[IN_VMEM] * len(out_shape),
        compiler_params=PARAMS,
        cost_estimate=SMALL,
        name="scores",
    )(ranges, hidden, *flat, *[held_in_vmem(b) for b in before], *after)


def base_kernel(n_after, which, hidden, weight, *refs):
    refs[n_after][...] = jnp.dot(
        hidden[...], weight[...], preferred_element_type=F32
    ).astype(BF16)


def base_product(which, hidden, weight, columns, after):
    total_rows, width = hidden.shape
    tile = min(256, columns)
    tiles = columns // tile
    return pl.pallas_call(
        functools.partial(base_kernel, len(after)),
        grid_spec=pltpu.PrefetchScalarGridSpec(
            num_scalar_prefetch=1,
            grid=(tiles,),
            in_specs=[
                IN_VMEM,
                pl.BlockSpec((width, tile), lambda j, which: (0, which[0] * tiles + j)),
            ]
            + [ANYWHERE] * len(after),
            out_specs=pl.BlockSpec((total_rows, tile), lambda j, which: (0, j)),
        ),
        out_shape=jax.ShapeDtypeStruct((total_rows, columns), BF16),
        compiler_params=PARAMS,
        cost_estimate=SMALL,
        name="base_product",
    )(which, hidden, pltpu.with_memory_space_constraint(weight, pltpu.HBM), *after)


def spread_kernel(slots, rank, rows, ranges, own, got, out):
    row = row_of_lane(rows, own.shape[1] // rows)
    proj = own[...] + got[...].astype(F32)
    for k in range(slots):
        here = (row >= ranges[2 * k]) & (row < ranges[2 * k + 1])
        out[k * rank : (k + 1) * rank, :] = jnp.where(here, proj, 0.0).astype(BF16)


def spread(slots, rank, rows, ranges, own, got):
    return pl.pallas_call(
        functools.partial(spread_kernel, slots, rank, rows),
        out_shape=pltpu.VMEM((slots * rank, own.shape[1]), BF16),
        in_specs=[IN_SMEM, IN_VMEM, IN_VMEM],
        out_specs=IN_VMEM,
        compiler_params=PARAMS,
        cost_estimate=SMALL,
        name="spread",
    )(ranges, held_in_vmem(own), held_in_vmem(got))


def final_kernel(n_added, left, *refs):
    added, blocks, (out, held, sems) = refs[:n_added], refs[n_added:-3], refs[-3:]
    tile = held.shape[2]
    copies = []
    for j in range(held.shape[0]):
        here = slice(j * tile, (j + 1) * tile)
        total = lax.dot_general(
            left[...],
            jnp.concatenate([b[:, here] for b in blocks], axis=0),
            (((0,), (0,)), ((), ())),
            preferred_element_type=F32,
        )
        for term in added:
            total = total + term[:, here].astype(F32)
        held[j] = total.astype(BF16)
        copy = pltpu.make_async_copy(held.at[j], out.at[:, pl.ds(j * tile, tile)], sems.at[j])
        copy.start()
        copies.append(copy)
    for copy in copies:
        copy.wait()


def final(left, added, blocks):
    total_rows = left.shape[1]
    columns = blocks[0].shape[2]
    flat = [held_in_vmem(b.reshape(-1, columns)) for b in blocks]
    tile = min(256, columns)
    tiles = columns // tile
    return pl.pallas_call(
        functools.partial(final_kernel, len(added)),
        out_shape=jax.ShapeDtypeStruct((total_rows, columns), BF16),
        in_specs=[IN_VMEM] * (1 + len(added) + len(flat)),
        out_specs=ANYWHERE,
        scratch_shapes=[
            pltpu.VMEM((tiles, total_rows, tile), BF16),
            pltpu.SemaphoreType.DMA((tiles,)),
        ],
        compiler_params=PARAMS,
        cost_estimate=SMALL,
        name="final",
    )(held_in_vmem(left), *[held_in_vmem(a) for a in added], *flat)


def send(value, hop, owners):
    return lax.ppermute(value, "rollout", [(i, i ^ hop) for i in range(owners)])


class Extra:

    def __init__(self, sizes, counts):
        rows, owners = sizes.rows, sizes.owners
        self.sizes = sizes
        self.me = lax.axis_index("rollout")
        order = jnp.arange(sizes.adapters, dtype=I32)
        bounds = jnp.sum(jnp.where(order[:, None] <= order[None, :], counts[:, None], 0), axis=0)

        def at_most(positions):
            return jnp.sum((bounds <= positions[:, None]).astype(I32), axis=-1)

        self.row_adapter = at_most(self.me * rows + jnp.arange(rows, dtype=I32))
        device = jnp.arange(owners, dtype=I32)
        low = at_most(device * rows)
        owner = device[:, None]
        low_pair = low[device // 2 * 2][None, :]
        self.covered = jnp.where(
            (owner % 2) == (device[None, :] % 2),
            pair_start(owner, low_pair, sizes) + sizes.kept,
            forward_start(owner, low[None, :], low_pair, sizes) + sizes.passed,
        )

    def blocks(self, stored, turn):
        sizes, me = self.sizes, self.me
        blocks, adapters = [], []
        for hop in range(sizes.owners):
            wanted = jnp.minimum(self.covered[me, me ^ hop] + turn, sizes.held - 1)
            block = lax.dynamic_slice_in_dim(stored, wanted, 1, axis=0)
            blocks.append(block if hop == 0 else send(block, hop, sizes.owners))
            source = me ^ hop
            slot = self.covered[source, me] + turn
            adapters.append(jnp.where(slot < sizes.held, source + sizes.owners * slot, -1))
        return jnp.concatenate(blocks), self.row_adapter[:, None] == jnp.stack(adapters)[None, :]

    def more_rank(self, hidden, down, turn, total):
        blocks, mask = self.blocks(down, turn)
        rank = blocks.shape[1]
        every = jnp.einsum("srd,nkd->srnk", hidden, blocks, preferred_element_type=F32)
        more = jnp.sum(every * mask[None, :, :, None].astype(F32), axis=2)
        return total + more.transpose(2, 0, 1).reshape(total.shape)

    def more_delta(self, rank_proj, up, turn, total):
        blocks, mask = self.blocks(up, turn)
        wide = rank_proj[:, :, None, :] * mask[None, :, :, None].astype(BF16)
        wide = wide.reshape(wide.shape[:2] + (-1,))
        more = jnp.einsum(
            "srw,wc->src",
            wide,
            blocks.reshape(-1, blocks.shape[2]),
            preferred_element_type=F32,
        )
        return total + more.reshape(total.shape)


def local(hidden, counts, key_value_weight, down, up):
    steps, rows, width = hidden.shape
    owners = lax.axis_size("rollout")
    sides = lax.axis_size("tensor")
    held, rank = down.shape[:2]
    sizes = Sizes(owners, counts.shape[0], held, rows)
    pairs = sizes.pairs
    side = lax.axis_index("tensor")
    flat = hidden.reshape(steps * rows, width)
    own_columns = key_value_weight.shape[1] // sides

    def swap_sides(value):
        return lax.ppermute(value, "tensor", [(0, 1), (1, 0)])

    hops = [2 * m for m in range(1, pairs)]
    late = [hops[-1]]
    kept_bases = [sizes.kept_base(m) for m in range(pairs)]
    passed_bases = [sizes.passed_base(m) for m in range(pairs)]

    *to_pairs, to_side, bounds, windows = pack(sizes, counts, down)
    near = held_in_vmem(flat)
    from_side = send(to_side, 1, owners)
    from_pairs = [send(b, hop, owners) for b, hop in zip(to_pairs, hops) if hop not in late]
    ranges, extra = ranges_of(sizes, bounds, windows)
    kept0 = cut(windows, 0, down, sizes.kept, after=[ranges])

    if sides == 2:
        side_index = jnp.reshape(side, (1,)).astype(I32)
        theirs = base_product(1 - side_index, near, key_value_weight, own_columns, [kept0])
        to_pairs[-1:] = gate(to_pairs[-1:], [theirs, from_side])
        added = [swap_sides(theirs)]
        mine = base_product(side_index, near, key_value_weight, own_columns, to_pairs[-1:])
        added.append(mine)
    else:
        partial = jnp.dot(flat, key_value_weight, preferred_element_type=F32).astype(BF16)
        added = [lax.psum_scatter(partial, "tensor", scatter_dimension=1, tiled=True)]
        mine = added[0]
    from_pairs.append(send(to_pairs[-1], hops[-1], owners))

    group_count = lax.axis_size("groups")
    rounds = extra
    for turn in range(1, group_count):
        around = [(i, (i + turn) % group_count) for i in range(group_count)]
        rounds = jnp.maximum(rounds, lax.ppermute(extra, "groups", around))
    more = rounds[0] > 0

    kept, passed = [kept0] + from_pairs, [from_side]
    before, order = (), [mine, rounds]
    for m in range(1, pairs):
        if m == pairs - 1:
            *to_pairs_up, to_side_up, kept_up = pack_again(sizes, windows, up, order)
            order = [kept_up]
        part = cut(windows, pairs + 1 + m, kept[m], sizes.passed, order)
        passed.append(send(part, 1, owners))
        if m == pairs - 1:
            to_side_up, *to_pairs_up = gate([to_side_up, *to_pairs_up], [part])
            order = [to_side_up]
        else:
            order = [part]
        blocks, bases = [kept[m], passed[m - 1]], [kept_bases[m], passed_bases[m - 1]]
        if m == 1:
            blocks, bases = [kept0] + blocks, kept_bases[:1] + bases
        before = scores(ranges, near, blocks, bases, rows, before, order)
        order = before
    own, sent = scores(ranges, near, passed[-1:], passed_bases[-1:], rows, before, fold=True)

    def over_sides(own, sent):
        if sides == 2:
            return own, swap_sides(sent)
        return jnp.zeros_like(own), lax.psum(sent, "tensor")

    from_pairs_up = [send(b, hop, owners) for hop, b in zip(hops, to_pairs_up)]
    ups = [kept_up] + from_pairs_up + [send(to_side_up, 1, owners)]
    order = [sent]
    for m in range(1, pairs):
        part = cut(windows, pairs + 1 + m, from_pairs_up[m - 1], sizes.passed, order)
        order = [part]
        ups.append(send(part, 1, owners))
    spread_out = functools.partial(spread, sizes.slots, rank, rows, ranges)

    def with_rest():
        rest = Extra(sizes, counts)
        more_rank = functools.partial(rest.more_rank, hidden, down)
        total = lax.fori_loop(0, rounds[0], more_rank, own)
        total, got = over_sides(total, total.astype(BF16))
        proj = (total + got.astype(F32)).astype(BF16)
        proj = proj.reshape(rank, steps, rows).transpose(1, 2, 0)
        more_delta = functools.partial(rest.more_delta, proj, up)
        delta = lax.fori_loop(0, rounds[0], more_delta, jnp.zeros(added[0].shape, F32))
        return final(spread_out(total, got), added + [delta], ups)

    left = spread_out(*over_sides(own, sent))
    out = lax.cond(more, with_rest, lambda: final(left, added, ups))
    return out.reshape(steps, rows, own_columns).transpose(2, 0, 1)


def solution(mesh):
    placed = (
        P(None, ("groups", "rollout"), "tensor"),
        P("groups"),
        P("tensor", None),
        P(("groups", "rollout"), None, "tensor"),
        P(("groups", "rollout"), None, "tensor"),
    )
    return jax.shard_map(
        local,
        mesh=mesh,
        in_specs=placed,
        out_specs=P("tensor", None, ("groups", "rollout")),
        check_vma=False,
    )
```

time: 197 us -> 113 us (0.57)
  waiting for transfers between devices: 61.1 us -> 22.1 us
  Pallas kernels: 98.5 us -> 62 us
  starting transfers between devices: 32.7 us -> 24.9 us
  local copies, waits for them, and re-layouts: 2.51 us -> 0.01 us
    ppermute x14, waiting for transfers between devices: 61.1 us -> 19.8 us  [send(): return lax.ppermute(value, 'rollout', [(i, i ^ hop) for i in range(owners)])]
    pallas_call x8 -> x4, Pallas kernels: 39.4 us -> 19.9 us  [scores(): pl.pallas_call(functools.partial(scores_kernel, bases, rank, rows, fold,...]
    pallas_call x12 -> x15, Pallas kernels: 54.7 us -> 37.6 us  [the longest x2 21.6 us: base_product(): pl.pallas_call(functools.partial(base_kernel, len(after)), grid_spec=pltp...]
    ppermute x14, starting transfers between devices: 31.1 us -> 23.3 us  [send(): return lax.ppermute(value, 'rollout', [(i, i ^ hop) for i in range(owners)])]
    unnamed x12 -> x6, local copies, waits for them, and re-layouts: 2.51 us -> 0.01 us
    ppermute x1, waiting for transfers between devices: 0.01 us -> 2.34 us  [local(): rounds = jnp.maximum(rounds, lax.ppermute(extra, 'groups', around))]
  transfers between devices with their start and end apart: 17 -> 17, of which waited for: 4 -> 5; matrix products, arithmetic and copies ran while one was open for 0% -> 0% of each run, Pallas kernels for 35% -> 50%
where the time goes in v3:
time: 113 us; the launch traced here: 111 us
  Pallas kernels  62 us (55%)
  starting transfers between devices  24.9 us (22%)
  waiting for transfers between devices  22.1 us (20%)
  between operations  1.62 us (1%)
    ppermute x14, starting transfers between devices, send(): return lax.ppermute(value, 'rollout', [(i, i ^ hop) for i in range(owners)])  23.3 us
    pallas_call x2, Pallas kernels, base_product(): pl.pallas_call(functools.partial(base_kernel, len(after)), grid_spec=pltp...  21.6 us
    pallas_call x4, Pallas kernels, scores(): pl.pallas_call(functools.partial(scores_kernel, bases, rank, rows, fold,...  19.9 us
    ppermute x14, waiting for transfers between devices, send(): return lax.ppermute(value, 'rollout', [(i, i ^ hop) for i in range(owners)])  19.8 us
    pallas_call x7, Pallas kernels, cut(): pl.pallas_call(functools.partial(cut_kernel, index, size, len(after)), ou...  6.56 us
    pallas_call x1, Pallas kernels, pack(): pl.pallas_call(functools.partial(pack_kernel, sizes), out_shape=[in_vmem(...  4.43 us
    pallas_call x1, Pallas kernels, ranges_of(): pl.pallas_call(functools.partial(ranges_kernel, sizes), out_shape=[jax.Sh...  4.41 us
    pallas_call x1, Pallas kernels, final(): pl.pallas_call(functools.partial(final_kernel, len(added)), out_shape=jax...  2.49 us
  transfers between devices with their start and end apart: 17, of which 5 were waited for; matrix products, arithmetic and copies ran while one was open for 0% of the time, Pallas kernels for 50%

profile of v3, /device:TPU:0, one launch (start us, length us, event | category | flops | bytes accessed | tf_op | source)
XLA Modules:
  0.0 110.9 jit_solution(91123943834735885)
XLA Ops:
  0.0 4.4 %pack.1 = (bf16[3,32,4096]{2,1,0:T(8,128)(2,1)}, bf16[3,32,4096]{2,1,0:T(8,128)(2,1)}, bf16[3,32,4096]{2,1,0:T(8,128)(2,1)S(1)}, bf16[2,32,4096]{2,1,0:T(8,128)(2,1)}, s32[65]{0:T(128)S(1)}, /*index=5*/s32[11]{0:T(128)S(1)}) custom-call(s32[64]{0:T(128)} %counts.1, bf16[8,32,4096]{2,1,0:T(8,128)(2,1)} %block.1), custom_call_target="tpu_custom_call" | custom-call | flops 1000 | bytes 1000 | tf_op jit(solution)/shard_map/pack/pallas_call | solution.py:116
  4.4 3.1 %collective-permute-start.17 = (bf16[3,32,4096]{2,1,0:T(8,128)(2,1)}, bf16[3,32,4096]{2,1,0:T(8,128)(2,1)}, u32[]{:S(2)}, u32[]{:S(2)}) collective-permute-start(bf16[3,32,4096]{2,1,0:T(8,128)(2,1)} %get-tuple-element.570), channel_id=1, source_target_pairs={{0,4},{2,6},{4,0},{6,2},{8,12},{10,14},{12,8},{14,10},{1,5},{3,7},... | collective-permute-start | bytes 2359304 | tf_op jit(solution)/shard_map/ppermute | solution.py:421
  7.5 1.5 %collective-permute-start.18 = (bf16[2,32,4096]{2,1,0:T(8,128)(2,1)}, bf16[2,32,4096]{2,1,0:T(8,128)(2,1)}, u32[]{:S(2)}, u32[]{:S(2)}) collective-permute-start(bf16[2,32,4096]{2,1,0:T(8,128)(2,1)} %get-tuple-element.572), channel_id=1, source_target_pairs={{0,2},{2,0},{4,6},{6,4},{8,10},{10,8},{12,14},{14,12},{1,3},{3,1},... | collective-permute-start | bytes 1572872 | tf_op jit(solution)/shard_map/ppermute | solution.py:421
  9.0 2.6 %collective-permute-start.16 = (bf16[3,32,4096]{2,1,0:T(8,128)(2,1)}, bf16[3,32,4096]{2,1,0:T(8,128)(2,1)}, u32[]{:S(2)}, u32[]{:S(2)}) collective-permute-start(bf16[3,32,4096]{2,1,0:T(8,128)(2,1)} %get-tuple-element.569), channel_id=1, source_target_pairs={{0,8},{2,10},{4,12},{6,14},{8,0},{10,2},{12,4},{14,6},{1,9},{3,11}... | collective-permute-start | bytes 2359304 | tf_op jit(solution)/shard_map/ppermute | solution.py:421
  11.6 4.4 %ranges.1 = (s32[40]{0:T(128)S(1)}, s32[1]{0:T(128)}) custom-call(s32[65]{0:T(128)S(1)} %get-tuple-element.565.bounds, s32[11]{0:T(128)S(1)} %get-tuple-element.566.windows), custom_call_target="tpu_custom_call" | custom-call | flops 1000 | bytes 1000 | tf_op jit(solution)/shard_map/ranges/pallas_call | solution.py:258
  16.7 10.8 %base_product.2.refs_1_ = bf16[768,1024]{1,0:T(8,128)(2,1)S(1)} custom-call(s32[1]{0:T(128)S(6)} %sub.18.which, bf16[768,4096]{1,0:T(8,128)(2,1)} %bitcast.72.hidden, bf16[4096,2048]{1,0:T(8,128)(2,1)} %weight.3, bf16[3,32,4096]{2,1,0:T(8,128)(2,1)S(1)} %cut.7.refs_0_), custom_call_target="tpu_custom_call" | custom-call | flops 1000 | bytes 1000 | tf_op jit(solution)/shard_map/base_product/pallas_call | solution.py:338
  27.9 1.5 %collective-permute-start.15 = (s32[1]{0:T(128)}, s32[1]{0:T(128)}, u32[]{:S(2)}, u32[]{:S(2)}) collective-permute-start(s32[1]{0:T(128)} %get-tuple-element.567), channel_id=1, source_target_pairs={{0,16},{16,0},{1,17},{17,1},{2,18},{18,2},{3,19},{19,3},{4,20},{20... | collective-permute-start | bytes 20 | tf_op jit(solution)/shard_map/ppermute | solution.py:522
  29.4 2.3 %collective-permute-done.15 = s32[1]{0:T(128)} collective-permute-done((s32[1]{0:T(128)}, s32[1]{0:T(128)}, u32[]{:S(2)}, u32[]{:S(2)}) %collective-permute-start.15) | collective-permute-done | bytes 36 | tf_op jit(solution)/shard_map/ppermute | solution.py:522
  32.9 10.8 %base_product.3.refs_0_ = bf16[768,1024]{1,0:T(8,128)(2,1)S(1)} custom-call(s32[1]{0:T(128)} %bitcast.74.which, bf16[768,4096]{1,0:T(8,128)(2,1)} %bitcast.72.hidden, bf16[4096,2048]{1,0:T(8,128)(2,1)} %weight.3, bf16[3,32,4096]{2,1,0:T(8,128)(2,1)S(1)} %gate.2.refs_0_), custom_call_target="tpu_custom_call" | custom-call | flops 1000 | bytes 1000 | tf_op jit(solution)/shard_map/base_product/pallas_call | solution.py:338
  43.7 1.6 %cut.8.refs_3_ = bf16[2,32,4096]{2,1,0:T(8,128)(2,1)S(1)} custom-call(s32[11]{0:T(128)S(1)} %get-tuple-element.566.windows, bf16[3,32,4096]{2,1,0:T(8,128)(2,1)} %collective-permute-done.17.block, bf16[768,1024]{1,0:T(8,128)(2,1)S(1)} %base_product.3.refs_0_, s32[1]{0:T(128)} %max.3.refs_1_), custom_call_target="tpu_custom_call" | custom-call | flops 1000 | bytes 1000 | tf_op jit(solution)/shard_map/cut/pallas_call | solution.py:175
  45.8 4.9 %scores.4.refs_0_.refs_2_ = f32[32,768]{1,0:T(8,128)S(1)} custom-call(s32[40]{0:T(128)S(1)} %get-tuple-element.568.refs_0_.ranges, bf16[768,4096]{1,0:T(8,128)(2,1)} %bitcast.72.hidden, bf16[96,4096]{1,0:T(8,128)(2,1)S(1)} %bitcast.218, bf16[96,4096]{1,0:T(8,128)(2,1)} %bitcast.77.refs_1_, bf16[64,4096]{1,0:T(8,128)(2,1)} %bitcast.78.refs_2_, ...), custom_call_target="tpu_custom_call" | custom-call | flops 1000 | bytes 1000 | tf_op jit(solution)/shard_map/scores/pallas_call | solution.py:315
  50.7 13.3 %collective-permute-done.16.block = bf16[3,32,4096]{2,1,0:T(8,128)(2,1)} collective-permute-done((bf16[3,32,4096]{2,1,0:T(8,128)(2,1)}, bf16[3,32,4096]{2,1,0:T(8,128)(2,1)}, u32[]{:S(2)}, u32[]{:S(2)}) %collective-permute-start.16) | collective-permute-done | bytes 786464 | tf_op jit(solution)/shard_map/ppermute | solution.py:421
  64.0 1.6 %cut.9.refs_3_ = bf16[2,32,4096]{2,1,0:T(8,128)(2,1)S(1)} custom-call(s32[11]{0:T(128)S(1)} %get-tuple-element.566.windows, bf16[3,32,4096]{2,1,0:T(8,128)(2,1)} %collective-permute-done.16.block, f32[32,768]{1,0:T(8,128)S(1)} %scores.4.refs_0_.refs_2_), custom_call_target="tpu_custom_call" | custom-call | flops 1000 | bytes 1000 | tf_op jit(solution)/shard_map/cut/pallas_call | solution.py:175
  65.7 5.2 %scores.5.refs_0_.refs_2_ = f32[32,768]{1,0:T(8,128)S(1)} custom-call(s32[40]{0:T(128)S(1)} %get-tuple-element.568.refs_0_.ranges, bf16[768,4096]{1,0:T(8,128)(2,1)} %bitcast.72.hidden, bf16[96,4096]{1,0:T(8,128)(2,1)} %bitcast.73.refs_0_, bf16[64,4096]{1,0:T(8,128)(2,1)S(1)} %bitcast.237, f32[32,768]{1,0:T(8,128)S(1)} %scores.4.refs_0_.refs_2_, ...), custom_call_target="tpu_custom_call" | custom-call | flops 1000 | bytes 1000 | tf_op jit(solution)/shard_map/scores/pallas_call | solution.py:315
  70.9 1.8 %pack_again.1 = (bf16[3,32,1024]{2,1,0:T(8,128)(2,1)S(1)}, bf16[3,32,1024]{2,1,0:T(8,128)(2,1)S(1)}, bf16[3,32,1024]{2,1,0:T(8,128)(2,1)S(1)}, bf16[2,32,1024]{2,1,0:T(8,128)(2,1)S(1)}, bf16[3,32,1024]{2,1,0:T(8,128)(2,1)S(1)}) custom-call(s32[11]{0:T(128)S(1)} %get-tuple-element.566.windows, bf16[8,32,1024]{2,1,0:T(8,128)(2,1)S(1)} %copy-done.21, ...), custom_call_target="tpu_custom_call" | custom-call | flops 1000 | bytes 1000 | tf_op jit(solution)/shard_map/pack_again/pallas_call | solution.py:154
  73.3 2.1 %collective-permute-start.25 = (bf16[2,32,4096]{2,1,0:T(8,128)(2,1)S(1)}, bf16[2,32,4096]{2,1,0:T(8,128)(2,1)S(1)}, u32[]{:S(2)}, u32[]{:S(2)}) collective-permute-start(bf16[2,32,4096]{2,1,0:T(8,128)(2,1)S(1)} %cut.10.refs_4_), channel_id=1, source_target_pairs={{0,2},{2,0},{4,6},{6,4},{8,10},{10,8},{12,14},{14,12},{1,3},{3,1},... | collective-permute-start | bytes 1572872 | tf_op jit(solution)/shard_map/ppermute | solution.py:421
  75.4 5.8 %collective-permute-start.21 = (bf16[3,32,1024]{2,1,0:T(8,128)(2,1)S(1)}, bf16[3,32,1024]{2,1,0:T(8,128)(2,1)S(1)}, u32[]{:S(2)}, u32[]{:S(2)}) collective-permute-start(bf16[3,32,1024]{2,1,0:T(8,128)(2,1)S(1)} %get-tuple-element.578), channel_id=1, source_target_pairs={{0,4},{2,6},{4,0},{6,2},{8,12},{10,14},{12,8},{14,10},{1,5},{3,7},... | collective-permute-start | bytes 589832 | tf_op jit(solution)/shard_map/ppermute | solution.py:421
  83.7 5.0 %scores.6.refs_1_ = f32[32,768]{1,0:T(8,128)S(1)} custom-call(s32[40]{0:T(128)S(1)} %get-tuple-element.568.refs_0_.ranges, bf16[768,4096]{1,0:T(8,128)(2,1)} %bitcast.72.hidden, bf16[96,4096]{1,0:T(8,128)(2,1)S(1)} %bitcast.219, bf16[64,4096]{1,0:T(8,128)(2,1)S(1)} %bitcast.236, f32[32,768]{1,0:T(8,128)S(1)} %scores.5.refs_0_.refs_2_, ...), custom_call_target="tpu_custom_call" | custom-call | flops 1000 | bytes 1000 | tf_op jit(solution)/shard_map/scores/pallas_call | solution.py:315
  88.7 4.8 %scores.7 = (f32[32,768]{1,0:T(8,128)S(1)}, bf16[32,768]{1,0:T(8,128)(2,1)S(1)}) custom-call(s32[40]{0:T(128)S(1)} %get-tuple-element.568.refs_0_.ranges, bf16[768,4096]{1,0:T(8,128)(2,1)} %bitcast.72.hidden, bf16[64,4096]{1,0:T(8,128)(2,1)S(1)} %bitcast.238, f32[32,768]{1,0:T(8,128)S(1)} %scores.6.refs_1_), custom_call_target="tpu_custom_call" | custom-call | flops 1000 | bytes 1000 | tf_op jit(solution)/shard_map/scores/pallas_call | solution.py:315
  93.6 1.6 %collective-permute-start.24 = (bf16[2,32,1024]{2,1,0:T(8,128)(2,1)S(1)}, bf16[2,32,1024]{2,1,0:T(8,128)(2,1)S(1)}, u32[]{:S(2)}, u32[]{:S(2)}) collective-permute-start(bf16[2,32,1024]{2,1,0:T(8,128)(2,1)S(1)} %get-tuple-element.581.refs_3_), channel_id=1, source_target_pairs={{0,2},{2,0},{4,6},{6,4},{8,10},{10,8},{12,14},{14,12},{1,3},{3,1},... | collective-permute-start | bytes 393224 | tf_op jit(solution)/shard_map/ppermute | solution.py:421
  95.9 1.7 %collective-permute-done.22.block = bf16[3,32,1024]{2,1,0:T(8,128)(2,1)S(1)} collective-permute-done((bf16[3,32,1024]{2,1,0:T(8,128)(2,1)S(1)}, bf16[3,32,1024]{2,1,0:T(8,128)(2,1)S(1)}, u32[]{:S(2)}, u32[]{:S(2)}) %collective-permute-start.22) | collective-permute-done | bytes 196640 | tf_op jit(solution)/shard_map/ppermute | solution.py:421
  103.2 3.3 %collective-permute-done.29 = bf16[2,32,1024]{2,1,0:T(8,128)(2,1)S(1)} collective-permute-done((bf16[2,32,1024]{2,1,0:T(8,128)(2,1)S(1)}, bf16[2,32,1024]{2,1,0:T(8,128)(2,1)S(1)}, u32[]{:S(2)}, u32[]{:S(2)}) %collective-permute-start.29) | collective-permute-done | bytes 131104 | tf_op jit(solution)/shard_map/ppermute | solution.py:421
  108.0 2.7 %conditional.1 = (bf16[768,1024]{1,0:T(8,128)(2,1)}) conditional(s32[]{:T(128)} %bitcast.71, (bf16[3,32,1024]{2,1,0:T(8,128)(2,1)S(1)}, bf16[3,32,1024]{2,1,0:T(8,128)(2,1)S(1)}, bf16[3,32,1024]{2,1,0:T(8,128)(2,1)S(1)}, bf16[3,32,1024]{2,1,0:T(8,128)(2,1)S(1)}, bf16[2,32,1024]{2,1,0:T(8,128)(2,1)S(1)}, ...), branch_computations={%region_0.0_spmd, %region_1.10_spmd} | conditional | flops 2014802176 | bytes 82381032 | solution.py:571
  108.0 2.5 %final.2 = bf16[768,1024]{1,0:T(8,128)(2,1)} custom-call(bf16[640,768]{1,0:T(8,128)(2,1)S(1)} %get-tuple-element.454.left, bf16[768,1024]{1,0:T(8,128)(2,1)S(1)} %get-tuple-element.455.refs_0_, bf16[768,1024]{1,0:T(8,128)(2,1)S(1)} %get-tuple-element.456.refs_1_, bf16[96,1024]{1,0:T(8,128)(2,1)S(1)} %bitcast.226, bf16[96,1024]{1,0:T(8,128)(2,1)S(1)} %bitcast.220, ...), custom_call_target="tpu_custom_call" | custom-call | flops 1000 | bytes 1000 | tf_op jit(solution)/shard_map/cond/branch_0_fun/final/pallas_call | solution.py:405
  (37 shorter events, 12.3 us)
Async XLA Ops:
  0.0 16.0 %copy-start.20 = (bf16[8,32,4096]{2,1,0:T(8,128)(2,1)S(1)}, bf16[8,32,4096]{2,1,0:T(8,128)(2,1)}, u32[]{:S(2)}) copy-start(bf16[8,32,4096]{2,1,0:T(8,128)(2,1)} %block.1) | copy-start | bytes 6291460
  4.4 39.3 %collective-permute-start.17 = (bf16[3,32,4096]{2,1,0:T(8,128)(2,1)}, bf16[3,32,4096]{2,1,0:T(8,128)(2,1)}, u32[]{:S(2)}, u32[]{:S(2)}) collective-permute-start(bf16[3,32,4096]{2,1,0:T(8,128)(2,1)} %get-tuple-element.570), channel_id=1, source_target_pairs={{0,4},{2,6},{4,0},{6,2},{8,12},{10,14},{12,8},{14,10},{1,5},{3,7},... | collective-permute-start | bytes 2359304 | tf_op jit(solution)/shard_map/ppermute | solution.py:421
  7.5 20.0 %collective-permute-start.18 = (bf16[2,32,4096]{2,1,0:T(8,128)(2,1)}, bf16[2,32,4096]{2,1,0:T(8,128)(2,1)}, u32[]{:S(2)}, u32[]{:S(2)}) collective-permute-start(bf16[2,32,4096]{2,1,0:T(8,128)(2,1)} %get-tuple-element.572), channel_id=1, source_target_pairs={{0,2},{2,0},{4,6},{6,4},{8,10},{10,8},{12,14},{14,12},{1,3},{3,1},... | collective-permute-start | bytes 1572872 | tf_op jit(solution)/shard_map/ppermute | solution.py:421
  9.0 54.9 %collective-permute-start.16 = (bf16[3,32,4096]{2,1,0:T(8,128)(2,1)}, bf16[3,32,4096]{2,1,0:T(8,128)(2,1)}, u32[]{:S(2)}, u32[]{:S(2)}) collective-permute-start(bf16[3,32,4096]{2,1,0:T(8,128)(2,1)} %get-tuple-element.569), channel_id=1, source_target_pairs={{0,8},{2,10},{4,12},{6,14},{8,0},{10,2},{12,4},{14,6},{1,9},{3,11}... | collective-permute-start | bytes 2359304 | tf_op jit(solution)/shard_map/ppermute | solution.py:421
  27.5 75.8 %collective-permute-start.31 = (bf16[768,1024]{1,0:T(8,128)(2,1)S(1)}, bf16[768,1024]{1,0:T(8,128)(2,1)S(1)}, u32[]{:S(2)}, u32[]{:S(2)}) collective-permute-start(bf16[768,1024]{1,0:T(8,128)(2,1)S(1)} %base_product.2.refs_1_), channel_id=1, source_target_pairs={{0,1},{1,0},{2,3},{3,2},{4,5},{5,4},{6,7},{7,6},{8,9},{9,8},{10,11... | collective-permute-start | bytes 4718600 | tf_op jit(solution)/shard_map/ppermute | solution.py:491
  27.6 45.1 %collective-permute-start.20 = (bf16[3,32,4096]{2,1,0:T(8,128)(2,1)S(1)}, bf16[3,32,4096]{2,1,0:T(8,128)(2,1)S(1)}, u32[]{:S(2)}, u32[]{:S(2)}) collective-permute-start(bf16[3,32,4096]{2,1,0:T(8,128)(2,1)S(1)} %gate.2.refs_0_), channel_id=1, source_target_pairs={{0,12},{2,14},{4,8},{6,10},{8,4},{10,6},{12,0},{14,2},{1,13},{3,15... | collective-permute-start | bytes 2359304 | tf_op jit(solution)/shard_map/ppermute | solution.py:421
  27.9 3.9 %collective-permute-start.15 = (s32[1]{0:T(128)}, s32[1]{0:T(128)}, u32[]{:S(2)}, u32[]{:S(2)}) collective-permute-start(s32[1]{0:T(128)} %get-tuple-element.567), channel_id=1, source_target_pairs={{0,16},{16,0},{1,17},{17,1},{2,18},{18,2},{3,19},{19,3},{4,20},{20... | collective-permute-start | bytes 20 | tf_op jit(solution)/shard_map/ppermute | solution.py:522
  45.3 20.3 %collective-permute-start.19 = (bf16[2,32,4096]{2,1,0:T(8,128)(2,1)S(1)}, bf16[2,32,4096]{2,1,0:T(8,128)(2,1)S(1)}, u32[]{:S(2)}, u32[]{:S(2)}) collective-permute-start(bf16[2,32,4096]{2,1,0:T(8,128)(2,1)S(1)} %cut.8.refs_3_), channel_id=1, source_target_pairs={{0,2},{2,0},{4,6},{6,4},{8,10},{10,8},{12,14},{14,12},{1,3},{3,1},... | collective-permute-start | bytes 1572872 | tf_op jit(solution)/shard_map/ppermute | solution.py:421
  65.6 16.7 %collective-permute-start.26 = (bf16[2,32,4096]{2,1,0:T(8,128)(2,1)S(1)}, bf16[2,32,4096]{2,1,0:T(8,128)(2,1)S(1)}, u32[]{:S(2)}, u32[]{:S(2)}) collective-permute-start(bf16[2,32,4096]{2,1,0:T(8,128)(2,1)S(1)} %cut.9.refs_3_), channel_id=1, source_target_pairs={{0,2},{2,0},{4,6},{6,4},{8,10},{10,8},{12,14},{14,12},{1,3},{3,1},... | collective-permute-start | bytes 1572872 | tf_op jit(solution)/shard_map/ppermute | solution.py:421
  65.7 5.2 %copy-start.21 = (bf16[8,32,1024]{2,1,0:T(8,128)(2,1)S(1)}, bf16[8,32,1024]{2,1,0:T(8,128)(2,1)}, u32[]{:S(2)}) copy-start(bf16[8,32,1024]{2,1,0:T(8,128)(2,1)} %stored.3) | copy-start | bytes 1572868
  73.3 15.4 %collective-permute-start.25 = (bf16[2,32,4096]{2,1,0:T(8,128)(2,1)S(1)}, bf16[2,32,4096]{2,1,0:T(8,128)(2,1)S(1)}, u32[]{:S(2)}, u32[]{:S(2)}) collective-permute-start(bf16[2,32,4096]{2,1,0:T(8,128)(2,1)S(1)} %cut.10.refs_4_), channel_id=1, source_target_pairs={{0,2},{2,0},{4,6},{6,4},{8,10},{10,8},{12,14},{14,12},{1,3},{3,1},... | collective-permute-start | bytes 1572872 | tf_op jit(solution)/shard_map/ppermute | solution.py:421
  75.4 18.3 %collective-permute-start.21 = (bf16[3,32,1024]{2,1,0:T(8,128)(2,1)S(1)}, bf16[3,32,1024]{2,1,0:T(8,128)(2,1)S(1)}, u32[]{:S(2)}, u32[]{:S(2)}) collective-permute-start(bf16[3,32,1024]{2,1,0:T(8,128)(2,1)S(1)} %get-tuple-element.578), channel_id=1, source_target_pairs={{0,4},{2,6},{4,0},{6,2},{8,12},{10,14},{12,8},{14,10},{1,5},{3,7},... | collective-permute-start | bytes 589832 | tf_op jit(solution)/shard_map/ppermute | solution.py:421
  81.2 16.4 %collective-permute-start.22 = (bf16[3,32,1024]{2,1,0:T(8,128)(2,1)S(1)}, bf16[3,32,1024]{2,1,0:T(8,128)(2,1)S(1)}, u32[]{:S(2)}, u32[]{:S(2)}) collective-permute-start(bf16[3,32,1024]{2,1,0:T(8,128)(2,1)S(1)} %get-tuple-element.579), channel_id=1, source_target_pairs={{0,8},{2,10},{4,12},{6,14},{8,0},{10,2},{12,4},{14,6},{1,9},{3,11}... | collective-permute-start | bytes 589832 | tf_op jit(solution)/shard_map/ppermute | solution.py:421
  82.2 17.4 %collective-permute-start.23 = (bf16[3,32,1024]{2,1,0:T(8,128)(2,1)S(1)}, bf16[3,32,1024]{2,1,0:T(8,128)(2,1)S(1)}, u32[]{:S(2)}, u32[]{:S(2)}) collective-permute-start(bf16[3,32,1024]{2,1,0:T(8,128)(2,1)S(1)} %get-tuple-element.580), channel_id=1, source_target_pairs={{0,12},{2,14},{4,8},{6,10},{8,4},{10,6},{12,0},{14,2},{1,13},{3,15... | collective-permute-start | bytes 589832 | tf_op jit(solution)/shard_map/ppermute | solution.py:421
  93.5 14.4 %copy-start.22 = (s32[64]{0:T(128)S(1)}, s32[64]{0:T(128)}, u32[]{:S(2)}) copy-start(s32[64]{0:T(128)} %counts.1) | copy-start | bytes 772
  93.5 7.7 %collective-permute-start.30 = (bf16[32,768]{1,0:T(8,128)(2,1)S(1)}, bf16[32,768]{1,0:T(8,128)(2,1)S(1)}, u32[]{:S(2)}, u32[]{:S(2)}) collective-permute-start(bf16[32,768]{1,0:T(8,128)(2,1)S(1)} %get-tuple-element.582.refs_0_), channel_id=1, source_target_pairs={{0,1},{1,0},{2,3},{3,2},{4,5},{5,4},{6,7},{7,6},{8,9},{9,8},{10,11... | collective-permute-start | bytes 147464 | tf_op jit(solution)/shard_map/ppermute | solution.py:491
  93.6 9.6 %collective-permute-start.24 = (bf16[2,32,1024]{2,1,0:T(8,128)(2,1)S(1)}, bf16[2,32,1024]{2,1,0:T(8,128)(2,1)S(1)}, u32[]{:S(2)}, u32[]{:S(2)}) collective-permute-start(bf16[2,32,1024]{2,1,0:T(8,128)(2,1)S(1)} %get-tuple-element.581.refs_3_), channel_id=1, source_target_pairs={{0,2},{2,0},{4,6},{6,4},{8,10},{10,8},{12,14},{14,12},{1,3},{3,1},... | collective-permute-start | bytes 393224 | tf_op jit(solution)/shard_map/ppermute | solution.py:421
  98.4 8.2 %collective-permute-start.28 = (bf16[2,32,1024]{2,1,0:T(8,128)(2,1)S(1)}, bf16[2,32,1024]{2,1,0:T(8,128)(2,1)S(1)}, u32[]{:S(2)}, u32[]{:S(2)}) collective-permute-start(bf16[2,32,1024]{2,1,0:T(8,128)(2,1)S(1)} %cut.12.refs_0_), channel_id=1, source_target_pairs={{0,2},{2,0},{4,6},{6,4},{8,10},{10,8},{12,14},{14,12},{1,3},{3,1},... | collective-permute-start | bytes 393224 | tf_op jit(solution)/shard_map/ppermute | solution.py:421
  100.4 6.2 %collective-permute-start.29 = (bf16[2,32,1024]{2,1,0:T(8,128)(2,1)S(1)}, bf16[2,32,1024]{2,1,0:T(8,128)(2,1)S(1)}, u32[]{:S(2)}, u32[]{:S(2)}) collective-permute-start(bf16[2,32,1024]{2,1,0:T(8,128)(2,1)S(1)} %cut.13), channel_id=1, source_target_pairs={{0,2},{2,0},{4,6},{6,4},{8,10},{10,8},{12,14},{14,12},{1,3},{3,1},... | collective-permute-start | bytes 393224 | tf_op jit(solution)/shard_map/ppermute | solution.py:421
  101.3 6.7 %collective-permute-start.27 = (bf16[2,32,1024]{2,1,0:T(8,128)(2,1)S(1)}, bf16[2,32,1024]{2,1,0:T(8,128)(2,1)S(1)}, u32[]{:S(2)}, u32[]{:S(2)}) collective-permute-start(bf16[2,32,1024]{2,1,0:T(8,128)(2,1)S(1)} %cut.11.refs_0_), channel_id=1, source_target_pairs={{0,2},{2,0},{4,6},{6,4},{8,10},{10,8},{12,14},{14,12},{1,3},{3,1},... | collective-permute-start | bytes 393224 | tf_op jit(solution)/shard_map/ppermute | solution.py:421

commit v4 on v3

v4 whole, which is shorter than its diff:
```python
import functools

import jax
import jax.numpy as jnp
from jax import lax
from jax.experimental import pallas as pl
from jax.experimental.pallas import tpu as pltpu
from jax.sharding import PartitionSpec as P

PAIR_SLOTS = 3
FORWARD_SLOTS = 2
BF16 = jnp.bfloat16
F32 = jnp.float32
I32 = jnp.int32
SMALL = pl.CostEstimate(flops=1000, bytes_accessed=1000, transcendentals=0)
MIB = 1024 * 1024
PARAMS = pltpu.CompilerParams(vmem_limit_bytes=8 * MIB)
WIDE_PARAMS = pltpu.CompilerParams(vmem_limit_bytes=22 * MIB)
IN_SMEM = pl.BlockSpec(memory_space=pltpu.SMEM)
IN_VMEM = pl.BlockSpec(memory_space=pltpu.VMEM)
ANYWHERE = pl.BlockSpec(memory_space=pl.ANY)


def first_slot(owner, adapter, owners):
    return lax.div(adapter - owner + (owners - 1), jnp.int32(owners))


def end_slot(owner, adapter, owners):
    return lax.div(adapter - owner + owners, jnp.int32(owners))


def pair_start(owner, pair, lows, sizes):
    own = jnp.minimum(first_slot(owner, lows(pair), sizes.owners), sizes.held - sizes.kept)
    base = jnp.minimum(first_slot(owner, lows(pair & -2), sizes.owners), sizes.held - sizes.kept)
    apart = (owner >> 2) != (pair >> 1)
    second = (pair & 1) == 1
    return jnp.where(apart & second, jnp.minimum(own, base + (sizes.kept - 1)), own)


def own_start(owner, low, size, sizes):
    return jnp.minimum(first_slot(owner, low, sizes.owners), sizes.held - size)


def forward_start(owner, low, start, sizes):
    return jnp.minimum(
        first_slot(owner, low, sizes.owners), start + (sizes.kept - sizes.passed)
    )


class Sizes:
    def __init__(self, owners, counts, down, up, rows):
        self.owners, self.adapters, self.rows = owners, counts.shape[0], rows
        self.held, self.rank, self.columns = up.shape
        self.parts = down.shape[2] // self.columns
        self.kept, self.passed = PAIR_SLOTS, FORWARD_SLOTS
        self.direct = self.kept - 1
        self.pairs = owners // 2
        self.slots = self.pairs * (self.kept + self.passed)
        self.split = [m for m in range(2, self.pairs) if m % 2 == 0]
        self.whole = [m for m in range(self.pairs - 1, 0, -1) if m not in self.split]
        self.forward_at = self.pairs + 1
        self.third_at = 2 * self.pairs + 1
        self.scalars = 3 * self.pairs + 2

    def kept_base(self, m):
        return m * self.kept

    def passed_base(self, m):
        return self.pairs * self.kept + m * self.passed

    def is_split(self, m):
        return m in self.split


def bring(sizes, down, up, start, target, sems, copies):
    size, parts = target.shape[:2]
    for c in range(parts):
        if c < sizes.parts:
            piece = down.at[pl.ds(start, size), :, pl.ds(c * sizes.columns, sizes.columns)]
        else:
            piece = up.at[pl.ds(start, size)]
        copies.append(pltpu.make_async_copy(piece, target.at[:, c], sems.at[len(copies)]))
        copies[-1].start()


def pack_kernel(sizes, counts, down, up, *refs):
    pairs = sizes.pairs
    sent = dict(zip(sizes.whole, refs))
    passed0, bounds, windows, low_pair, sems = refs[len(sent) :]
    me = lax.axis_index("rollout")
    mine = me >> 1
    odd_row = (2 * mine + 1) * sizes.rows
    bounds[0] = jnp.int32(0)

    def add(a, carry):
        end = carry[0] + counts[a]
        bounds[a + 1] = end
        lows = [
            low + (end <= 2 * p * sizes.rows).astype(I32) for p, low in enumerate(carry[1 : pairs + 1])
        ]
        return (end, *lows, carry[pairs + 1] + (end <= odd_row).astype(I32))

    found = lax.fori_loop(0, sizes.adapters, add, (jnp.int32(0),) * (pairs + 2), unroll=8)
    for p in range(pairs):
        low_pair[p] = found[1 + p]
    odd = found[pairs + 1]

    def lows(p):
        return low_pair[p]

    copies = []
    is_even = (me & 1) == 0
    low_other = jnp.where(is_even, odd, low_pair[mine])
    low_me = jnp.where(is_even, low_pair[mine], odd)
    for m in sizes.whole + sizes.split:
        start = pair_start(me, mine ^ m, lows, sizes)
        windows[m] = start
        if m in sent:
            bring(sizes, down, up, start, sent[m], sems, copies)
    start = own_start(me, low_other, sizes.passed, sizes)
    windows[pairs] = start
    bring(sizes, down, up, start, passed0, sems, copies)
    windows[0] = own_start(me, low_me, sizes.kept, sizes)
    windows[sizes.forward_at] = jnp.int32(0)
    windows[sizes.third_at] = jnp.int32(0)
    for m in range(1, pairs):
        source = me ^ (2 * m)
        start = pair_start(source, mine, lows, sizes)
        windows[sizes.forward_at + m] = forward_start(source, low_other, start, sizes) - start
        beside = mine ^ 1
        third = pair_start(source, beside, lows, sizes) + jnp.where(
            (beside & 1) == 0, sizes.direct, 0
        )
        windows[sizes.third_at + m] = jnp.clip(third - start, 0, sizes.kept - 1)
    windows[sizes.scalars - 1] = mine & 1
    for copy in copies:
        copy.wait()


def held_in_vmem(value):
    return pltpu.with_memory_space_constraint(value, pltpu.VMEM)


def slots_in_vmem(sizes, slots, parts):
    return pltpu.VMEM((slots, parts, sizes.rank, sizes.columns), BF16)


def pack(sizes, counts, down, up):
    pairs, parts = sizes.pairs, sizes.parts
    return pl.pallas_call(
        functools.partial(pack_kernel, sizes),
        out_shape=[slots_in_vmem(sizes, sizes.kept, parts + 1)] * len(sizes.whole)
        + [
            slots_in_vmem(sizes, sizes.passed, parts + 1),
            jax.ShapeDtypeStruct((sizes.adapters + 1,), I32),
            jax.ShapeDtypeStruct((sizes.scalars,), I32),
        ],
        in_specs=[IN_SMEM, ANYWHERE, ANYWHERE],
        out_specs=[IN_VMEM] * (len(sizes.whole) + 1) + [IN_SMEM, IN_SMEM],
        scratch_shapes=[
            pltpu.SMEM((pairs,), I32),
            pltpu.SemaphoreType.DMA(((pairs + 1) * (parts + 1),)),
        ],
        compiler_params=PARAMS,
        cost_estimate=SMALL,
        name="pack",
    )(counts, down, up)


def pack_more_kernel(sizes, m, n_after, windows, down, up, *refs):
    target, sems = refs[n_after:]
    start = windows[m]
    if sizes.is_split(m):
        start = start + windows[sizes.scalars - 1]
    copies = []
    bring(sizes, down, up, start, target, sems, copies)
    for copy in copies:
        copy.wait()


def pack_more(sizes, m, windows, down, up, after):
    parts = sizes.parts
    shape = (sizes.direct, parts) if sizes.is_split(m) else (sizes.kept, parts + 1)
    return pl.pallas_call(
        functools.partial(pack_more_kernel, sizes, m, len(after)),
        out_shape=slots_in_vmem(sizes, *shape),
        in_specs=[IN_SMEM, ANYWHERE, ANYWHERE] + [ANYWHERE] * len(after),
        out_specs=IN_VMEM,
        scratch_shapes=[pltpu.SemaphoreType.DMA((parts + 1,))],
        compiler_params=PARAMS,
        cost_estimate=SMALL,
        name="pack_more",
    )(windows, down, up, *after)


def collect_kernel(places, n_after, *refs):
    blocks, (out, sems) = refs[: len(places)], refs[len(places) + n_after :]
    copies, at = [], 0
    for block, c in zip(blocks, places):
        size = block.shape[0]
        copies.append(
            pltpu.make_async_copy(
                block.at[:, c], out.at[pl.ds(at, size), 0], sems.at[len(copies)]
            )
        )
        copies[-1].start()
        at += size
    for copy in copies:
        copy.wait()


def collect(sizes, blocks, after):
    places = [sizes.parts] * len(blocks)
    return pl.pallas_call(
        functools.partial(collect_kernel, places, len(after)),
        out_shape=slots_in_vmem(sizes, sum(b.shape[0] for b in blocks), 1),
        in_specs=[ANYWHERE] * (len(blocks) + len(after)),
        out_specs=IN_VMEM,
        scratch_shapes=[pltpu.SemaphoreType.DMA((len(blocks),))],
        compiler_params=PARAMS,
        cost_estimate=SMALL,
        name="collect",
    )(*blocks, *after)


def pack_up_kernel(sizes, m, n_after, windows, up, *refs):
    target, sems = refs[n_after:]
    second = windows[sizes.scalars - 1]
    third = windows[m] + sizes.direct * (1 - second)
    copies = [
        pltpu.make_async_copy(
            up.at[pl.ds(windows[m] + second, sizes.direct)],
            target.at[pl.ds(0, sizes.direct), 0],
            sems.at[0],
        ),
        pltpu.make_async_copy(
            up.at[pl.ds(third, 1)], target.at[pl.ds(sizes.direct, 1), 0], sems.at[1]
        ),
    ]
    for copy in copies:
        copy.start()
    for copy in copies:
        copy.wait()


def pack_up(sizes, m, windows, up, after):
    return pl.pallas_call(
        functools.partial(pack_up_kernel, sizes, m, len(after)),
        out_shape=slots_in_vmem(sizes, sizes.kept, 1),
        in_specs=[IN_SMEM, ANYWHERE] + [ANYWHERE] * len(after),
        out_specs=IN_VMEM,
        scratch_shapes=[pltpu.SemaphoreType.DMA((2,))],
        compiler_params=PARAMS,
        cost_estimate=SMALL,
        name="pack_up",
    )(windows, up, *after)


def cut_kernel(index, n_after, windows, block, *refs):
    out, sem = refs[n_after:]
    size, parts = out.shape[:2]
    piece = block.at[pl.ds(windows[index], size), pl.ds(0, parts)]
    copy = pltpu.make_async_copy(piece, out, sem)
    copy.start()
    copy.wait()


def cut(sizes, windows, index, block, size, parts, after=()):
    return pl.pallas_call(
        functools.partial(cut_kernel, index, len(after)),
        out_shape=slots_in_vmem(sizes, size, parts),
        in_specs=[IN_SMEM, ANYWHERE] + [ANYWHERE] * len(after),
        out_specs=IN_VMEM,
        scratch_shapes=[pltpu.SemaphoreType.DMA],
        compiler_params=PARAMS,
        cost_estimate=SMALL,
        name="cut",
    )(windows, block, *after)


def join_kernel(forward_at, second_at, third_at, n_after, windows, direct, third, *refs):
    out, sem = refs[n_after:]
    later = windows[forward_at] == 1
    second = windows[second_at] == 1
    third = third.at[pl.ds(third_at, 1)]

    def take(first, last):
        one = pltpu.make_async_copy(first, out.at[pl.ds(0, 1)], sem.at[0])
        two = pltpu.make_async_copy(last, out.at[pl.ds(1, 1)], sem.at[1])
        one.start()
        two.start()
        one.wait()
        two.wait()

    end = jnp.logical_and(later, jnp.logical_not(second))
    front = jnp.logical_and(jnp.logical_not(later), second)
    first, last = direct.at[pl.ds(0, 1)], direct.at[pl.ds(1, 1)]

    @pl.when(end)
    def _():
        take(last, third)

    @pl.when(front)
    def _():
        take(third, first)

    @pl.when(jnp.logical_not(jnp.logical_or(end, front)))
    def _():
        take(first, last)


def join(sizes, windows, m, direct, third, third_at, after=()):
    return pl.pallas_call(
        functools.partial(
            join_kernel, sizes.forward_at + m, sizes.scalars - 1, third_at, len(after)
        ),
        out_shape=slots_in_vmem(sizes, sizes.passed, direct.shape[1]),
        in_specs=[IN_SMEM, ANYWHERE, ANYWHERE] + [ANYWHERE] * len(after),
        out_specs=IN_VMEM,
        scratch_shapes=[pltpu.SemaphoreType.DMA((2,))],
        compiler_params=PARAMS,
        cost_estimate=SMALL,
        name="join",
    )(windows, direct, third, *after)


def gate_kernel(*refs):
    pass


def gate(values, after):
    n = len(values)
    return pl.pallas_call(
        gate_kernel,
        out_shape=[pltpu.VMEM(v.shape, v.dtype) for v in values],
        in_specs=[IN_VMEM] * n + [ANYWHERE] * len(after),
        out_specs=[IN_VMEM] * n,
        input_output_aliases={i: i for i in range(n)},
        compiler_params=PARAMS,
        cost_estimate=SMALL,
        name="gate",
    )(*[held_in_vmem(v) for v in values], *after)


def ranges_kernel(sizes, bounds, windows, ranges, needs, lows, highs):
    me = lax.axis_index("rollout")
    mine = me >> 1
    first_row = me * sizes.rows

    places = [(d, last) for last in (0, sizes.rows - 1) for d in range(sizes.owners)]

    def count(a, carry):
        end = bounds[a + 1]
        return tuple(
            c + (end <= d * sizes.rows + last).astype(I32)
            for (d, last), c in zip(places, carry)
        )

    found = lax.fori_loop(0, sizes.adapters, count, (jnp.int32(0),) * len(places))
    for d in range(sizes.owners):
        lows[d] = found[d]
        highs[d] = found[sizes.owners + d]

    def low_pair(p):
        return lows[2 * p]

    def fill(index, source, slot):
        adapter = source + sizes.owners * slot
        ranges[2 * index] = bounds[adapter] - first_row
        ranges[2 * index + 1] = bounds[adapter + 1] - first_row

    for m in range(sizes.pairs):
        source = me ^ (2 * m)
        start = windows[0] if m == 0 else pair_start(source, mine, low_pair, sizes)
        second = mine & 1 if sizes.is_split(m) else 0
        for k in range(sizes.kept):
            slot = start + k
            if sizes.is_split(m):
                slot = start + (k + second if k < sizes.direct else sizes.direct * (1 - second))
            fill(sizes.kept_base(m) + k, source, slot)
        source = me ^ 1 ^ (2 * m)
        if m == 0:
            start = own_start(source, lows[me], sizes.passed, sizes)
        else:
            start = pair_start(source, mine, low_pair, sizes)
            start = forward_start(source, lows[me], start, sizes)
        for k in range(sizes.passed):
            fill(sizes.passed_base(m) + k, source, start + k)

    for hop in range(sizes.owners):

        def most(d, so_far, hop=hop):
            owner = d ^ hop
            past = covered(owner, d, hop, lows[d], low_pair, sizes)
            return jnp.maximum(so_far, end_slot(owner, highs[d], sizes.owners) - past)

        needs[hop] = lax.fori_loop(0, sizes.owners, most, jnp.int32(0))


def covered(owner, device, hop, low, low_pair, sizes):
    if hop == 0:
        return own_start(owner, low, sizes.kept, sizes) + sizes.kept
    if hop == 1:
        return own_start(owner, low, sizes.passed, sizes) + sizes.passed
    start = pair_start(owner, device >> 1, low_pair, sizes)
    if hop % 2 == 0:
        return start + sizes.kept
    return forward_start(owner, low, start, sizes) + sizes.passed


def ranges_of(sizes, bounds, windows):
    return pl.pallas_call(
        functools.partial(ranges_kernel, sizes),
        out_shape=[
            jax.ShapeDtypeStruct((2 * sizes.slots,), I32),
            jax.ShapeDtypeStruct((sizes.owners,), I32),
        ],
        in_specs=[IN_SMEM, IN_SMEM],
        out_specs=[IN_SMEM, IN_SMEM],
        scratch_shapes=[pltpu.SMEM((sizes.owners,), I32), pltpu.SMEM((sizes.owners,), I32)],
        compiler_params=PARAMS,
        cost_estimate=SMALL,
        name="ranges",
    )(bounds, windows)


def row_of_lane(rows, steps):
    lane = lax.broadcasted_iota(I32, (1, steps * rows), 1)
    row = lane
    for s in range(1, steps):
        row = jnp.where(lane >= s * rows, lane - s * rows, row)
    return row


def scores_kernel(bases, rank, rows, fold, n_before, n_after, ranges, hidden, *refs):
    blocks, refs = refs[: len(bases)], refs[len(bases) :]
    before, refs = refs[:n_before], refs[n_before + n_after :]
    out, total = refs[0], refs[-1]
    k = pl.program_id(0)
    part = lax.dot_general(
        jnp.concatenate([b[n, k] for b in blocks for n in range(b.shape[0])], axis=0),
        hidden[...],
        (((1,), (1,)), ((), ())),
        preferred_element_type=F32,
    )

    @pl.when(k == 0)
    def _():
        total[...] = part

    @pl.when(k > 0)
    def _():
        total[...] += part

    @pl.when(k == pl.num_programs(0) - 1)
    def _():
        row = row_of_lane(rows, hidden.shape[0] // rows)
        acc = before[0][...] if n_before else jnp.zeros((rank, hidden.shape[0]), F32)
        place = 0
        for base, block in zip(bases, blocks):
            for n in range(block.shape[0]):
                mask = (row >= ranges[2 * (base + n)]) & (row < ranges[2 * (base + n) + 1])
                acc = acc + jnp.where(mask, total[place : place + rank, :], 0.0)
                place += rank
        out[...] = acc
        if fold:
            refs[1][...] = acc.astype(BF16)


def scores(sizes, ranges, hidden, blocks, bases, before=(), after=(), fold=False):
    total_rows = hidden.shape[0]
    rank, rows = sizes.rank, sizes.rows
    deep = sum(b.shape[0] for b in blocks) * rank
    out_shape = [pltpu.VMEM((rank, total_rows), F32)]
    if fold:
        out_shape.append(pltpu.VMEM((rank, total_rows), BF16))
    return pl.pallas_call(
        functools.partial(scores_kernel, bases, rank, rows, fold, len(before), len(after)),
        grid=(sizes.parts,),
        out_shape=out_shape,
        in_specs=[IN_SMEM, pl.BlockSpec((total_rows, sizes.columns), lambda k: (0, k))]
        + [IN_VMEM] * (len(blocks) + len(before))
        + [ANYWHERE] * len(after),
        out_specs=[IN_VMEM] * len(out_shape),
        scratch_shapes=[pltpu.VMEM((deep, total_rows), F32)],
        compiler_params=WIDE_PARAMS,
        cost_estimate=SMALL,
        name="scores",
    )(ranges, hidden, *map(held_in_vmem, blocks), *map(held_in_vmem, before), *after)


def base_kernel(n_after, which, hidden, weight, *refs):
    refs[n_after][...] = jnp.dot(
        hidden[...], weight[...], preferred_element_type=F32
    ).astype(BF16)


def base_product(which, hidden, weight, columns, after):
    total_rows, width = hidden.shape
    tile = min(256, columns)
    tiles = columns // tile
    return pl.pallas_call(
        functools.partial(base_kernel, len(after)),
        grid_spec=pltpu.PrefetchScalarGridSpec(
            num_scalar_prefetch=1,
            grid=(tiles,),
            in_specs=[
                IN_VMEM,
                pl.BlockSpec((width, tile), lambda j, which: (0, which[0] * tiles + j)),
            ]
            + [ANYWHERE] * len(after),
            out_specs=pl.BlockSpec((total_rows, tile), lambda j, which: (0, j)),
        ),
        out_shape=jax.ShapeDtypeStruct((total_rows, columns), BF16),
        compiler_params=WIDE_PARAMS,
        cost_estimate=SMALL,
        name="base_product",
    )(which, hidden, pltpu.with_memory_space_constraint(weight, pltpu.HBM), *after)


def spread_kernel(slots, rank, rows, ranges, own, got, out):
    row = row_of_lane(rows, own.shape[1] // rows)
    proj = own[...] + got[...].astype(F32)
    for k, slot in enumerate(slots):
        here = (row >= ranges[2 * slot]) & (row < ranges[2 * slot + 1])
        out[k * rank : (k + 1) * rank, :] = jnp.where(here, proj, 0.0).astype(BF16)


def spread(slots, rank, rows, ranges, own, got):
    return pl.pallas_call(
        functools.partial(spread_kernel, slots, rank, rows),
        out_shape=pltpu.VMEM((len(slots) * rank, own.shape[1]), BF16),
        in_specs=[IN_SMEM, IN_VMEM, IN_VMEM],
        out_specs=IN_VMEM,
        compiler_params=PARAMS,
        cost_estimate=SMALL,
        name="spread",
    )(ranges, held_in_vmem(own), held_in_vmem(got))


def final_kernel(n_added, left, *refs):
    added, blocks = refs[:n_added], refs[n_added : -3 - n_added]
    out, held, sems = refs[-3 - n_added], refs[-2 - n_added], refs[-1]
    terms = refs[-1 - n_added : -1]
    tiles, tile, _ = held.shape
    brought = [
        [
            pltpu.make_async_copy(source.at[pl.ds(j * tile, tile)], term.at[j], sems.at[n + 1, j])
            for n, (source, term) in enumerate(zip(added, terms))
        ]
        for j in range(tiles)
    ]
    for copies in brought:
        for copy in copies:
            copy.start()
    right = jnp.concatenate([b[n, 0] for b in blocks for n in range(b.shape[0])], axis=0)
    taken = []
    for j in range(tiles):
        total = lax.dot_general(
            left[:, j * tile : (j + 1) * tile],
            right,
            (((0,), (0,)), ((), ())),
            preferred_element_type=F32,
        )
        for copy, term in zip(brought[j], terms):
            copy.wait()
            total = total + term[j].astype(F32)
        held[j] = total.astype(BF16)
        taken.append(
            pltpu.make_async_copy(held.at[j], out.at[pl.ds(j * tile, tile)], sems.at[0, j])
        )
        taken[-1].start()
    for copy in taken:
        copy.wait()


def final(left, added, blocks):
    total_rows = left.shape[1]
    columns = blocks[0].shape[3]
    tile = 256 if total_rows % 256 == 0 else total_rows
    tiles = total_rows // tile
    return pl.pallas_call(
        functools.partial(final_kernel, len(added)),
        out_shape=jax.ShapeDtypeStruct((total_rows, columns), BF16),
        in_specs=[IN_VMEM] + [ANYWHERE] * len(added) + [IN_VMEM] * len(blocks),
        out_specs=ANYWHERE,
        scratch_shapes=[pltpu.VMEM((tiles, tile, columns), BF16)]
        + [pltpu.VMEM((tiles, tile, columns), a.dtype) for a in added]
        + [pltpu.SemaphoreType.DMA((1 + len(added), tiles))],
        compiler_params=WIDE_PARAMS,
        cost_estimate=SMALL,
        name="final",
    )(held_in_vmem(left), *added, *map(held_in_vmem, blocks))


def send(value, hop, owners):
    return lax.ppermute(value, "rollout", [(i, i ^ hop) for i in range(owners)])


class Extra:

    def __init__(self, sizes, counts):
        rows, owners = sizes.rows, sizes.owners
        self.sizes = sizes
        self.me = lax.axis_index("rollout")
        order = jnp.arange(sizes.adapters, dtype=I32)
        bounds = jnp.sum(jnp.where(order[:, None] <= order[None, :], counts[:, None], 0), axis=0)

        def at_most(positions):
            return jnp.sum((bounds <= positions[:, None]).astype(I32), axis=-1)

        self.row_adapter = at_most(self.me * rows + jnp.arange(rows, dtype=I32))
        self.low = at_most(jnp.arange(owners, dtype=I32) * rows)

    def past(self, owner, device, hop):
        return covered(
            owner, device, hop, self.low[device], lambda p: self.low[2 * p], self.sizes
        )

    def add(self, hop, hidden, down, up, turn, delta):
        sizes, me, source = self.sizes, self.me, self.me ^ hop
        wanted = jnp.minimum(self.past(me, source, hop) + turn, sizes.held - 1)
        slot = self.past(source, me, hop) + turn
        adapter = jnp.where(slot < sizes.held, source + sizes.owners * slot, -1)
        down_block = lax.dynamic_slice_in_dim(down, wanted, 1, axis=0)
        up_block = lax.dynamic_slice_in_dim(up, wanted, 1, axis=0)
        if hop:
            down_block = send(down_block, hop, sizes.owners)
            up_block = send(up_block, hop, sizes.owners)
        part = jnp.einsum("srd,kd->srk", hidden, down_block[0], preferred_element_type=F32)
        here = (self.row_adapter == adapter)[None, :, None]
        part = jnp.where(here, part, 0.0)
        own, got = over_sides(part, part.astype(BF16))
        proj = (own + got.astype(F32)).astype(BF16)
        more = jnp.einsum("srk,kc->src", proj, up_block[0], preferred_element_type=F32)
        return delta + more.reshape(delta.shape)


def swap_sides(value):
    return lax.ppermute(value, "tensor", [(0, 1), (1, 0)])


def over_sides(own, sent):
    if lax.axis_size("tensor") == 2:
        return own, swap_sides(sent)
    return jnp.zeros_like(own), lax.psum(sent, "tensor")


def local(hidden, counts, key_value_weight, down, up):
    steps, rows, width = hidden.shape
    owners = lax.axis_size("rollout")
    sides = lax.axis_size("tensor")
    sizes = Sizes(owners, counts, down, up, rows)
    pairs, rank, parts = sizes.pairs, sizes.rank, sizes.parts
    side = lax.axis_index("tensor")
    flat = hidden.reshape(steps * rows, width)
    own_columns = key_value_weight.shape[1] // sides
    kept_bases = [sizes.kept_base(m) for m in range(pairs)]
    passed_bases = [sizes.passed_base(m) for m in range(pairs)]
    split, far = sizes.split, sizes.whole[:-1]

    *to_pairs, to_side, bounds, windows = pack(sizes, counts, down, up)
    from_pair = {m: send(b, 2 * m, owners) for m, b in zip(sizes.whole, to_pairs)}
    passed, third = {0: send(to_side, 1, owners)}, {}
    ranges, needs = ranges_of(sizes, bounds, windows)

    group_count = lax.axis_size("groups")
    rounds = needs
    for turn in range(1, group_count):
        around = [(i, (i + turn) % group_count) for i in range(group_count)]
        rounds = jnp.maximum(rounds, lax.ppermute(needs, "groups", around))

    side_index = jnp.reshape(side, (1,)).astype(I32)

    def base(index, order):
        return base_product(index, flat, key_value_weight, own_columns, order)

    if sides == 2:
        theirs = base(1 - side_index, [ranges])
        added, order = [swap_sides(theirs)], [theirs]
    else:
        partial = jnp.dot(flat, key_value_weight, preferred_element_type=F32).astype(BF16)
        added = [lax.psum_scatter(partial, "tensor", scatter_dimension=1, tiled=True)]
        order = [ranges]
    def pass_on(m, order):
        part = cut(
            sizes, windows, sizes.forward_at + m, from_pair[m], sizes.passed, parts + 1, order
        )
        passed[m] = send(part, 1, owners)
        return [part]

    use = functools.partial(scores, sizes, ranges, flat)
    own_block = pack_more(sizes, 0, windows, down, up, [*order, rounds])
    order = [own_block]
    if sides == 2:
        added.append(base(side_index, order))
        order = added[-1:]
    order = pass_on(1, order)
    for m in split:
        block = pack_more(sizes, m, windows, down, up, order)
        from_pair[m] = send(block, 2 * m, owners)
        order = [block]
    before = use(
        [own_block, passed[0], from_pair[1]],
        [kept_bases[0], passed_bases[0], kept_bases[1]],
        (),
        order,
    )
    order = list(before)
    late = [(passed[1], passed_bases[1])]
    for m in far:
        part = cut(sizes, windows, sizes.third_at + m, from_pair[m], 1, parts, order)
        third[m - 1] = send(part, 2, owners)
        order = pass_on(m, [part])
        late += [(from_pair[m], kept_bases[m]), (passed[m], passed_bases[m])]

    last_up, passed_up = {}, {}
    for m in split:
        last_up[m] = pack_up(sizes, m, windows, up, order)
        order = [last_up[m]]
    for m in split:
        part = join(sizes, windows, m, from_pair[m], third[m], 0, order)
        passed[m] = send(part, 1, owners)
        order = [part]
        late += [(from_pair[m], kept_bases[m]), (third[m], kept_bases[m] + sizes.direct)]
    gated = gate([last_up[m] for m in split], order)
    for m, block in zip(split, gated):
        last_up[m] = send(block, 2 * m, owners)
    before = use(*map(list, zip(*late)), before, [gated[0]])
    order = before
    for m in split:
        part = join(sizes, windows, m, last_up[m], last_up[m], sizes.direct, order)
        passed_up[m] = send(part, 1, owners)
        order = [part]
    whole = sizes.whole[::-1]
    both = [own_block] + [from_pair[m] for m in whole] + [passed[m] for m in [0] + whole]
    held_up = collect(sizes, both, order)
    own, sent = use(
        [passed[m] for m in split], [passed_bases[m] for m in split], before, [held_up], fold=True
    )

    ups = [held_up] + [last_up[m] for m in split] + [passed_up[m] for m in split]
    slots = []
    for ms, start, size in (
        ([0] + whole, sizes.kept_base, sizes.kept),
        ([0] + whole, sizes.passed_base, sizes.passed),
        (split, sizes.kept_base, sizes.kept),
        (split, sizes.passed_base, sizes.passed),
    ):
        slots += [start(m) + k for m in ms for k in range(size)]
    left = spread(slots, rank, rows, ranges, *over_sides(own, sent))

    def with_rest():
        rest = Extra(sizes, counts)
        delta = jnp.zeros(added[0].shape, F32)
        for hop in range(owners):
            delta = lax.fori_loop(
                0, rounds[hop], functools.partial(rest.add, hop, hidden, down, up), delta
            )
        return final(left, added + [delta], ups)

    more = jnp.max(rounds) > 0
    out = lax.cond(more, with_rest, lambda: final(left, added, ups))
    return out.reshape(steps, rows, own_columns).transpose(2, 0, 1)


def solution(mesh):
    placed = (
        P(None, ("groups", "rollout"), "tensor"),
        P("groups"),
        P("tensor", None),
        P(("groups", "rollout"), None, "tensor"),
        P(("groups", "rollout"), None, "tensor"),
    )
    return jax.shard_map(
        local,
        mesh=mesh,
        in_specs=placed,
        out_specs=P("tensor", None, ("groups", "rollout")),
        check_vma=False,
    )
```

time: 113 us -> 108 us (0.956); the launches traced: 111 us -> 107 us
  Pallas kernels: 62 us -> 52.1 us
  waiting for transfers between devices: 22.1 us -> 26.5 us
    pallas_call x4 -> x3, Pallas kernels: 19.9 us -> 11.4 us  [scores(): pl.pallas_call(functools.partial(scores_kernel, bases, rank, rows, fold,...]
    ppermute x14 -> x10, waiting for transfers between devices: 19.8 us -> 23.9 us  [send(): return lax.ppermute(value, 'rollout', [(i, i ^ hop) for i in range(owners)])]
    pallas_call x9 -> x10, Pallas kernels: 12.8 us -> 10.5 us  [the longest x1 4.2 us: pack(): pl.pallas_call(functools.partial(pack_kernel, sizes), out_shape=[slots_in...]
    pallas_call x1, Pallas kernels: 2.49 us -> 4.01 us  [final(): pl.pallas_call(functools.partial(final_kernel, len(added)), out_shape=jax...]
    ppermute x14 -> x10, starting transfers between devices: 23.3 us -> 23.9 us  [send(): return lax.ppermute(value, 'rollout', [(i, i ^ hop) for i in range(owners)])]
  transfers between devices with their start and end apart: 17 -> 13, of which waited for: 5 -> 6; matrix products, arithmetic and copies ran while one was open for 0% -> 1% of each run, Pallas kernels for 50% -> 41%
where the time goes in v4:
time: 108 us; the launch traced here: 107 us
  Pallas kernels  52.1 us (48%)
  waiting for transfers between devices  26.5 us (25%)
  starting transfers between devices  25.5 us (24%)
  between operations  1.12 us (1%)
    ppermute x10, waiting for transfers between devices, send(): return lax.ppermute(value, 'rollout', [(i, i ^ hop) for i in range(owners)])  23.9 us
    ppermute x10, starting transfers between devices, send(): return lax.ppermute(value, 'rollout', [(i, i ^ hop) for i in range(owners)])  23.9 us
    pallas_call x2, Pallas kernels, base_product(): pl.pallas_call(functools.partial(base_kernel, len(after)), grid_spec=pltp...  20.9 us
    pallas_call x3, Pallas kernels, scores(): pl.pallas_call(functools.partial(scores_kernel, bases, rank, rows, fold,...  11.4 us
    pallas_call x1, Pallas kernels, ranges_of(): pl.pallas_call(functools.partial(ranges_kernel, sizes), out_shape=[jax.Sh...  4.62 us
    pallas_call x1, Pallas kernels, pack(): pl.pallas_call(functools.partial(pack_kernel, sizes), out_shape=[slots_in...  4.2 us
    pallas_call x1, Pallas kernels, final(): pl.pallas_call(functools.partial(final_kernel, len(added)), out_shape=jax...  4.01 us
  transfers between devices with their start and end apart: 13, of which 6 were waited for; matrix products, arithmetic and copies ran while one was open for 1% of the time, Pallas kernels for 41%

profile of v4, /device:TPU:0, one launch (start us, length us, event | category | flops | bytes accessed | tf_op | source)
XLA Modules:
  0.0 107.1 jit_solution(6137656058968406122)
XLA Ops:
  0.0 4.2 %pack.1 = (bf16[3,5,32,1024]{3,2,1,0:T(8,128)(2,1)S(1)}, bf16[3,5,32,1024]{3,2,1,0:T(8,128)(2,1)}, bf16[2,5,32,1024]{3,2,1,0:T(8,128)(2,1)S(1)}, s32[65]{0:T(128)S(1)}, s32[14]{0:T(128)S(1)}) custom-call(s32[64]{0:T(128)} %counts.1, bf16[8,32,4096]{2,1,0:T(8,128)(2,1)} %down.5, bf16[8,32,1024]{2,1,0:T(8,128)(2,1)} %up.7), custom_call_target="tpu_custom_call" | custom-call | flops 1000 | bytes 1000 | tf_op jit(solution)/shard_map/pack/pallas_call | solution.py:150
  4.2 0.8 copy-done.2
  5.0 3.0 %collective-permute-start.23 = (bf16[3,5,32,1024]{3,2,1,0:T(8,128)(2,1)}, bf16[3,5,32,1024]{3,2,1,0:T(8,128)(2,1)S(1)}, u32[]{:S(2)}, u32[]{:S(2)}) collective-permute-start(bf16[3,5,32,1024]{3,2,1,0:T(8,128)(2,1)} %get-tuple-element.1577), channel_id=1, source_target_pairs={{0,4},{2,6},{4,0},{6,2},{8,12},{10,14},{12,8},{14,10},{1,5},{3,7},... | collective-permute-start | bytes 2949128 | tf_op jit(solution)/shard_map/ppermute | solution.py:597
  8.1 2.5 %collective-permute-start.25 = (bf16[3,5,32,1024]{3,2,1,0:T(8,128)(2,1)S(1)}, bf16[3,5,32,1024]{3,2,1,0:T(8,128)(2,1)S(1)}, u32[]{:S(2)}, u32[]{:S(2)}) collective-permute-start(bf16[3,5,32,1024]{3,2,1,0:T(8,128)(2,1)S(1)} %get-tuple-element.1578), channel_id=1, source_target_pairs={{0,12},{2,14},{4,8},{6,10},{8,4},{10,6},{12,0},{14,2},{1,13},{3,15... | collective-permute-start | bytes 2949128 | tf_op jit(solution)/shard_map/ppermute | solution.py:597
  10.5 4.6 %ranges.1 = (s32[40]{0:T(128)S(1)}, s32[8]{0:T(128)S(1)}) custom-call(s32[65]{0:T(128)S(1)} %get-tuple-element.1573.bounds, s32[14]{0:T(128)S(1)} %get-tuple-element.1574.windows), custom_call_target="tpu_custom_call" | custom-call | flops 1000 | bytes 1000 | tf_op jit(solution)/shard_map/ranges/pallas_call | solution.py:412
  15.2 11.9 %base_product.2.refs_0_ = bf16[768,1024]{1,0:T(8,128)(2,1)} custom-call(s32[1]{0:T(128)S(6)} %sub.169.which, bf16[768,4096]{1,0:T(8,128)(2,1)} %bitcast.216, bf16[4096,2048]{1,0:T(8,128)(2,1)} %weight.3, s32[40]{0:T(128)S(1)} %get-tuple-element.1576.refs_0_.ranges), custom_call_target="tpu_custom_call" | custom-call | flops 1000 | bytes 1000 | tf_op jit(solution)/shard_map/base_product/pallas_call | solution.py:502
  27.2 1.6 %collective-permute-start.26 = (bf16[2,5,32,1024]{3,2,1,0:T(8,128)(2,1)S(1)}, bf16[2,5,32,1024]{3,2,1,0:T(8,128)(2,1)S(1)}, u32[]{:S(2)}, u32[]{:S(2)}) collective-permute-start(bf16[2,5,32,1024]{3,2,1,0:T(8,128)(2,1)S(1)} %copy-done.3), channel_id=1, source_target_pairs={{0,2},{2,0},{4,6},{6,4},{8,10},{10,8},{12,14},{14,12},{1,3},{3,1},... | collective-permute-start | bytes 1966088 | tf_op jit(solution)/shard_map/ppermute | solution.py:597
  28.7 1.5 %collective-permute-start.22 = (s32[8]{0:T(128)S(1)}, s32[8]{0:T(128)S(1)}, u32[]{:S(2)}, u32[]{:S(2)}) collective-permute-start(s32[8]{0:T(128)S(1)} %get-tuple-element.1575), channel_id=1, source_target_pairs={{0,16},{16,0},{1,17},{17,1},{2,18},{18,2},{3,19},{19,3},{4,20},{20... | collective-permute-start | bytes 104 | tf_op jit(solution)/shard_map/ppermute | solution.py:671
  30.2 2.0 %collective-permute-done.22 = s32[8]{0:T(128)S(1)} collective-permute-done((s32[8]{0:T(128)S(1)}, s32[8]{0:T(128)S(1)}, u32[]{:S(2)}, u32[]{:S(2)}) %collective-permute-start.22) | collective-permute-done | bytes 64 | tf_op jit(solution)/shard_map/ppermute | solution.py:671
  32.9 0.8 pack_more.2.refs_0_
  33.8 8.9 %base_product.3.refs_0_ = bf16[768,1024]{1,0:T(8,128)(2,1)S(1)} custom-call(s32[1]{0:T(128)} %bitcast.60.which, bf16[768,4096]{1,0:T(8,128)(2,1)S(1)} %bitcast.219, bf16[4096,2048]{1,0:T(8,128)(2,1)} %weight.3, bf16[3,5,32,1024]{3,2,1,0:T(8,128)(2,1)S(1)} %pack_more.2.refs_0_), custom_call_target="tpu_custom_call" | custom-call | flops 1000 | bytes 1000 | tf_op jit(solution)/shard_map/base_product/pallas_call | solution.py:502
  44.4 3.7 %scores.3.refs_0_.refs_5_ = f32[32,768]{1,0:T(8,128)S(1)} custom-call(s32[40]{0:T(128)S(1)} %get-tuple-element.1576.refs_0_.ranges, bf16[768,4096]{1,0:T(8,128)(2,1)S(1)} %bitcast.220, bf16[3,5,32,1024]{3,2,1,0:T(8,128)(2,1)S(1)} %pack_more.2.refs_0_, bf16[2,5,32,1024]{3,2,1,0:T(8,128)(2,1)S(1)} %collective-permute-done.26.refs_1_.refs_3_, ...), custom_call_target="tpu_custom_call" | custom-call | flops 1000 | bytes 1000 | tf_op jit(solution)/shard_map/scores/pallas_call | solution.py:477
  48.1 6.4 %collective-permute-done.25.block.refs_1_.refs_2_ = bf16[3,5,32,1024]{3,2,1,0:T(8,128)(2,1)S(1)} collective-permute-done((bf16[3,5,32,1024]{3,2,1,0:T(8,128)(2,1)S(1)}, bf16[3,5,32,1024]{3,2,1,0:T(8,128)(2,1)S(1)}, u32[]{:S(2)}, u32[]{:S(2)}) %collective-permute-start.25) | collective-permute-done | bytes 983072 | tf_op jit(solution)/shard_map/ppermute | solution.py:597
  55.1 10.8 %collective-permute-start.27 = (bf16[1,4,32,1024]{3,2,1,0:T(8,128)(2,1)S(1)}, bf16[1,4,32,1024]{3,2,1,0:T(8,128)(2,1)S(1)}, u32[]{:S(2)}, u32[]{:S(2)}) collective-permute-start(bf16[1,4,32,1024]{3,2,1,0:T(8,128)(2,1)S(1)} %cut.4.refs_0_), channel_id=1, source_target_pairs={{0,4},{2,6},{4,0},{6,2},{8,12},{10,14},{12,8},{14,10},{1,5},{3,7},... | collective-permute-start | bytes 786440 | tf_op jit(solution)/shard_map/ppermute | solution.py:597
  66.7 1.6 %collective-permute-start.30 = (bf16[2,5,32,1024]{3,2,1,0:T(8,128)(2,1)S(1)}, bf16[2,5,32,1024]{3,2,1,0:T(8,128)(2,1)S(1)}, u32[]{:S(2)}, u32[]{:S(2)}) collective-permute-start(bf16[2,5,32,1024]{3,2,1,0:T(8,128)(2,1)S(1)} %cut.5.refs_0_), channel_id=1, source_target_pairs={{0,2},{2,0},{4,6},{6,4},{8,10},{10,8},{12,14},{14,12},{1,3},{3,1},... | collective-permute-start | bytes 1966088 | tf_op jit(solution)/shard_map/ppermute | solution.py:597
  68.8 0.8 pack_up.1.refs_0_
  69.6 8.9 %collective-permute-done.27.third.refs_4_ = bf16[1,4,32,1024]{3,2,1,0:T(8,128)(2,1)S(1)} collective-permute-done((bf16[1,4,32,1024]{3,2,1,0:T(8,128)(2,1)S(1)}, bf16[1,4,32,1024]{3,2,1,0:T(8,128)(2,1)S(1)}, u32[]{:S(2)}, u32[]{:S(2)}) %collective-permute-start.27) | collective-permute-done | bytes 262176 | tf_op jit(solution)/shard_map/ppermute | solution.py:597
  79.2 1.6 %collective-permute-start.28 = (bf16[2,4,32,1024]{3,2,1,0:T(8,128)(2,1)S(1)}, bf16[2,4,32,1024]{3,2,1,0:T(8,128)(2,1)S(1)}, u32[]{:S(2)}, u32[]{:S(2)}) collective-permute-start(bf16[2,4,32,1024]{3,2,1,0:T(8,128)(2,1)S(1)} %join.2.refs_1_), channel_id=1, source_target_pairs={{0,2},{2,0},{4,6},{6,4},{8,10},{10,8},{12,14},{14,12},{1,3},{3,1},... | collective-permute-start | bytes 1572872 | tf_op jit(solution)/shard_map/ppermute | solution.py:597
  81.4 8.4 %collective-permute-done.29.refs_0_.refs_4_ = bf16[2,5,32,1024]{3,2,1,0:T(8,128)(2,1)S(1)} collective-permute-done((bf16[2,5,32,1024]{3,2,1,0:T(8,128)(2,1)S(1)}, bf16[2,5,32,1024]{3,2,1,0:T(8,128)(2,1)S(1)}, u32[]{:S(2)}, u32[]{:S(2)}) %collective-permute-start.29) | collective-permute-done | bytes 655392 | tf_op jit(solution)/shard_map/ppermute | solution.py:597
  89.8 4.2 %scores.4.refs_0_.refs_1_ = f32[32,768]{1,0:T(8,128)S(1)} custom-call(s32[40]{0:T(128)S(1)} %get-tuple-element.1576.refs_0_.ranges, bf16[768,4096]{1,0:T(8,128)(2,1)S(1)} %bitcast.221, bf16[2,5,32,1024]{3,2,1,0:T(8,128)(2,1)S(1)} %collective-permute-done.29.refs_0_.refs_4_, bf16[3,5,32,1024]{3,2,1,0:T(8,128)(2,1)S(1)} %collective-permute-done.25.block.refs_1_.refs_2_, ...), custom_call_target="tpu_custom_call" | custom-call | flops 1000 | bytes 1000 | tf_op jit(solution)/shard_map/scores/pallas_call | solution.py:477
  94.8 1.6 %collective-permute-start.34 = (bf16[2,1,32,1024]{3,2,1,0:T(8,128)(2,1)S(1)}, bf16[2,1,32,1024]{3,2,1,0:T(8,128)(2,1)S(1)}, u32[]{:S(2)}, u32[]{:S(2)}) collective-permute-start(bf16[2,1,32,1024]{3,2,1,0:T(8,128)(2,1)S(1)} %join.3.refs_6_), channel_id=1, source_target_pairs={{0,2},{2,0},{4,6},{6,4},{8,10},{10,8},{12,14},{14,12},{1,3},{3,1},... | collective-permute-start | bytes 393224 | tf_op jit(solution)/shard_map/ppermute | solution.py:597
  97.1 3.4 %scores.5 = (f32[32,768]{1,0:T(8,128)S(1)}, bf16[32,768]{1,0:T(8,128)(2,1)S(1)}) custom-call(s32[40]{0:T(128)S(1)} %get-tuple-element.1576.refs_0_.ranges, bf16[768,4096]{1,0:T(8,128)(2,1)S(1)} %bitcast.222, bf16[2,4,32,1024]{3,2,1,0:T(8,128)(2,1)S(1)} %collective-permute-done.28.refs_0_, f32[32,768]{1,0:T(8,128)S(1)} %scores.4.refs_0_.refs_1_, ...), custom_call_target="tpu_custom_call" | custom-call | flops 1000 | bytes 1000 | tf_op jit(solution)/shard_map/scores/pallas_call | solution.py:477
  102.6 4.3 %conditional.1 = (bf16[768,1024]{1,0:T(8,128)(2,1)}) conditional(s32[]{:T(128)} %convert_element_type.129, (bf16[640,768]{1,0:T(8,128)(2,1)S(1)}, bf16[768,1024]{1,0:T(8,128)(2,1)}, bf16[768,1024]{1,0:T(8,128)(2,1)}, bf16[15,1,32,1024]{3,2,1,0:T(8,128)(2,1)S(1)}, bf16[3,1,32,1024]{3,2,1,0:T(8,128)(2,1)S(1)}, ...), branch_computations={%region_1.0_spmd, %region_2.22_spmd} | conditional | flops 2020593920 | bytes 134372608 | solution.py:763
  102.6 4.0 %final.2 = bf16[768,1024]{1,0:T(8,128)(2,1)} custom-call(bf16[640,768]{1,0:T(8,128)(2,1)S(1)} %get-tuple-element.1444.left, bf16[768,1024]{1,0:T(8,128)(2,1)} %get-tuple-element.1445.refs_0_, bf16[768,1024]{1,0:T(8,128)(2,1)} %get-tuple-element.1446.refs_1_, bf16[15,1,32,1024]{3,2,1,0:T(8,128)(2,1)S(1)} %get-tuple-element.1447.refs_2_, ...), custom_call_target="tpu_custom_call" | custom-call | flops 1000 | bytes 1000 | tf_op jit(solution)/shard_map/cond/branch_0_fun/final/pallas_call | solution.py:582
  (42 shorter events, 8.3 us)
Async XLA Ops:
  4.2 0.8 copy-start.2
  5.0 37.7 %collective-permute-start.23 = (bf16[3,5,32,1024]{3,2,1,0:T(8,128)(2,1)}, bf16[3,5,32,1024]{3,2,1,0:T(8,128)(2,1)S(1)}, u32[]{:S(2)}, u32[]{:S(2)}) collective-permute-start(bf16[3,5,32,1024]{3,2,1,0:T(8,128)(2,1)} %get-tuple-element.1577), channel_id=1, source_target_pairs={{0,4},{2,6},{4,0},{6,2},{8,12},{10,14},{12,8},{14,10},{1,5},{3,7},... | collective-permute-start | bytes 2949128 | tf_op jit(solution)/shard_map/ppermute | solution.py:597
  8.1 46.5 %collective-permute-start.25 = (bf16[3,5,32,1024]{3,2,1,0:T(8,128)(2,1)S(1)}, bf16[3,5,32,1024]{3,2,1,0:T(8,128)(2,1)S(1)}, u32[]{:S(2)}, u32[]{:S(2)}) collective-permute-start(bf16[3,5,32,1024]{3,2,1,0:T(8,128)(2,1)S(1)} %get-tuple-element.1578), channel_id=1, source_target_pairs={{0,12},{2,14},{4,8},{6,10},{8,4},{10,6},{12,0},{14,2},{1,13},{3,15... | collective-permute-start | bytes 2949128 | tf_op jit(solution)/shard_map/ppermute | solution.py:597
  15.2 18.6 %slice-start = ((s8[6291456]{0:T(1024)(128)(4,1)}), s8[4194304]{0:T(1024)(128)(4,1)S(1)}, s32[]{:S(2)}) async-start(s8[6291456]{0:T(1024)(128)(4,1)} %bitcast.217), calls=%async_computation | async-start | bytes 8388608
  15.2 12.0 %copy-start.3 = (bf16[2,5,32,1024]{3,2,1,0:T(8,128)(2,1)S(1)}, bf16[2,5,32,1024]{3,2,1,0:T(8,128)(2,1)}, u32[]{:S(2)}) copy-start(bf16[2,5,32,1024]{3,2,1,0:T(8,128)(2,1)} %copy-done.2) | copy-start | bytes 1966084
  15.2 17.7 %copy-start.4 = (bf16[8,32,4096]{2,1,0:T(8,128)(2,1)S(1)}, bf16[8,32,4096]{2,1,0:T(8,128)(2,1)}, u32[]{:S(2)}) copy-start(bf16[8,32,4096]{2,1,0:T(8,128)(2,1)} %down.5) | copy-start | bytes 6291460
  15.2 17.7 %copy-start.5 = (bf16[8,32,1024]{2,1,0:T(8,128)(2,1)S(1)}, bf16[8,32,1024]{2,1,0:T(8,128)(2,1)}, u32[]{:S(2)}) copy-start(bf16[8,32,1024]{2,1,0:T(8,128)(2,1)} %up.7) | copy-start | bytes 1572868
  15.2 18.5 %slice-start.1 = ((s8[6291456]{0:T(1024)(128)(4,1)}), s8[2097152]{0:T(1024)(128)(4,1)S(1)}, s32[]{:S(2)}) async-start(s8[6291456]{0:T(1024)(128)(4,1)} %bitcast.217), calls=%async_computation.1 | async-start | bytes 4194304
  27.2 75.4 %collective-permute-start.33 = (bf16[768,1024]{1,0:T(8,128)(2,1)}, bf16[768,1024]{1,0:T(8,128)(2,1)}, u32[]{:S(2)}, u32[]{:S(2)}) collective-permute-start(bf16[768,1024]{1,0:T(8,128)(2,1)} %base_product.2.refs_0_), channel_id=1, source_target_pairs={{0,1},{1,0},{2,3},{3,2},{4,5},{5,4},{6,7},{7,6},{8,9},{9,8},{10,11... | collective-permute-start | bytes 4718600 | tf_op jit(solution)/shard_map/ppermute | solution.py:640
  27.2 17.2 %collective-permute-start.26 = (bf16[2,5,32,1024]{3,2,1,0:T(8,128)(2,1)S(1)}, bf16[2,5,32,1024]{3,2,1,0:T(8,128)(2,1)S(1)}, u32[]{:S(2)}, u32[]{:S(2)}) collective-permute-start(bf16[2,5,32,1024]{3,2,1,0:T(8,128)(2,1)S(1)} %copy-done.3), channel_id=1, source_target_pairs={{0,2},{2,0},{4,6},{6,4},{8,10},{10,8},{12,14},{14,12},{1,3},{3,1},... | collective-permute-start | bytes 1966088 | tf_op jit(solution)/shard_map/ppermute | solution.py:597
  28.7 3.5 %collective-permute-start.22 = (s32[8]{0:T(128)S(1)}, s32[8]{0:T(128)S(1)}, u32[]{:S(2)}, u32[]{:S(2)}) collective-permute-start(s32[8]{0:T(128)S(1)} %get-tuple-element.1575), channel_id=1, source_target_pairs={{0,16},{16,0},{1,17},{17,1},{2,18},{18,2},{3,19},{19,3},{4,20},{20... | collective-permute-start | bytes 104 | tf_op jit(solution)/shard_map/ppermute | solution.py:671
  42.7 24.0 %copy-start.7 = (bf16[768,1024]{1,0:T(8,128)(2,1)}, bf16[768,1024]{1,0:T(8,128)(2,1)S(1)}, u32[]{:S(2)}) copy-start(bf16[768,1024]{1,0:T(8,128)(2,1)S(1)} %base_product.3.refs_0_) | copy-start | bytes 4718596
  44.2 34.4 %collective-permute-start.24 = (bf16[2,4,32,1024]{3,2,1,0:T(8,128)(2,1)S(1)}, bf16[2,4,32,1024]{3,2,1,0:T(8,128)(2,1)S(1)}, u32[]{:S(2)}, u32[]{:S(2)}) collective-permute-start(bf16[2,4,32,1024]{3,2,1,0:T(8,128)(2,1)S(1)} %pack_more.3.refs_3_), channel_id=1, source_target_pairs={{0,8},{2,10},{4,12},{6,14},{8,0},{10,2},{12,4},{14,6},{1,9},{3,11}... | collective-permute-start | bytes 1572872 | tf_op jit(solution)/shard_map/ppermute | solution.py:597
  55.1 23.5 %collective-permute-start.27 = (bf16[1,4,32,1024]{3,2,1,0:T(8,128)(2,1)S(1)}, bf16[1,4,32,1024]{3,2,1,0:T(8,128)(2,1)S(1)}, u32[]{:S(2)}, u32[]{:S(2)}) collective-permute-start(bf16[1,4,32,1024]{3,2,1,0:T(8,128)(2,1)S(1)} %cut.4.refs_0_), channel_id=1, source_target_pairs={{0,4},{2,6},{4,0},{6,2},{8,12},{10,14},{12,8},{14,10},{1,5},{3,7},... | collective-permute-start | bytes 786440 | tf_op jit(solution)/shard_map/ppermute | solution.py:597
  66.7 14.7 %collective-permute-start.30 = (bf16[2,5,32,1024]{3,2,1,0:T(8,128)(2,1)S(1)}, bf16[2,5,32,1024]{3,2,1,0:T(8,128)(2,1)S(1)}, u32[]{:S(2)}, u32[]{:S(2)}) collective-permute-start(bf16[2,5,32,1024]{3,2,1,0:T(8,128)(2,1)S(1)} %cut.5.refs_0_), channel_id=1, source_target_pairs={{0,2},{2,0},{4,6},{6,4},{8,10},{10,8},{12,14},{14,12},{1,3},{3,1},... | collective-permute-start | bytes 1966088 | tf_op jit(solution)/shard_map/ppermute | solution.py:597
  68.3 21.5 %collective-permute-start.29 = (bf16[2,5,32,1024]{3,2,1,0:T(8,128)(2,1)S(1)}, bf16[2,5,32,1024]{3,2,1,0:T(8,128)(2,1)S(1)}, u32[]{:S(2)}, u32[]{:S(2)}) collective-permute-start(bf16[2,5,32,1024]{3,2,1,0:T(8,128)(2,1)S(1)} %cut.3.refs_0_), channel_id=1, source_target_pairs={{0,2},{2,0},{4,6},{6,4},{8,10},{10,8},{12,14},{14,12},{1,3},{3,1},... | collective-permute-start | bytes 1966088 | tf_op jit(solution)/shard_map/ppermute | solution.py:597
  79.2 17.9 %collective-permute-start.28 = (bf16[2,4,32,1024]{3,2,1,0:T(8,128)(2,1)S(1)}, bf16[2,4,32,1024]{3,2,1,0:T(8,128)(2,1)S(1)}, u32[]{:S(2)}, u32[]{:S(2)}) collective-permute-start(bf16[2,4,32,1024]{3,2,1,0:T(8,128)(2,1)S(1)} %join.2.refs_1_), channel_id=1, source_target_pairs={{0,2},{2,0},{4,6},{6,4},{8,10},{10,8},{12,14},{14,12},{1,3},{3,1},... | collective-permute-start | bytes 1572872 | tf_op jit(solution)/shard_map/ppermute | solution.py:597
  80.7 13.3 %collective-permute-start.31 = (bf16[3,1,32,1024]{3,2,1,0:T(8,128)(2,1)S(1)}, bf16[3,1,32,1024]{3,2,1,0:T(8,128)(2,1)S(1)}, u32[]{:S(2)}, u32[]{:S(2)}) collective-permute-start(bf16[3,1,32,1024]{3,2,1,0:T(8,128)(2,1)S(1)} %gate.1.refs_6_), channel_id=1, source_target_pairs={{0,8},{2,10},{4,12},{6,14},{8,0},{10,2},{12,4},{14,6},{1,9},{3,11}... | collective-permute-start | bytes 589832 | tf_op jit(solution)/shard_map/ppermute | solution.py:597
  94.8 7.8 %collective-permute-start.34 = (bf16[2,1,32,1024]{3,2,1,0:T(8,128)(2,1)S(1)}, bf16[2,1,32,1024]{3,2,1,0:T(8,128)(2,1)S(1)}, u32[]{:S(2)}, u32[]{:S(2)}) collective-permute-start(bf16[2,1,32,1024]{3,2,1,0:T(8,128)(2,1)S(1)} %join.3.refs_6_), channel_id=1, source_target_pairs={{0,2},{2,0},{4,6},{6,4},{8,10},{10,8},{12,14},{14,12},{1,3},{3,1},... | collective-permute-start | bytes 393224 | tf_op jit(solution)/shard_map/ppermute | solution.py:597
  96.9 5.6 %copy-start.6 = (bf16[8,32,1024]{2,1,0:T(8,128)(2,1)S(1)}, bf16[8,32,1024]{2,1,0:T(8,128)(2,1)}, u32[]{:S(2)}) copy-start(bf16[8,32,1024]{2,1,0:T(8,128)(2,1)} %up.7) | copy-start | bytes 1572868
  96.9 5.6 %copy-start.8 = (s32[64]{0:T(128)S(1)}, s32[64]{0:T(128)}, u32[]{:S(2)}) copy-start(s32[64]{0:T(128)} %counts.1) | copy-start | bytes 772
  100.5 1.3 %collective-permute-start.32 = (bf16[32,768]{1,0:T(8,128)(2,1)S(1)}, bf16[32,768]{1,0:T(8,128)(2,1)S(1)}, u32[]{:S(2)}, u32[]{:S(2)}) collective-permute-start(bf16[32,768]{1,0:T(8,128)(2,1)S(1)} %get-tuple-element.1581), channel_id=1, source_target_pairs={{0,1},{1,0},{2,3},{3,2},{4,5},{5,4},{6,7},{7,6},{8,9},{9,8},{10,11... | collective-permute-start | bytes 147464 | tf_op jit(solution)/shard_map/ppermute | solution.py:640

commit v5 on v4

--- a/solution.py
+++ b/solution.py
@@ -432,14 +432,16 @@
     return row
 
 
-def scores_kernel(bases, rank, rows, fold, n_before, n_after, ranges, hidden, *refs):
+def scores_kernel(bases, rank, rows, fold, n_before, n_after, staged, ranges, hidden, *refs):
     blocks, refs = refs[: len(bases)], refs[len(bases) :]
     before, refs = refs[:n_before], refs[n_before + n_after :]
     out, total = refs[0], refs[-1]
     k = pl.program_id(0)
+    tile = blocks[0].shape[3]
+    here = pl.ds(pl.multiple_of(k * tile, tile), tile)
     part = lax.dot_general(
         jnp.concatenate([b[n, k] for b in blocks for n in range(b.shape[0])], axis=0),
-        hidden[...],
+        hidden[:, here] if staged else hidden[...],
         (((1,), (1,)), ((), ())),
         preferred_element_type=F32,
     )
@@ -467,7 +469,7 @@
             refs[1][...] = acc.astype(BF16)
 
 
-def scores(sizes, ranges, hidden, blocks, bases, before=(), after=(), fold=False):
+def scores(sizes, ranges, hidden, blocks, bases, before=(), after=(), fold=False, staged=False):
     total_rows = hidden.shape[0]
     rank, rows = sizes.rank, sizes.rows
     deep = sum(b.shape[0] for b in blocks) * rank
@@ -475,10 +477,15 @@
     if fold:
         out_shape.append(pltpu.VMEM((rank, total_rows), BF16))
     return pl.pallas_call(
-        functools.partial(scores_kernel, bases, rank, rows, fold, len(before), len(after)),
+        functools.partial(
+            scores_kernel, bases, rank, rows, fold, len(before), len(after), staged
+        ),
         grid=(sizes.parts,),
         out_shape=out_shape,
-        in_specs=[IN_SMEM, pl.BlockSpec((total_rows, sizes.columns), lambda k: (0, k))]
+        in_specs=[
+            IN_SMEM,
+            IN_VMEM if staged else pl.BlockSpec((total_rows, sizes.columns), lambda k: (0, k)),
+        ]
         + [IN_VMEM] * (len(blocks) + len(before))
         + [ANYWHERE] * len(after),
         out_specs=[IN_VMEM] * len(out_shape),
@@ -487,6 +494,26 @@
         cost_estimate=SMALL,
         name="scores",
     )(ranges, hidden, *map(held_in_vmem, blocks), *map(held_in_vmem, before), *after)
+
+
+def stage_kernel(n_after, hidden, *refs):
+    out, sem = refs[n_after:]
+    copy = pltpu.make_async_copy(hidden, out, sem)
+    copy.start()
+    copy.wait()
+
+
+def stage(hidden, after):
+    return pl.pallas_call(
+        functools.partial(stage_kernel, len(after)),
+        out_shape=pltpu.VMEM(hidden.shape, hidden.dtype),
+        in_specs=[ANYWHERE] * (1 + len(after)),
+        out_specs=IN_VMEM,
+        scratch_shapes=[pltpu.SemaphoreType.DMA],
+        compiler_params=PARAMS,
+        cost_estimate=SMALL,
+        name="stage",
+    )(hidden, *after)
 
 
 def base_kernel(n_after, which, hidden, weight, *refs):
@@ -690,16 +717,12 @@
         return [part]
 
     use = functools.partial(scores, sizes, ranges, flat)
-    own_block = pack_more(sizes, 0, windows, down, up, [*order, rounds])
+    own_block = pack_more(sizes, 0, windows, down, up, [*order, rounds, passed[0]])
     order = [own_block]
     if sides == 2:
         added.append(base(side_index, order))
         order = added[-1:]
     order = pass_on(1, order)
-    for m in split:
-        block = pack_more(sizes, m, windows, down, up, order)
-        from_pair[m] = send(block, 2 * m, owners)
-        order = [block]
     before = use(
         [own_block, passed[0], from_pair[1]],
         [kept_bases[0], passed_bases[0], kept_bases[1]],
@@ -707,6 +730,11 @@
         order,
     )
     order = list(before)
+    for m in split:
+        block = pack_more(sizes, m, windows, down, up, order)
+        from_pair[m] = send(block, 2 * m, owners)
+        order = [block]
+    order = [*order, passed[1]]
     late = [(passed[1], passed_bases[1])]
     for m in far:
         part = cut(sizes, windows, sizes.third_at + m, from_pair[m], 1, parts, order)
@@ -727,18 +755,26 @@
     for m, block in zip(split, gated):
         last_up[m] = send(block, 2 * m, owners)
     before = use(*map(list, zip(*late)), before, [gated[0]])
-    order = before
+    whole = sizes.whole[::-1]
+    both = [own_block] + [from_pair[m] for m in whole] + [passed[m] for m in [0] + whole]
+    held_up = collect(sizes, both, before)
+    staged = stage(flat, [held_up])
+    order = [staged]
     for m in split:
         part = join(sizes, windows, m, last_up[m], last_up[m], sizes.direct, order)
         passed_up[m] = send(part, 1, owners)
         order = [part]
-    whole = sizes.whole[::-1]
-    both = [own_block] + [from_pair[m] for m in whole] + [passed[m] for m in [0] + whole]
-    held_up = collect(sizes, both, order)
-    own, sent = use(
-        [passed[m] for m in split], [passed_bases[m] for m in split], before, [held_up], fold=True
+    own, sent = scores(
+        sizes,
+        ranges,
+        held_in_vmem(staged),
+        [passed[m] for m in split],
+        [passed_bases[m] for m in split],
+        before,
+        order,
+        fold=True,
+        staged=True,
     )
-
     ups = [held_up] + [last_up[m] for m in split] + [passed_up[m] for m in split]
     slots = []
     for ms, start, size in (

time: 108 us -> 104 us (0.963)
  starting transfers between devices: 25.5 us -> 23.3 us
    ppermute x10, starting transfers between devices: 23.9 us -> 21.6 us  [send(): return lax.ppermute(value, 'rollout', [(i, i ^ hop) for i in range(owners)])]
    ppermute x1, waiting for transfers between devices: 2.02 us -> 0.01 us  [local(): rounds = jnp.maximum(rounds, lax.ppermute(needs, 'groups', around))]
    ppermute x10, waiting for transfers between devices: 23.9 us -> 25.4 us  [send(): return lax.ppermute(value, 'rollout', [(i, i ^ hop) for i in range(owners)])]
  transfers between devices with their start and end apart: 13 -> 13, of which waited for: 6 -> 6; matrix products, arithmetic and copies ran while one was open for 1% -> 1% of each run, Pallas kernels for 41% -> 42%
where the time goes in v5:
time: 104 us
  Pallas kernels  52.6 us (51%)
  waiting for transfers between devices  26.1 us (25%)
  starting transfers between devices  23.3 us (22%)
    ppermute x10, waiting for transfers between devices, send(): return lax.ppermute(value, 'rollout', [(i, i ^ hop) for i in range(owners)])  25.4 us
    ppermute x10, starting transfers between devices, send(): return lax.ppermute(value, 'rollout', [(i, i ^ hop) for i in range(owners)])  21.6 us
    pallas_call x2, Pallas kernels, base_product(): pl.pallas_call(functools.partial(base_kernel, len(after)), grid_spec=pltp...  20.7 us
    pallas_call x3, Pallas kernels, scores(): pl.pallas_call(functools.partial(scores_kernel, bases, rank, rows, fold,...  11 us
    pallas_call x1, Pallas kernels, pack(): pl.pallas_call(functools.partial(pack_kernel, sizes), out_shape=[slots_in...  4.7 us
    pallas_call x1, Pallas kernels, ranges_of(): pl.pallas_call(functools.partial(ranges_kernel, sizes), out_shape=[jax.Sh...  4.62 us
    pallas_call x1, Pallas kernels, final(): pl.pallas_call(functools.partial(final_kernel, len(added)), out_shape=jax...  4.01 us
    pallas_call x3, Pallas kernels, cut(): pl.pallas_call(functools.partial(cut_kernel, index, len(after)), out_shap...  2.09 us
  transfers between devices with their start and end apart: 13, of which 6 were waited for; matrix products, arithmetic and copies ran while one was open for 1% of the time, Pallas kernels for 42%

profile of v5, /device:TPU:0, one launch (start us, length us, event | category | flops | bytes accessed | tf_op | source)
XLA Modules:
  0.0 104.0 jit_solution(10932189271613927340)
XLA Ops:
  0.0 4.7 %pack.1 = (bf16[3,5,32,1024]{3,2,1,0:T(8,128)(2,1)}, bf16[3,5,32,1024]{3,2,1,0:T(8,128)(2,1)}, bf16[2,5,32,1024]{3,2,1,0:T(8,128)(2,1)}, s32[65]{0:T(128)S(1)}, s32[14]{0:T(128)S(1)}) custom-call(s32[64]{0:T(128)} %counts.1, bf16[8,32,4096]{2,1,0:T(8,128)(2,1)} %down.5, bf16[8,32,1024]{2,1,0:T(8,128)(2,1)} %up.7), custom_call_target="tpu_custom_call" | custom-call | flops 1000 | bytes 1000 | tf_op jit(solution)/shard_map/pack/pallas_call | solution.py:150
  4.7 3.1 %collective-permute-start.24 = (bf16[3,5,32,1024]{3,2,1,0:T(8,128)(2,1)}, bf16[3,5,32,1024]{3,2,1,0:T(8,128)(2,1)S(1)}, u32[]{:S(2)}, u32[]{:S(2)}) collective-permute-start(bf16[3,5,32,1024]{3,2,1,0:T(8,128)(2,1)} %get-tuple-element.1578), channel_id=1, source_target_pairs={{0,4},{2,6},{4,0},{6,2},{8,12},{10,14},{12,8},{14,10},{1,5},{3,7},... | collective-permute-start | bytes 2949128 | tf_op jit(solution)/shard_map/ppermute | solution.py:624
  7.8 1.5 %collective-permute-start.23 = (bf16[2,5,32,1024]{3,2,1,0:T(8,128)(2,1)}, bf16[2,5,32,1024]{3,2,1,0:T(8,128)(2,1)S(1)}, u32[]{:S(2)}, u32[]{:S(2)}) collective-permute-start(bf16[2,5,32,1024]{3,2,1,0:T(8,128)(2,1)} %get-tuple-element.1577), channel_id=1, source_target_pairs={{0,2},{2,0},{4,6},{6,4},{8,10},{10,8},{12,14},{14,12},{1,3},{3,1},... | collective-permute-start | bytes 1966088 | tf_op jit(solution)/shard_map/ppermute | solution.py:624
  9.3 2.5 %collective-permute-start.25 = (bf16[3,5,32,1024]{3,2,1,0:T(8,128)(2,1)}, bf16[3,5,32,1024]{3,2,1,0:T(8,128)(2,1)S(1)}, u32[]{:S(2)}, u32[]{:S(2)}) collective-permute-start(bf16[3,5,32,1024]{3,2,1,0:T(8,128)(2,1)} %get-tuple-element.1579), channel_id=1, source_target_pairs={{0,12},{2,14},{4,8},{6,10},{8,4},{10,6},{12,0},{14,2},{1,13},{3,15... | collective-permute-start | bytes 2949128 | tf_op jit(solution)/shard_map/ppermute | solution.py:624
  11.8 4.6 %ranges.1 = (s32[40]{0:T(128)S(1)}, s32[8]{0:T(128)S(1)}) custom-call(s32[65]{0:T(128)S(1)} %get-tuple-element.1573.bounds, s32[14]{0:T(128)S(1)} %get-tuple-element.1574.windows), custom_call_target="tpu_custom_call" | custom-call | flops 1000 | bytes 1000 | tf_op jit(solution)/shard_map/ranges/pallas_call | solution.py:412
  16.4 1.6 %collective-permute-start.22 = (s32[8]{0:T(128)S(1)}, s32[8]{0:T(128)S(1)}, u32[]{:S(2)}, u32[]{:S(2)}) collective-permute-start(s32[8]{0:T(128)S(1)} %get-tuple-element.1575), channel_id=1, source_target_pairs={{0,16},{16,0},{1,17},{17,1},{2,18},{18,2},{3,19},{19,3},{4,20},{20... | collective-permute-start | bytes 104 | tf_op jit(solution)/shard_map/ppermute | solution.py:698
  18.0 11.8 %base_product.2.refs_0_ = bf16[768,1024]{1,0:T(8,128)(2,1)} custom-call(s32[1]{0:T(128)S(6)} %sub.169.which, bf16[768,4096]{1,0:T(8,128)(2,1)} %bitcast.216, bf16[4096,2048]{1,0:T(8,128)(2,1)} %weight.3, s32[40]{0:T(128)S(1)} %get-tuple-element.1576.refs_0_.ranges), custom_call_target="tpu_custom_call" | custom-call | flops 1000 | bytes 1000 | tf_op jit(solution)/shard_map/base_product/pallas_call | solution.py:529
  30.4 0.8 pack_more.2.refs_0_
  31.3 8.9 %base_product.3.refs_0_ = bf16[768,1024]{1,0:T(8,128)(2,1)S(1)} custom-call(s32[1]{0:T(128)} %bitcast.60.which, bf16[768,4096]{1,0:T(8,128)(2,1)S(1)} %bitcast.219, bf16[4096,2048]{1,0:T(8,128)(2,1)} %weight.3, bf16[3,5,32,1024]{3,2,1,0:T(8,128)(2,1)S(1)} %pack_more.2.refs_0_), custom_call_target="tpu_custom_call" | custom-call | flops 1000 | bytes 1000 | tf_op jit(solution)/shard_map/base_product/pallas_call | solution.py:529
  40.2 0.8 cut.3.refs_3_
  41.6 3.7 %scores.3.refs_0_.refs_5_ = f32[32,768]{1,0:T(8,128)S(1)} custom-call(s32[40]{0:T(128)S(1)} %get-tuple-element.1576.refs_0_.ranges, bf16[768,4096]{1,0:T(8,128)(2,1)S(1)} %bitcast.220, bf16[3,5,32,1024]{3,2,1,0:T(8,128)(2,1)S(1)} %pack_more.2.refs_0_, bf16[2,5,32,1024]{3,2,1,0:T(8,128)(2,1)S(1)} %collective-permute-done.23.refs_2_.refs_1_.refs_3_, ...), custom_call_target="tpu_custom_call" | custom-call | flops 1000 | bytes 1000 | tf_op jit(solution)/shard_map/scores/pallas_call | solution.py:479
  46.2 8.1 %collective-permute-done.25.block.refs_1_.refs_2_ = bf16[3,5,32,1024]{3,2,1,0:T(8,128)(2,1)S(1)} collective-permute-done((bf16[3,5,32,1024]{3,2,1,0:T(8,128)(2,1)}, bf16[3,5,32,1024]{3,2,1,0:T(8,128)(2,1)S(1)}, u32[]{:S(2)}, u32[]{:S(2)}) %collective-permute-start.25) | collective-permute-done | bytes 983072 | tf_op jit(solution)/shard_map/ppermute | solution.py:624
  54.3 3.9 %collective-permute-done.26.refs_1_.refs_0_.refs_4_ = bf16[2,5,32,1024]{3,2,1,0:T(8,128)(2,1)S(1)} collective-permute-done((bf16[2,5,32,1024]{3,2,1,0:T(8,128)(2,1)S(1)}, bf16[2,5,32,1024]{3,2,1,0:T(8,128)(2,1)S(1)}, u32[]{:S(2)}, u32[]{:S(2)}) %collective-permute-start.26) | collective-permute-done | bytes 655392 | tf_op jit(solution)/shard_map/ppermute | solution.py:624
  58.8 9.1 %collective-permute-start.29 = (bf16[1,4,32,1024]{3,2,1,0:T(8,128)(2,1)S(1)}, bf16[1,4,32,1024]{3,2,1,0:T(8,128)(2,1)S(1)}, u32[]{:S(2)}, u32[]{:S(2)}) collective-permute-start(bf16[1,4,32,1024]{3,2,1,0:T(8,128)(2,1)S(1)} %cut.4.refs_0_), channel_id=1, source_target_pairs={{0,4},{2,6},{4,0},{6,2},{8,12},{10,14},{12,8},{14,10},{1,5},{3,7},... | collective-permute-start | bytes 786440 | tf_op jit(solution)/shard_map/ppermute | solution.py:624
  69.0 0.8 pack_up.1.refs_0_
  69.9 7.1 %collective-permute-done.28.direct.refs_3_ = bf16[2,4,32,1024]{3,2,1,0:T(8,128)(2,1)S(1)} collective-permute-done((bf16[2,4,32,1024]{3,2,1,0:T(8,128)(2,1)S(1)}, bf16[2,4,32,1024]{3,2,1,0:T(8,128)(2,1)S(1)}, u32[]{:S(2)}, u32[]{:S(2)}) %collective-permute-start.28) | collective-permute-done | bytes 524320 | tf_op jit(solution)/shard_map/ppermute | solution.py:624
  76.9 3.1 %collective-permute-done.29.third.refs_4_ = bf16[1,4,32,1024]{3,2,1,0:T(8,128)(2,1)S(1)} collective-permute-done((bf16[1,4,32,1024]{3,2,1,0:T(8,128)(2,1)S(1)}, bf16[1,4,32,1024]{3,2,1,0:T(8,128)(2,1)S(1)}, u32[]{:S(2)}, u32[]{:S(2)}) %collective-permute-start.29) | collective-permute-done | bytes 262176 | tf_op jit(solution)/shard_map/ppermute | solution.py:624
  80.8 2.5 %collective-permute-start.31 = (bf16[3,1,32,1024]{3,2,1,0:T(8,128)(2,1)S(1)}, bf16[3,1,32,1024]{3,2,1,0:T(8,128)(2,1)S(1)}, u32[]{:S(2)}, u32[]{:S(2)}) collective-permute-start(bf16[3,1,32,1024]{3,2,1,0:T(8,128)(2,1)S(1)} %gate.1.refs_6_), channel_id=1, source_target_pairs={{0,8},{2,10},{4,12},{6,14},{8,0},{10,2},{12,4},{14,6},{1,9},{3,11}... | collective-permute-start | bytes 589832 | tf_op jit(solution)/shard_map/ppermute | solution.py:624
  83.3 4.2 %scores.4.refs_6_.refs_1_ = f32[32,768]{1,0:T(8,128)S(1)} custom-call(s32[40]{0:T(128)S(1)} %get-tuple-element.1576.refs_0_.ranges, bf16[768,4096]{1,0:T(8,128)(2,1)S(1)} %bitcast.221, bf16[2,5,32,1024]{3,2,1,0:T(8,128)(2,1)S(1)} %collective-permute-done.26.refs_1_.refs_0_.refs_4_, ...), custom_call_target="tpu_custom_call" | custom-call | flops 1000 | bytes 1000 | tf_op jit(solution)/shard_map/scores/pallas_call | solution.py:479
  88.5 3.3 %collective-permute-done.31.direct.third = bf16[3,1,32,1024]{3,2,1,0:T(8,128)(2,1)S(1)} collective-permute-done((bf16[3,1,32,1024]{3,2,1,0:T(8,128)(2,1)S(1)}, bf16[3,1,32,1024]{3,2,1,0:T(8,128)(2,1)S(1)}, u32[]{:S(2)}, u32[]{:S(2)}) %collective-permute-start.31) | collective-permute-done | bytes 196640 | tf_op jit(solution)/shard_map/ppermute | solution.py:624
  92.6 1.7 %collective-permute-start.34 = (bf16[2,1,32,1024]{3,2,1,0:T(8,128)(2,1)S(1)}, bf16[2,1,32,1024]{3,2,1,0:T(8,128)(2,1)S(1)}, u32[]{:S(2)}, u32[]{:S(2)}) collective-permute-start(bf16[2,1,32,1024]{3,2,1,0:T(8,128)(2,1)S(1)} %join.3.refs_2_), channel_id=1, source_target_pairs={{0,2},{2,0},{4,6},{6,4},{8,10},{10,8},{12,14},{14,12},{1,3},{3,1},... | collective-permute-start | bytes 393224 | tf_op jit(solution)/shard_map/ppermute | solution.py:624
  94.3 3.1 %scores.5 = (f32[32,768]{1,0:T(8,128)S(1)}, bf16[32,768]{1,0:T(8,128)(2,1)S(1)}) custom-call(s32[40]{0:T(128)S(1)} %get-tuple-element.1576.refs_0_.ranges, bf16[768,4096]{1,0:T(8,128)(2,1)S(1)} %stage.1.refs_0_.hidden, bf16[2,4,32,1024]{3,2,1,0:T(8,128)(2,1)S(1)} %collective-permute-done.30.refs_0_, f32[32,768]{1,0:T(8,128)S(1)} %scores.4.refs_6_.refs_1_, ...), custom_call_target="tpu_custom_call" | custom-call | flops 1000 | bytes 1000 | tf_op jit(solution)/shard_map/scores/pallas_call | solution.py:479
  99.5 4.3 %conditional.1 = (bf16[768,1024]{1,0:T(8,128)(2,1)}) conditional(s32[]{:T(128)} %convert_element_type.129, (bf16[640,768]{1,0:T(8,128)(2,1)S(1)}, bf16[768,1024]{1,0:T(8,128)(2,1)}, bf16[768,1024]{1,0:T(8,128)(2,1)}, bf16[15,1,32,1024]{3,2,1,0:T(8,128)(2,1)S(1)}, bf16[3,1,32,1024]{3,2,1,0:T(8,128)(2,1)S(1)}, ...), branch_computations={%region_1.0_spmd, %region_2.22_spmd} | conditional | flops 2020593920 | bytes 135421216 | solution.py:799
  99.5 4.0 %final.2 = bf16[768,1024]{1,0:T(8,128)(2,1)} custom-call(bf16[640,768]{1,0:T(8,128)(2,1)S(1)} %get-tuple-element.1444.left, bf16[768,1024]{1,0:T(8,128)(2,1)} %get-tuple-element.1445.refs_0_, bf16[768,1024]{1,0:T(8,128)(2,1)} %get-tuple-element.1446.refs_1_, bf16[15,1,32,1024]{3,2,1,0:T(8,128)(2,1)S(1)} %get-tuple-element.1447.refs_2_, ...), custom_call_target="tpu_custom_call" | custom-call | flops 1000 | bytes 1000 | tf_op jit(solution)/shard_map/cond/branch_0_fun/final/pallas_call | solution.py:609
  (43 shorter events, 7.8 us)
Async XLA Ops:
  4.7 35.5 %collective-permute-start.24 = (bf16[3,5,32,1024]{3,2,1,0:T(8,128)(2,1)}, bf16[3,5,32,1024]{3,2,1,0:T(8,128)(2,1)S(1)}, u32[]{:S(2)}, u32[]{:S(2)}) collective-permute-start(bf16[3,5,32,1024]{3,2,1,0:T(8,128)(2,1)} %get-tuple-element.1578), channel_id=1, source_target_pairs={{0,4},{2,6},{4,0},{6,2},{8,12},{10,14},{12,8},{14,10},{1,5},{3,7},... | collective-permute-start | bytes 2949128 | tf_op jit(solution)/shard_map/ppermute | solution.py:624
  7.8 22.6 %collective-permute-start.23 = (bf16[2,5,32,1024]{3,2,1,0:T(8,128)(2,1)}, bf16[2,5,32,1024]{3,2,1,0:T(8,128)(2,1)S(1)}, u32[]{:S(2)}, u32[]{:S(2)}) collective-permute-start(bf16[2,5,32,1024]{3,2,1,0:T(8,128)(2,1)} %get-tuple-element.1577), channel_id=1, source_target_pairs={{0,2},{2,0},{4,6},{6,4},{8,10},{10,8},{12,14},{14,12},{1,3},{3,1},... | collective-permute-start | bytes 1966088 | tf_op jit(solution)/shard_map/ppermute | solution.py:624
  9.3 45.0 %collective-permute-start.25 = (bf16[3,5,32,1024]{3,2,1,0:T(8,128)(2,1)}, bf16[3,5,32,1024]{3,2,1,0:T(8,128)(2,1)S(1)}, u32[]{:S(2)}, u32[]{:S(2)}) collective-permute-start(bf16[3,5,32,1024]{3,2,1,0:T(8,128)(2,1)} %get-tuple-element.1579), channel_id=1, source_target_pairs={{0,12},{2,14},{4,8},{6,10},{8,4},{10,6},{12,0},{14,2},{1,13},{3,15... | collective-permute-start | bytes 2949128 | tf_op jit(solution)/shard_map/ppermute | solution.py:624
  16.4 13.4 %collective-permute-start.22 = (s32[8]{0:T(128)S(1)}, s32[8]{0:T(128)S(1)}, u32[]{:S(2)}, u32[]{:S(2)}) collective-permute-start(s32[8]{0:T(128)S(1)} %get-tuple-element.1575), channel_id=1, source_target_pairs={{0,16},{16,0},{1,17},{17,1},{2,18},{18,2},{3,19},{19,3},{4,20},{20... | collective-permute-start | bytes 104 | tf_op jit(solution)/shard_map/ppermute | solution.py:698
  18.0 13.2 %slice-start = ((s8[6291456]{0:T(1024)(128)(4,1)}), s8[4194304]{0:T(1024)(128)(4,1)S(1)}, s32[]{:S(2)}) async-start(s8[6291456]{0:T(1024)(128)(4,1)} %bitcast.217), calls=%async_computation | async-start | bytes 8388608
  18.0 12.4 %copy-start.6 = (bf16[8,32,4096]{2,1,0:T(8,128)(2,1)S(1)}, bf16[8,32,4096]{2,1,0:T(8,128)(2,1)}, u32[]{:S(2)}) copy-start(bf16[8,32,4096]{2,1,0:T(8,128)(2,1)} %down.5) | copy-start | bytes 6291460
  18.0 12.4 %copy-start.7 = (bf16[8,32,1024]{2,1,0:T(8,128)(2,1)S(1)}, bf16[8,32,1024]{2,1,0:T(8,128)(2,1)}, u32[]{:S(2)}) copy-start(bf16[8,32,1024]{2,1,0:T(8,128)(2,1)} %up.7) | copy-start | bytes 1572868
  18.0 13.3 %slice-start.1 = ((s8[6291456]{0:T(1024)(128)(4,1)}), s8[2097152]{0:T(1024)(128)(4,1)S(1)}, s32[]{:S(2)}) async-start(s8[6291456]{0:T(1024)(128)(4,1)} %bitcast.217), calls=%async_computation.1 | async-start | bytes 4194304
  29.8 69.7 %collective-permute-start.33 = (bf16[768,1024]{1,0:T(8,128)(2,1)}, bf16[768,1024]{1,0:T(8,128)(2,1)}, u32[]{:S(2)}, u32[]{:S(2)}) collective-permute-start(bf16[768,1024]{1,0:T(8,128)(2,1)} %base_product.2.refs_0_), channel_id=1, source_target_pairs={{0,1},{1,0},{2,3},{3,2},{4,5},{5,4},{6,7},{7,6},{8,9},{9,8},{10,11... | collective-permute-start | bytes 4718600 | tf_op jit(solution)/shard_map/ppermute | solution.py:667
  30.4 11.2 %copy-start.2 = (bf16[2,5,32,1024]{3,2,1,0:T(8,128)(2,1)}, bf16[2,5,32,1024]{3,2,1,0:T(8,128)(2,1)S(1)}, u32[]{:S(2)}) copy-start(bf16[2,5,32,1024]{3,2,1,0:T(8,128)(2,1)S(1)} %collective-permute-done.23.refs_2_.refs_1_.refs_3_) | copy-start | bytes 1966084
  40.2 28.5 %copy-start.9 = (bf16[768,1024]{1,0:T(8,128)(2,1)}, bf16[768,1024]{1,0:T(8,128)(2,1)S(1)}, u32[]{:S(2)}) copy-start(bf16[768,1024]{1,0:T(8,128)(2,1)S(1)} %base_product.3.refs_0_) | copy-start | bytes 4718596
  41.0 17.2 %collective-permute-start.26 = (bf16[2,5,32,1024]{3,2,1,0:T(8,128)(2,1)S(1)}, bf16[2,5,32,1024]{3,2,1,0:T(8,128)(2,1)S(1)}, u32[]{:S(2)}, u32[]{:S(2)}) collective-permute-start(bf16[2,5,32,1024]{3,2,1,0:T(8,128)(2,1)S(1)} %cut.3.refs_3_), channel_id=1, source_target_pairs={{0,2},{2,0},{4,6},{6,4},{8,10},{10,8},{12,14},{14,12},{1,3},{3,1},... | collective-permute-start | bytes 1966088 | tf_op jit(solution)/shard_map/ppermute | solution.py:624
  46.0 30.9 %collective-permute-start.28 = (bf16[2,4,32,1024]{3,2,1,0:T(8,128)(2,1)S(1)}, bf16[2,4,32,1024]{3,2,1,0:T(8,128)(2,1)S(1)}, u32[]{:S(2)}, u32[]{:S(2)}) collective-permute-start(bf16[2,4,32,1024]{3,2,1,0:T(8,128)(2,1)S(1)} %pack_more.3.refs_0_), channel_id=1, source_target_pairs={{0,8},{2,10},{4,12},{6,14},{8,0},{10,2},{12,4},{14,6},{1,9},{3,11}... | collective-permute-start | bytes 1572872 | tf_op jit(solution)/shard_map/ppermute | solution.py:624
  58.8 21.2 %collective-permute-start.29 = (bf16[1,4,32,1024]{3,2,1,0:T(8,128)(2,1)S(1)}, bf16[1,4,32,1024]{3,2,1,0:T(8,128)(2,1)S(1)}, u32[]{:S(2)}, u32[]{:S(2)}) collective-permute-start(bf16[1,4,32,1024]{3,2,1,0:T(8,128)(2,1)S(1)} %cut.4.refs_0_), channel_id=1, source_target_pairs={{0,4},{2,6},{4,0},{6,2},{8,12},{10,14},{12,8},{14,10},{1,5},{3,7},... | collective-permute-start | bytes 786440 | tf_op jit(solution)/shard_map/ppermute | solution.py:624
  68.7 14.6 %collective-permute-start.27 = (bf16[2,5,32,1024]{3,2,1,0:T(8,128)(2,1)S(1)}, bf16[2,5,32,1024]{3,2,1,0:T(8,128)(2,1)S(1)}, u32[]{:S(2)}, u32[]{:S(2)}) collective-permute-start(bf16[2,5,32,1024]{3,2,1,0:T(8,128)(2,1)S(1)} %cut.5.refs_0_), channel_id=1, source_target_pairs={{0,2},{2,0},{4,6},{6,4},{8,10},{10,8},{12,14},{14,12},{1,3},{3,1},... | collective-permute-start | bytes 1966088 | tf_op jit(solution)/shard_map/ppermute | solution.py:624
  80.6 13.7 %collective-permute-start.30 = (bf16[2,4,32,1024]{3,2,1,0:T(8,128)(2,1)S(1)}, bf16[2,4,32,1024]{3,2,1,0:T(8,128)(2,1)S(1)}, u32[]{:S(2)}, u32[]{:S(2)}) collective-permute-start(bf16[2,4,32,1024]{3,2,1,0:T(8,128)(2,1)S(1)} %join.2.refs_1_), channel_id=1, source_target_pairs={{0,2},{2,0},{4,6},{6,4},{8,10},{10,8},{12,14},{14,12},{1,3},{3,1},... | collective-permute-start | bytes 1572872 | tf_op jit(solution)/shard_map/ppermute | solution.py:624
  80.8 6.7 %copy-start.3 = (bf16[2,5,32,1024]{3,2,1,0:T(8,128)(2,1)S(1)}, bf16[2,5,32,1024]{3,2,1,0:T(8,128)(2,1)}, u32[]{:S(2)}) copy-start(bf16[2,5,32,1024]{3,2,1,0:T(8,128)(2,1)} %copy-done.2) | copy-start | bytes 1966084
  80.8 11.0 %collective-permute-start.31 = (bf16[3,1,32,1024]{3,2,1,0:T(8,128)(2,1)S(1)}, bf16[3,1,32,1024]{3,2,1,0:T(8,128)(2,1)S(1)}, u32[]{:S(2)}, u32[]{:S(2)}) collective-permute-start(bf16[3,1,32,1024]{3,2,1,0:T(8,128)(2,1)S(1)} %gate.1.refs_6_), channel_id=1, source_target_pairs={{0,8},{2,10},{4,12},{6,14},{8,0},{10,2},{12,4},{14,6},{1,9},{3,11}... | collective-permute-start | bytes 589832 | tf_op jit(solution)/shard_map/ppermute | solution.py:624
  92.6 6.9 %copy-start.8 = (bf16[8,32,1024]{2,1,0:T(8,128)(2,1)S(1)}, bf16[8,32,1024]{2,1,0:T(8,128)(2,1)}, u32[]{:S(2)}) copy-start(bf16[8,32,1024]{2,1,0:T(8,128)(2,1)} %up.7) | copy-start | bytes 1572868
  92.6 6.9 %copy-start.10 = (s32[64]{0:T(128)S(1)}, s32[64]{0:T(128)}, u32[]{:S(2)}) copy-start(s32[64]{0:T(128)} %counts.1) | copy-start | bytes 772
  92.6 6.8 %collective-permute-start.34 = (bf16[2,1,32,1024]{3,2,1,0:T(8,128)(2,1)S(1)}, bf16[2,1,32,1024]{3,2,1,0:T(8,128)(2,1)S(1)}, u32[]{:S(2)}, u32[]{:S(2)}) collective-permute-start(bf16[2,1,32,1024]{3,2,1,0:T(8,128)(2,1)S(1)} %join.3.refs_2_), channel_id=1, source_target_pairs={{0,2},{2,0},{4,6},{6,4},{8,10},{10,8},{12,14},{14,12},{1,3},{3,1},... | collective-permute-start | bytes 393224 | tf_op jit(solution)/shard_map/ppermute | solution.py:624
  97.4 1.3 %collective-permute-start.32 = (bf16[32,768]{1,0:T(8,128)(2,1)S(1)}, bf16[32,768]{1,0:T(8,128)(2,1)S(1)}, u32[]{:S(2)}, u32[]{:S(2)}) collective-permute-start(bf16[32,768]{1,0:T(8,128)(2,1)S(1)} %get-tuple-element.1581), channel_id=1, source_target_pairs={{0,1},{1,0},{2,3},{3,2},{4,5},{5,4},{6,7},{7,6},{8,9},{9,8},{10,11... | collective-permute-start | bytes 147464 | tf_op jit(solution)/shard_map/ppermute | solution.py:667
